TPU v7x, 32 devices: a whole 2x2x4 slice. The times are simulated.
32 devices in a mesh: groups: 2 (over y), adapter: 4 (over z), tensor: 4 (over x, core).
Axes of the slice: x: 2, y: 2, z: 4, core: 2. Of those that a mesh axis runs over, the one named last changes fastest.
Arguments:
- tokens: bfloat16 [256, 8192], P(('groups', 'adapter')), parts along dimension 0, may hold values from -6 to 6
- attention_gain: float32 [8192], replicated, may hold values from 0.5 to 1.5
- query_weight: bfloat16 [8192, 4096], P('adapter', 'tensor'), may hold values from -0.0625 to 0.0625
- key_weight: bfloat16 [8192, 512], P('adapter', 'tensor'), may hold values from -0.0625 to 0.0625
- value_weight: bfloat16 [8192, 512], P('adapter', 'tensor'), may hold values from -0.0625 to 0.0625
- speaker_question_lowering: bfloat16 [8192, 32, 64], P('tensor', 'adapter'), may hold values from -0.0625 to 0.0625
- speaker_question_raising: bfloat16 [32, 64, 4096], P('adapter', None, 'tensor'), may hold values from -0.75 to 0.75
- speaker_content_lowering: bfloat16 [8192, 32, 64], P('tensor', 'adapter'), may hold values from -0.0625 to 0.0625
- speaker_content_raising: bfloat16 [32, 64, 512], P('adapter', None, 'tensor'), may hold values from -0.75 to 0.75
- rotated_key_cache: bfloat16 [256, 4, 128, 128], P(('groups', 'adapter'), 'tensor'), parts along dimension 0, may hold values from -400 to 400
- stored_value_cache: bfloat16 [256, 4, 128, 128], P(('groups', 'adapter'), 'tensor'), parts along dimension 0, may hold values from -6 to 6
- sequence_speaker_label: int32 [256], P(('groups', 'adapter')), parts along dimension 0, may hold values from 0 to 31, as said below
- lengths: int32 [256], P(('groups', 'adapter')), parts along dimension 0, may hold values from 1 to 127, as said below
- output_weight: bfloat16 [4096, 8192], P('tensor', 'adapter'), may hold values from -0.09375 to 0.09375
- closing_gain: float32 [8192], replicated, may hold values from 0.5 to 1.5
- codebook_weight: bfloat16 [8192, 16384], P('adapter', 'tensor'), may hold values from -0.19921875 to 0.19921875
- delays: int32 [8], replicated, may hold values from 0 to 63
Outputs:
- hidden: bfloat16 [256, 8192], P(('groups', 'tensor'), 'adapter'), parts along dimension 0
- logits: float32 [256, 8, 2048], P(('groups', 'adapter'), 'tensor'), parts along dimension 0
There are 2 independent parts, one for each index of `groups`. A program takes and returns all parts, laid end to end along the dimension named above; an argument that names none is the same for every part. Nothing has to cross between parts.
Inputs may be any that keep to these rules, and one draw needn't show every extreme that they name: Call sequence_speaker_label[s] // 8 the owner of stream s. Among the 32 streams of one index of adapter, no owner is named more than 16 times; in every draw some owner is named 16 times within the streams of every index of adapter. `lengths`: some stream reaches the largest length.
All inputs are finite; a program needn't handle non-finite values.
Results may differ from a plain program's by a relative error of at most 0.0065.
The roundings to bfloat16 on the way count: a program that leaves them out, or rounds other values in their place, can miss the bound.
Values may be sent and summed in bfloat16 or wider, within the bound.
No kernel may reach another device: no remote copies, remote signals or barrier semaphores. Data moves between devices by JAX's collectives and lax.ppermute only.
A program may use at most 128 MiB of HBM per device.

v0:
```python
import jax
import jax.numpy as jnp
from jax import lax
from jax.sharding import PartitionSpec as P

CB = 8
VOC = 2048


ROPE_BASE = 500000.0
NORM_EPS = 1e-05
ADAPTER_SCALE = 0.5


def rotate(values, positions):
    head_dim = values.shape[-1]
    half_dim = head_dim // 2
    spacing = jnp.arange(half_dim, dtype=jnp.float32) * (2.0 / head_dim)
    angles = positions.astype(jnp.float32)[:, None] * jnp.power(ROPE_BASE, -spacing)[None, :]
    new_shape = (values.shape[0],) + (1,) * (values.ndim - 2) + (half_dim,)
    cosine = jnp.cos(angles).reshape(new_shape)
    sine = jnp.sin(angles).reshape(new_shape)
    first_half = values[..., :half_dim]
    second_half = values[..., half_dim:]
    return jnp.concatenate(
        [first_half * cosine - second_half * sine, first_half * sine + second_half * cosine],
        axis=-1,
    )


def per_device(
    tokens,
    attention_gain,
    query_weight,
    key_weight,
    value_weight,
    speaker_question_lowering,
    speaker_question_raising,
    speaker_content_lowering,
    speaker_content_raising,
    rotated_key_cache,
    stored_value_cache,
    sequence_speaker_label,
    lengths,
    output_weight,
    closing_gain,
    codebook_weight,
    delays,
):
    n_adapter = lax.axis_size("adapter")
    n_tensor = lax.axis_size("tensor")
    adapter_pos = lax.axis_index("adapter")
    tensor_pos = lax.axis_index("tensor")
    str_dev, model_width = tokens.shape
    all_streams = str_dev * n_adapter
    d_slice = model_width // n_adapter
    tensor_width = model_width // n_tensor
    tok_f = tokens.astype(jnp.float32)
    inverse = lax.rsqrt(jnp.mean(tok_f * tok_f, axis=-1, keepdims=True) + NORM_EPS)
    rescaled_hidden_state = (tok_f * inverse * attention_gain).astype(jnp.bfloat16)
    raw_cols, norm_cols = (
        lax.all_to_all(tokens, "adapter", split_axis=1, concat_axis=0, tiled=True),
        lax.all_to_all(rescaled_hidden_state, "adapter", split_axis=1, concat_axis=0, tiled=True),
    )
    query_columns = query_weight.shape[1]
    key_value_columns = key_weight.shape[1]
    weights_cat = jnp.concatenate([query_weight, key_weight, value_weight], axis=1)
    full_proj = jnp.dot(norm_cols, weights_cat, preferred_element_type=jnp.float32)
    summed = lax.psum(full_proj, "adapter")
    projected = lax.dynamic_slice_in_dim(summed, adapter_pos * str_dev, str_dev, 0)
    plain_query = projected[:, :query_columns]
    key_base = projected[:, query_columns : query_columns + key_value_columns]
    plain_value = projected[:, query_columns + key_value_columns :]
    voices_per_shard = speaker_question_raising.shape[0]
    adapter_rank_size = speaker_question_raising.shape[1]
    slot_cap = max(2, 2 * str_dev // n_adapter)
    slot_total = n_adapter * slot_cap
    owner_ids = sequence_speaker_label // voices_per_shard
    local_voice = sequence_speaker_label % voices_per_shard
    same_owner = owner_ids[:, None] == owner_ids[None, :]
    earlier = jnp.arange(str_dev)[:, None] > jnp.arange(str_dev)[None, :]
    owner_rank = jnp.sum((same_owner & earlier).astype(jnp.int32), axis=1)
    slot_ids = owner_ids * slot_cap + owner_rank
    placing = (slot_ids[None, :] == jnp.arange(slot_total)[:, None]).astype(jnp.bfloat16)
    voice_onehot = (local_voice[:, None] == jnp.arange(voices_per_shard)[None, :]).astype(
        jnp.bfloat16
    )
    normed_part = lax.dynamic_slice_in_dim(
        rescaled_hidden_state, tensor_pos * tensor_width, tensor_width, 1
    )
    send_rows = jnp.dot(placing, normed_part, preferred_element_type=jnp.float32).astype(
        jnp.bfloat16
    )
    send_voice = jnp.dot(placing, voice_onehot, preferred_element_type=jnp.float32).astype(
        jnp.bfloat16
    )
    send_rows = send_rows.reshape(n_adapter, slot_cap, tensor_width)
    send_voice = send_voice.reshape(n_adapter, slot_cap, voices_per_shard)
    query_down_matrix = speaker_question_lowering.reshape(
        tensor_width, voices_per_shard * adapter_rank_size
    )
    value_down_matrix = speaker_content_lowering.reshape(
        tensor_width, voices_per_shard * adapter_rank_size
    )
    query_up_matrix = speaker_question_raising.reshape(
        voices_per_shard * adapter_rank_size, query_columns
    )
    value_up_matrix = speaker_content_raising.reshape(
        voices_per_shard * adapter_rank_size, key_value_columns
    )
    rows_in = lax.all_to_all(send_rows, "adapter", split_axis=0, concat_axis=0, tiled=True)
    voices_in = lax.all_to_all(send_voice, "adapter", split_axis=0, concat_axis=0, tiled=True)
    item_count = rows_in.shape[1]
    flat_rows = rows_in.reshape(-1, tensor_width)
    onehot_b = voices_in.reshape(-1, voices_per_shard)
    onehot_f = onehot_b.astype(jnp.float32)
    all_q = jnp.dot(flat_rows, query_down_matrix, preferred_element_type=jnp.float32).reshape(
        -1, voices_per_shard, adapter_rank_size
    )
    all_v = jnp.dot(flat_rows, value_down_matrix, preferred_element_type=jnp.float32).reshape(
        -1, voices_per_shard, adapter_rank_size
    )
    down_q = jnp.sum(onehot_f[:, :, None] * all_q, axis=1)
    down_v = jnp.sum(onehot_f[:, :, None] * all_v, axis=1)
    down_q, down_v = lax.psum((down_q, down_v), "tensor")
    query_broadcast = (onehot_b[:, :, None] * down_q.astype(jnp.bfloat16)[:, None, :]).reshape(
        -1, voices_per_shard * adapter_rank_size
    )
    value_broadcast = (onehot_b[:, :, None] * down_v.astype(jnp.bfloat16)[:, None, :]).reshape(
        -1, voices_per_shard * adapter_rank_size
    )
    question_raised_product = (
        jnp.dot(query_broadcast, query_up_matrix, preferred_element_type=jnp.float32)
        * ADAPTER_SCALE
    ).astype(jnp.bfloat16)
    content_raised_product = (
        jnp.dot(value_broadcast, value_up_matrix, preferred_element_type=jnp.float32)
        * ADAPTER_SCALE
    ).astype(jnp.bfloat16)
    outgoing = jnp.concatenate([question_raised_product, content_raised_product], axis=1).reshape(
        n_adapter, item_count, query_columns + key_value_columns
    )
    returned = lax.all_to_all(outgoing, "adapter", split_axis=0, concat_axis=0, tiled=True)
    adapter_summands = jnp.einsum(
        "ms,mc->sc",
        placing,
        returned.reshape(slot_total, query_columns + key_value_columns),
        preferred_element_type=jnp.float32,
    )
    kv_local = rotated_key_cache.shape[1]
    head_dim = rotated_key_cache.shape[3]
    ctx_len = rotated_key_cache.shape[2]
    group_size = query_columns // (kv_local * head_dim)
    adapted_query = (plain_query + adapter_summands[:, :query_columns]).reshape(
        str_dev, kv_local, group_size, head_dim
    )
    query = rotate(adapted_query, lengths).astype(jnp.bfloat16)
    key_new = rotate(key_base.reshape(str_dev, kv_local, head_dim), lengths).astype(jnp.bfloat16)
    value_new = (
        (plain_value + adapter_summands[:, query_columns:])
        .reshape(str_dev, kv_local, head_dim)
        .astype(jnp.bfloat16)
    )
    scale_factor = 1.0 / head_dim**0.5
    scores = (
        jnp.einsum("skgd,skcd->skgc", query, rotated_key_cache, preferred_element_type=jnp.float32)
        * scale_factor
    )
    own_score = (
        jnp.einsum("skgd,skd->skg", query, key_new, preferred_element_type=jnp.float32)
        * scale_factor
    )
    valid = (jnp.arange(ctx_len)[None, :] < lengths[:, None])[:, None, None, :]
    masked = jnp.where(valid, scores, -1e30)
    top_score = jnp.maximum(jnp.max(masked, axis=-1), own_score)
    weights_all = jnp.where(valid, jnp.exp(scores - top_score[..., None]), 0.0)
    own_weight = jnp.exp(own_score - top_score)
    total = jnp.sum(weights_all, axis=-1) + own_weight
    probs = (weights_all / total[..., None]).astype(jnp.bfloat16)
    own_prob = (own_weight / total).astype(jnp.bfloat16)
    mixed = jnp.einsum(
        "skgc,skcd->skgd", probs, stored_value_cache, preferred_element_type=jnp.float32
    )
    mixed = (
        mixed
        + own_prob.astype(jnp.float32)[..., None] * value_new.astype(jnp.float32)[:, :, None, :]
    )
    attended = mixed.astype(jnp.bfloat16).reshape(str_dev, query_columns)
    partial_out = jnp.dot(
        lax.all_gather(attended, "adapter", axis=0, tiled=True),
        output_weight,
        preferred_element_type=jnp.float32,
    )
    final_slice = lax.dynamic_slice_in_dim(closing_gain, adapter_pos * d_slice, d_slice)
    rows_tensor = all_streams // n_tensor
    summed_out = lax.psum(partial_out, "tensor")
    hidden_all = (raw_cols.astype(jnp.float32) + summed_out).astype(jnp.bfloat16)
    hidden_f = hidden_all.astype(jnp.float32)
    square_sum = lax.psum(jnp.sum(hidden_f * hidden_f, axis=-1), "adapter")
    final_normed = (
        hidden_f * lax.rsqrt(square_sum / model_width + NORM_EPS)[:, None] * final_slice
    ).astype(jnp.bfloat16)
    hidden_out = lax.dynamic_slice_in_dim(hidden_all, tensor_pos * rows_tensor, rows_tensor, 0)
    logit_rows = lax.psum_scatter(
        jnp.dot(final_normed, codebook_weight, preferred_element_type=jnp.float32),
        "adapter",
        scatter_dimension=0,
        tiled=True,
    )
    books_local = CB // n_tensor
    book_delays = lax.dynamic_slice_in_dim(delays, tensor_pos * books_local, books_local)
    active = (lengths[:, None] >= book_delays[None, :]).astype(jnp.float32)
    logits = logit_rows.reshape(str_dev, books_local, VOC) * active[:, :, None]
    return (hidden_out, logits)


def solution(mesh):
    in_specs = (
        P(("groups", "adapter"), None),
        P(),
        P("adapter", "tensor"),
        P("adapter", "tensor"),
        P("adapter", "tensor"),
        P("tensor", "adapter", None),
        P("adapter", None, "tensor"),
        P("tensor", "adapter", None),
        P("adapter", None, "tensor"),
        P(("groups", "adapter"), "tensor", None, None),
        P(("groups", "adapter"), "tensor", None, None),
        P(("groups", "adapter")),
        P(("groups", "adapter")),
        P("tensor", "adapter"),
        P(),
        P("adapter", "tensor"),
        P(),
    )
    out_specs = (P(("groups", "tensor"), "adapter"), P(("groups", "adapter"), "tensor", None))
    return jax.shard_map(
        per_device, mesh=mesh, in_specs=in_specs, out_specs=out_specs, check_vma=False
    )
```

profile of v0, /device:TPU:0, one launch (start us, length us, event | category | flops | bytes accessed | tf_op | source)
XLA Modules:
  0.0 234.6 jit_solution(396375081374093081)
XLA Ops:
  7.2 0.0 copy-start
  7.2 0.8 and_select_fusion
  8.0 0.2 convert_reduce_fusion
  8.2 0.2 convolution_convert_fusion.1
  8.4 0.1 reshape.344
  8.5 0.6 copy.38
  9.1 6.3 %all-to-all-start.2 = ((bf16[4,16,8]{1,2,0:T(8,128)(2,1)}), bf16[4,16,8]{1,2,0:T(8,128)(2,1)S(1)}, u32[]{:S(2)}, u32[]{:S(2)}) async-start(bf16[4,16,8]{1,2,0:T(8,128)(2,1)} %copy.38), calls=%async_computation.2 | async-start | bytes 16384 | tf_op jit(solution)/shard_map/all_to_all | solution.py:112
  15.4 1.2 fusion.27
  16.7 1.2 fusion.29
  18.0 0.9 convolution_convert_fusion
  18.9 2.2 all-to-all-done.2
  21.0 3.5 %all-to-all-start.3 = ((bf16[4,16,2048]{2,1,0:T(8,128)(2,1)}), bf16[4,16,2048]{2,1,0:T(8,128)(2,1)S(1)}, u32[]{:S(2)}, u32[]{:S(2)}) async-start(bf16[4,16,2048]{2,1,0:T(8,128)(2,1)} %bitcast.4), calls=%async_computation.3 | async-start | bytes 524288 | tf_op jit(solution)/shard_map/all_to_all | solution.py:111
  24.6 0.8 copy.52
  25.4 0.7 convert_element_type.111
  26.1 1.9 copy.53
  28.0 0.1 multiply_cosine_fusion.1
  28.1 0.1 mul.249
  28.2 4.4 %all-to-all-done.3 = bf16[4,16,2048]{2,1,0:T(8,128)(2,1)S(1)} async-done(((bf16[4,16,2048]{2,1,0:T(8,128)(2,1)}), bf16[4,16,2048]{2,1,0:T(8,128)(2,1)S(1)}, u32[]{:S(2)}, u32[]{:S(2)}) %all-to-all-start.3) | async-done | bytes 262176 | tf_op jit(solution)/shard_map/all_to_all | solution.py:111
  32.6 3.5 %all-to-all-start.1 = ((bf16[32,4,2048]{2,0,1:T(8,128)(2,1)}), bf16[32,4,2048]{2,0,1:T(8,128)(2,1)S(1)}, u32[]{:S(2)}, u32[]{:S(2)}) async-start(bf16[32,4,2048]{2,0,1:T(8,128)(2,1)} %bitcast.99), calls=%async_computation.1 | async-start | bytes 1048576 | tf_op jit(solution)/shard_map/all_to_all | solution.py:63
  36.1 0.0 all-reduce.4.cloned.1.call-start
  36.1 1.1 fusion.18
  37.3 2.7 %fusion.21 = f32[64,64]{1,0:T(8,128)S(1)} fusion(bf16[64,2048,1]{1,0,2:T(8,128)(2,1)S(1)} %bitcast.105, bf16[2048,8,64]{0,2,1:T(8,128)(2,1)} %param.22, f32[64,8]{0,1:T(8,128)S(1)} %convert_element_type.105), kind=kOutput, calls=%fused_computation.21 | convolution fusion | flops 134279168 | bytes 2377728 | tf_op jit(solution)/shard_map/dot_general | solution.py:117
  40.0 11.1 %all-reduce = (bf16[64,64]{1,0:T(8,128)(2,1)S(1)}, bf16[64,64]{1,0:T(8,128)(2,1)S(1)}) all-reduce(f32[64,64]{1,0:T(8,128)S(1)} %fusion.18, f32[64,64]{1,0:T(8,128)S(1)} %fusion.21), channel_id=1, replica_groups=mesh['groups'=2,'adapter'=4,'tensor'=4] {'tensor'}, use_global_device_ids=true, to_apply=%region_6.7 | all-reduce | flops 8192 | bytes 49152 | tf_op jit(solution)/shard_map/psum | solution.py:125
  51.1 0.3 fusion.26
  51.4 1.6 fusion.17
  53.1 0.0 all-to-all-done.1
  53.1 0.0 copy-start.2
  53.1 4.0 %fusion = f32[128,1280]{1,0:T(8,128)} fusion(bf16[128,2048]{1,0:T(8,128)(2,1)S(1)} %bitcast.108, bf16[2048,128]{1,0:T(8,128)(2,1)} %param.21, bf16[2048,128]{1,0:T(8,128)(2,1)} %param.20, bf16[2048,1024]{1,0:T(8,128)(2,1)} %param.19), kind=kOutput, calls=%fused_computation | convolution fusion | flops 686817280 | bytes 6422528 | tf_op jit(solution)/shard_map/dot_general | solution.py:68
  57.0 0.0 all-reduce.4.cloned.1.call-update
  57.1 0.7 pad_maximum_fusion
  57.7 4.6 %all-to-all-start.4 = ((bf16[4,16,1152]{2,1,0:T(8,128)(2,1)}), bf16[4,16,1152]{2,1,0:T(8,128)(2,1)S(1)}, u32[]{:S(2)}, u32[]{:S(2)}) async-start(bf16[4,16,1152]{2,1,0:T(8,128)(2,1)} %bitcast.16), calls=%async_computation.4 | async-start | bytes 294912 | tf_op jit(solution)/shard_map/all_to_all | solution.py:143
  62.3 0.1 iota_compare_fusion.6
  62.4 10.1 %all-to-all-done.4 = bf16[4,16,1152]{2,1,0:T(8,128)(2,1)S(1)} async-done(((bf16[4,16,1152]{2,1,0:T(8,128)(2,1)}), bf16[4,16,1152]{2,1,0:T(8,128)(2,1)S(1)}, u32[]{:S(2)}, u32[]{:S(2)}) %all-to-all-start.4) | async-done | bytes 147488 | tf_op jit(solution)/shard_map/all_to_all | solution.py:143
  72.5 3.5 %all-to-all-start = ((bf16[32,4,2048]{2,0,1:T(8,128)(2,1)}), bf16[32,4,2048]{2,0,1:T(8,128)(2,1)S(1)}, u32[]{:S(2)}, u32[]{:S(2)}) async-start(bf16[32,4,2048]{2,0,1:T(8,128)(2,1)} %bitcast.100), calls=%async_computation | async-start | bytes 1048576 | tf_op jit(solution)/shard_map/all_to_all | solution.py:62
  75.9 0.0 all-reduce.6.cloned.1.call-start
  76.0 0.2 fusion.55
  76.2 26.9 %all-reduce.4.cloned.1.call-done = f32[128,1280]{1,0:T(8,128)} async-done(((f32[128,1280]{1,0:T(8,128)}), f32[128,1280]{1,0:T(8,128)}) %all-reduce.4.cloned.1.call-update) | async-done | bytes 655376 | tf_op jit(solution)/shard_map/psum | solution.py:69
  103.1 1.1 fusion.40
  104.2 1.0 dynamic-slice_bitcast_fusion
  105.2 0.1 fusion.75
  105.3 0.1 maximum_bitcast_fusion
  105.4 0.1 fusion.45
  105.5 0.2 fusion.68
  105.7 2.0 select_reduce_fusion
  107.7 0.2 fusion.44
  107.9 1.7 fusion.24
  109.6 14.0 %all_gather.3 = bf16[128,1024]{1,0:T(8,128)(2,1)S(1)} all-gather(bf16[32,1024]{1,0:T(8,128)(2,1)S(1)} %bitcast.109), channel_id=1, replica_groups=mesh['groups'=2,'adapter'=4,'tensor'=4] {'adapter'}, dimensions={0}, use_global_device_ids=true | all-gather | bytes 327680 | tf_op jit(solution)/shard_map/all_gather | solution.py:190
  123.7 1.8 fusion.83
  125.4 0.0 all-reduce.6.cloned.1.call-update
  125.5 0.0 reduce-scatter.2.cloned.1.call-start
  125.5 0.7 dynamic_slice.18
  126.2 0.0 all-to-all-done
  126.2 35.0 %all-reduce.6.cloned.1.call-done = f32[128,2048]{1,0:T(8,128)} async-done(((f32[128,2048]{1,0:T(8,128)}), f32[128,2048]{1,0:T(8,128)}) %all-reduce.6.cloned.1.call-update) | async-done | bytes 1048592 | tf_op jit(solution)/shard_map/psum | solution.py:196
  161.2 1.5 fusion.30
  162.6 11.7 %psum.39 = f32[128]{0:T(128)S(1)} all-reduce(f32[128]{0:T(128)S(1)} %get-tuple-element.4), channel_id=1, replica_groups=mesh['groups'=2,'adapter'=4,'tensor'=4] {'adapter'}, use_global_device_ids=true, to_apply=%region_11.12 | all-reduce | flops 128 | bytes 1024 | tf_op jit(solution)/shard_map/psum | solution.py:199
  174.3 9.6 %fusion.36 = f32[128,4096]{1,0:T(8,128)} fusion(bf16[2048,4096]{1,0:T(8,128)(2,1)} %param.32, bf16[128,2048]{1,0:T(8,128)(2,1)S(1)} %get-tuple-element.5, f32[2048]{0:T(1024)S(1)} %dynamic_slice.18, f32[128]{0:T(128)S(1)} %add_rsqrt_fusion), kind=kOutput, calls=%fused_computation.39 | convolution fusion | flops 2148532224 | bytes 19407360 | tf_op jit(solution)/shard_map/dot_general | solution.py:205
  183.9 0.0 reduce-scatter.2.cloned.1.call-update
  184.0 0.1 dynamic_slice.19
  184.0 0.1 compare_convert_fusion
  184.1 0.1 copy.40
  184.2 0.7 constant_dynamic-slice_fusion
  184.9 40.7 %reduce-scatter.2.cloned.1.call-done = f32[32,4096]{1,0:T(8,128)} async-done(((f32[128,4096]{1,0:T(8,128)}), f32[32,4096]{1,0:T(8,128)}) %reduce-scatter.2.cloned.1.call-update) | async-done | bytes 524304 | tf_op jit(solution)/shard_map/reduce_scatter | solution.py:204
  225.6 1.5 reshape.356
  227.1 1.0 broadcast_multiply_fusion
  (18 shorter events, 0.1 us)
Async XLA Ops:
  7.2 29.0 %copy-start = (bf16[2048,8,64]{0,2,1:T(8,128)(2,1)S(1)}, bf16[2048,8,64]{0,2,1:T(8,128)(2,1)}, u32[]{:S(2)}) copy-start(bf16[2048,8,64]{0,2,1:T(8,128)(2,1)} %param.24) | copy-start | bytes 6291460
  9.1 11.9 %all-to-all-start.2 = ((bf16[4,16,8]{1,2,0:T(8,128)(2,1)}), bf16[4,16,8]{1,2,0:T(8,128)(2,1)S(1)}, u32[]{:S(2)}, u32[]{:S(2)}) async-start(bf16[4,16,8]{1,2,0:T(8,128)(2,1)} %copy.38), calls=%async_computation.2 | async-start | bytes 16384 | tf_op jit(solution)/shard_map/all_to_all | solution.py:112
  21.0 30.1 %copy-start.3 = (bf16[8,64,128]{2,1,0:T(8,128)(2,1)S(1)}, bf16[8,64,128]{2,1,0:T(8,128)(2,1)}, u32[]{:S(2)}) copy-start(bf16[8,64,128]{2,1,0:T(8,128)(2,1)} %param.25) | copy-start | bytes 393220
  21.0 11.6 %all-to-all-start.3 = ((bf16[4,16,2048]{2,1,0:T(8,128)(2,1)}), bf16[4,16,2048]{2,1,0:T(8,128)(2,1)S(1)}, u32[]{:S(2)}, u32[]{:S(2)}) async-start(bf16[4,16,2048]{2,1,0:T(8,128)(2,1)} %bitcast.4), calls=%async_computation.3 | async-start | bytes 524288 | tf_op jit(solution)/shard_map/all_to_all | solution.py:111
  32.6 20.5 %all-to-all-start.1 = ((bf16[32,4,2048]{2,0,1:T(8,128)(2,1)}), bf16[32,4,2048]{2,0,1:T(8,128)(2,1)S(1)}, u32[]{:S(2)}, u32[]{:S(2)}) async-start(bf16[32,4,2048]{2,0,1:T(8,128)(2,1)} %bitcast.99), calls=%async_computation.1 | async-start | bytes 1048576 | tf_op jit(solution)/shard_map/all_to_all | solution.py:63
  36.1 67.0 %all-reduce.4.cloned.1.call-start = ((), (), s32[]{:S(2)}) async-start(), calls=%async_computation.6 | async-start | bytes 1310720 | tf_op jit(solution)/shard_map/psum | solution.py:69
  53.1 9.3 %copy-start.2 = (s32[32]{0:T(128)S(1)}, s32[32]{0:T(128)}, u32[]{:S(2)}) copy-start(s32[32]{0:T(128)} %param.29) | copy-start | bytes 388
  57.7 14.7 %all-to-all-start.4 = ((bf16[4,16,1152]{2,1,0:T(8,128)(2,1)}), bf16[4,16,1152]{2,1,0:T(8,128)(2,1)S(1)}, u32[]{:S(2)}, u32[]{:S(2)}) async-start(bf16[4,16,1152]{2,1,0:T(8,128)(2,1)} %bitcast.16), calls=%async_computation.4 | async-start | bytes 294912 | tf_op jit(solution)/shard_map/all_to_all | solution.py:143
  72.5 53.8 %all-to-all-start = ((bf16[32,4,2048]{2,0,1:T(8,128)(2,1)}), bf16[32,4,2048]{2,0,1:T(8,128)(2,1)S(1)}, u32[]{:S(2)}, u32[]{:S(2)}) async-start(bf16[32,4,2048]{2,0,1:T(8,128)(2,1)} %bitcast.100), calls=%async_computation | async-start | bytes 1048576 | tf_op jit(solution)/shard_map/all_to_all | solution.py:62
  75.9 85.2 %all-reduce.6.cloned.1.call-start = ((), (), s32[]{:S(2)}) async-start(), calls=%async_computation.7 | async-start | bytes 2097152 | tf_op jit(solution)/shard_map/psum | solution.py:196
  103.1 20.6 %copy-start.1 = (bf16[1024,2048]{1,0:T(8,128)(2,1)S(1)}, bf16[1024,2048]{1,0:T(8,128)(2,1)}, u32[]{:S(2)}) copy-start(bf16[1024,2048]{1,0:T(8,128)(2,1)} %param.30) | copy-start | bytes 12582916
  125.5 100.1 %reduce-scatter.2.cloned.1.call-start = ((), (), s32[]{:S(2)}) async-start(), calls=%async_computation.8 | async-start | bytes 2621440 | tf_op jit(solution)/shard_map/reduce_scatter | solution.py:204
  174.3 9.6 %copy-start.4 = (s32[8]{0:T(128)S(1)}, s32[8]{0:T(128)}, u32[]{:S(2)}) copy-start(s32[8]{0:T(128)} %param.33) | copy-start | bytes 100
Sparse Core Ops, SparseCore 0:
  57.2 45.8 all-reduce.3
  125.6 35.5 all-reduce.5
  184.1 41.4 reduce-scatter.1
where the time goes:
time: 236 us; the launch traced here: 235 us
  waiting for transfers between devices  119 us (50%)
  blocking collectives  36.8 us (16%)
  matrix products  26.3 us (11%)
  starting transfers between devices  21.5 us (9%)
  between operations  13.9 us (6%)
  other arithmetic  10.2 us (4%)
  local copies, waits for them, and re-layouts  6.59 us (3%)
    reduce_scatter x1, waiting for transfers between devices, per_device(): lax.psum_scatter(jnp.dot(final_normed, codebook_weight, preferred_element...  40.7 us
    psum x1, waiting for transfers between devices, per_device(): summed_out = lax.psum(partial_out, 'tensor')  35 us
    psum x1, waiting for transfers between devices, per_device(): summed = lax.psum(full_proj, 'adapter')  26.9 us
    all_gather x1, blocking collectives, per_device(): lax.all_gather(attended, 'adapter', axis=0, tiled=True)  14 us
    psum x1, blocking collectives, per_device(): square_sum = lax.psum(jnp.sum(hidden_f * hidden_f, axis=-1), 'adapter')  11.7 us
    psum x1, blocking collectives, per_device(): down_q, down_v = lax.psum((down_q, down_v), 'tensor')  11.1 us
    all_to_all x1, waiting for transfers between devices, per_device(): lax.all_to_all(outgoing, 'adapter', split_axis=0, concat_axis=0, tiled=True)  10.1 us
    dot_general x1, matrix products, per_device(): jnp.dot(final_normed, codebook_weight, preferred_element_type=jnp.float32)  9.59 us
  transfers between devices with their start and end apart: 8, of which 6 were waited for; matrix products, arithmetic and copies ran while one was open for 10% of the time, Pallas kernels for 0%

commit v1 on v0

--- a/solution.py
+++ b/solution.py
@@ -10,6 +10,7 @@
 ROPE_BASE = 500000.0
 NORM_EPS = 1e-05
 ADAPTER_SCALE = 0.5
+LOGIT_PARTS = 4
 
 
 def rotate(values, positions):
@@ -26,6 +27,222 @@
         [first_half * cosine - second_half * sine, first_half * sine + second_half * cosine],
         axis=-1,
     )
+
+
+def swap(value, axis, distance):
+    size = lax.axis_size(axis)
+    return lax.ppermute(value, axis, [(i, i ^ distance) for i in range(size)])
+
+
+def take_block(array, index, size, axis=0):
+    return lax.dynamic_slice_in_dim(array, index * size, size, axis)
+
+
+def per_device_four(
+    tokens,
+    attention_gain,
+    query_weight,
+    key_weight,
+    value_weight,
+    speaker_question_lowering,
+    speaker_question_raising,
+    speaker_content_lowering,
+    speaker_content_raising,
+    rotated_key_cache,
+    stored_value_cache,
+    sequence_speaker_label,
+    lengths,
+    output_weight,
+    closing_gain,
+    codebook_weight,
+    delays,
+):
+    n_adapter = lax.axis_size("adapter")
+    peers = range(1, n_adapter)
+    a = lax.axis_index("adapter")
+    t = lax.axis_index("tensor")
+    core = t % 2
+    str_dev, model_width = tokens.shape
+    half = str_dev // 2
+    d_slice = model_width // n_adapter
+    voices, rank = speaker_question_raising.shape[:2]
+    query_columns = query_weight.shape[1]
+    key_value_columns = key_weight.shape[1]
+
+    tok_f = tokens.astype(jnp.float32)
+    inverse = lax.rsqrt(jnp.mean(tok_f * tok_f, axis=-1, keepdims=True) + NORM_EPS)
+    normed = (tok_f * inverse * attention_gain).astype(jnp.bfloat16)
+
+    my_half = take_block(normed, core, half)
+    came = [swap(take_block(my_half, a ^ k, d_slice, 1), "adapter", k) for k in peers]
+
+    slot_cap = max(2, 2 * str_dev // n_adapter)
+    owner_ids = sequence_speaker_label // voices
+    local_voice = sequence_speaker_label % voices
+    same_owner = owner_ids[:, None] == owner_ids[None, :]
+    earlier = jnp.arange(str_dev)[:, None] > jnp.arange(str_dev)[None, :]
+    owner_rank = jnp.sum((same_owner & earlier).astype(jnp.int32), axis=1)
+    slot_ids = (owner_ids ^ a) * slot_cap + owner_rank
+    placing = (slot_ids[None, :] == jnp.arange(n_adapter * slot_cap)[:, None]).astype(jnp.bfloat16)
+    voice_onehot = (local_voice[:, None] == jnp.arange(128)[None, :]).astype(jnp.bfloat16)
+    sent_rows = jnp.dot(
+        placing,
+        jnp.concatenate([take_block(normed, t, d_slice, 1), voice_onehot], axis=1),
+        preferred_element_type=jnp.float32,
+    ).astype(jnp.bfloat16)
+    rows_in = [sent_rows[:slot_cap]] + [
+        swap(sent_rows[k * slot_cap : (k + 1) * slot_cap], "adapter", k) for k in peers
+    ]
+
+    came = jnp.stack(came)
+    other = swap(came, "tensor", 1)
+    first = jnp.where(core == 0, came, other)
+    second = jnp.where(core == 0, other, came)
+    arrived = jnp.concatenate([first, second], axis=1).reshape(-1, d_slice)
+    norm_cols = jnp.concatenate([take_block(normed, a, d_slice, 1), arrived], axis=0)
+    base = jnp.concatenate(
+        [
+            jnp.dot(norm_cols, weight, preferred_element_type=jnp.float32)
+            for weight in (query_weight, key_weight, value_weight)
+        ],
+        axis=1,
+    )
+    projected = base[:str_dev]
+    for k in peers:
+        projected = projected + swap(base[k * str_dev : (k + 1) * str_dev], "adapter", k)
+
+    rows = jnp.concatenate(rows_in, axis=0)
+    onehot_b = rows[:, d_slice : d_slice + voices]
+    onehot_f = onehot_b.astype(jnp.float32)
+    flat_rows = rows[:, :d_slice]
+    downs = []
+    for lowering in (speaker_question_lowering, speaker_content_lowering):
+        every = jnp.dot(
+            flat_rows, lowering.reshape(d_slice, voices * rank), preferred_element_type=jnp.float32
+        )
+        downs.append(jnp.sum(onehot_f[:, :, None] * every.reshape(-1, voices, rank), axis=1))
+    down = jnp.concatenate(downs, axis=1)
+    down = down + swap(down, "tensor", 1)
+    down = (down + swap(down, "tensor", 2)).astype(jnp.bfloat16)
+    ups = []
+    for i, raising in enumerate((speaker_question_raising, speaker_content_raising)):
+        spread = (
+            onehot_b[:, :, None] * down[:, None, i * rank : (i + 1) * rank]
+        ).reshape(-1, voices * rank)
+        up = jnp.dot(
+            spread, raising.reshape(voices * rank, -1), preferred_element_type=jnp.float32
+        )
+        ups.append((up * ADAPTER_SCALE).astype(jnp.bfloat16))
+    outgoing = jnp.concatenate(ups, axis=1)
+    returned = jnp.concatenate(
+        [outgoing[:slot_cap]]
+        + [swap(outgoing[k * slot_cap : (k + 1) * slot_cap], "adapter", k) for k in peers],
+        axis=0,
+    )
+    adapter_summands = jnp.einsum(
+        "ms,mc->sc", placing, returned, preferred_element_type=jnp.float32
+    )
+
+    kv_local, ctx_len, head_dim = rotated_key_cache.shape[1:]
+    group_size = query_columns // (kv_local * head_dim)
+    query = rotate(
+        (projected[:, :query_columns] + adapter_summands[:, :query_columns]).reshape(
+            str_dev, kv_local, group_size, head_dim
+        ),
+        lengths,
+    ).astype(jnp.bfloat16)
+    key_base = projected[:, query_columns : query_columns + key_value_columns]
+    key_new = rotate(key_base.reshape(str_dev, kv_local, head_dim), lengths).astype(jnp.bfloat16)
+    value_new = (
+        (projected[:, query_columns + key_value_columns :] + adapter_summands[:, query_columns:])
+        .reshape(str_dev, kv_local, head_dim)
+        .astype(jnp.bfloat16)
+    )
+    scale_factor = 1.0 / head_dim**0.5
+    scores = (
+        jnp.einsum("skgd,skcd->skgc", query, rotated_key_cache, preferred_element_type=jnp.float32)
+        * scale_factor
+    )
+    own_score = (
+        jnp.einsum("skgd,skd->skg", query, key_new, preferred_element_type=jnp.float32)
+        * scale_factor
+    )
+    valid = (jnp.arange(ctx_len)[None, :] < lengths[:, None])[:, None, None, :]
+    masked = jnp.where(valid, scores, -1e30)
+    top_score = jnp.maximum(jnp.max(masked, axis=-1), own_score)
+    weights_all = jnp.where(valid, jnp.exp(scores - top_score[..., None]), 0.0)
+    own_weight = jnp.exp(own_score - top_score)
+    total = jnp.sum(weights_all, axis=-1) + own_weight
+    probs = (weights_all / total[..., None]).astype(jnp.bfloat16)
+    own_prob = (own_weight / total).astype(jnp.bfloat16)
+    mixed = jnp.einsum(
+        "skgc,skcd->skgd", probs, stored_value_cache, preferred_element_type=jnp.float32
+    )
+    mixed = (
+        mixed
+        + own_prob.astype(jnp.float32)[..., None] * value_new.astype(jnp.float32)[:, :, None, :]
+    )
+    attended = mixed.astype(jnp.bfloat16).reshape(str_dev, query_columns)
+
+    raw = lax.ppermute(
+        take_block(tokens, t, d_slice, 1),
+        ("adapter", "tensor"),
+        [(i * n_adapter + j, j * n_adapter + i) for i in range(n_adapter) for j in range(n_adapter)],
+    )
+    gathered = jnp.concatenate(
+        [attended] + [swap(attended, "adapter", k) for k in peers], axis=0
+    )
+    partial_out = jnp.dot(gathered, output_weight, preferred_element_type=jnp.float32)
+    turn = a ^ t
+    near = swap(
+        jnp.concatenate(
+            [take_block(partial_out, turn ^ 1, str_dev), take_block(partial_out, turn ^ 3, str_dev)]
+        ),
+        "tensor",
+        1,
+    )
+    far = take_block(partial_out, turn ^ 2, str_dev) + near[str_dev:]
+    summed_out = take_block(partial_out, turn, str_dev) + near[:str_dev] + swap(far, "tensor", 2)
+    hidden_out = (raw.astype(jnp.float32) + summed_out).astype(jnp.bfloat16)
+
+    hidden_f = hidden_out.astype(jnp.float32)
+    square = jnp.sum(hidden_f * hidden_f, axis=-1)
+    square_pair = jnp.stack([square, swap(square, "tensor", 2)])
+    squares = jnp.concatenate([square_pair, swap(square_pair, "tensor", 1)]).reshape(-1)
+    square_sum = squares
+    for k in peers:
+        square_sum = square_sum + swap(squares, "adapter", k)
+    hidden_pair = jnp.concatenate([hidden_out, swap(hidden_out, "tensor", 2)])
+    hidden_all = jnp.concatenate([hidden_pair, swap(hidden_pair, "tensor", 1)])
+    final_slice = take_block(closing_gain, a, d_slice)
+    final_normed = (
+        hidden_all.astype(jnp.float32)
+        * lax.rsqrt(square_sum / model_width + NORM_EPS)[:, None]
+        * final_slice
+    ).astype(jnp.bfloat16)
+
+    books_local = CB // lax.axis_size("tensor")
+    book_delays = take_block(delays, t, books_local)
+    active = (lengths[:, None] >= book_delays[None, :]).astype(jnp.float32)
+    place = jnp.array([0, 2, 1, 3], jnp.int32)
+    parts = LOGIT_PARTS
+    width = codebook_weight.shape[1] // parts
+    outs = []
+    for p in range(parts):
+        partial = jnp.dot(
+            final_normed,
+            codebook_weight[:, p * width : (p + 1) * width],
+            preferred_element_type=jnp.float32,
+        )
+        total_p = take_block(partial, place[turn], str_dev)
+        for k in peers:
+            block = take_block(partial, place[turn ^ k], str_dev)
+            total_p = total_p + swap(
+                (block * 32.0).astype(jnp.float16), "adapter", k
+            ).astype(jnp.float32) * (1.0 / 32.0)
+        outs.append(total_p)
+    logits = jnp.concatenate(outs, axis=1).reshape(str_dev, books_local, VOC) * active[:, :, None]
+    return (hidden_out, logits)
 
 
 def per_device(
@@ -235,6 +452,7 @@
         P(),
     )
     out_specs = (P(("groups", "tensor"), "adapter"), P(("groups", "adapter"), "tensor", None))
+    four = mesh.shape["adapter"] == 4 and mesh.shape["tensor"] == 4
     return jax.shard_map(
-        per_device, mesh=mesh, in_specs=in_specs, out_specs=out_specs, check_vma=False
-    )
+        per_device_four if four else per_device, mesh=mesh, in_specs=in_specs, out_specs=out_specs, check_vma=False
+    )

time: 236 us -> 155 us (0.66)
  waiting for transfers between devices: 119 us -> 36.4 us
  blocking collectives: 36.8 us -> 0 us
  starting transfers between devices: 21.5 us -> 57.8 us
  local copies, waits for them, and re-layouts: 6.59 us -> 18 us
  between operations: 13.9 us -> 3.85 us
  other arithmetic: 10.2 us -> 14 us
    psum x2 -> x0, waiting for transfers between devices: 61.8 us -> none  [the longest x1 35 us: per_device(): summed_out = lax.psum(partial_out, 'tensor')]
    ppermute x0 -> x40, starting transfers between devices: none -> 57.8 us  [the longest x39 56.2 us: swap(): return lax.ppermute(value, axis, [(i, i ^ distance) for i in range(size)])]
    reduce_scatter x1 -> x0, waiting for transfers between devices: 40.7 us -> none  [per_device(): lax.psum_scatter(jnp.dot(final_normed, codebook_weight, preferred_element...]
    ppermute x0 -> x40, waiting for transfers between devices: none -> 36.4 us  [the longest x39 36.4 us: swap(): return lax.ppermute(value, axis, [(i, i ^ distance) for i in range(size)])]
    psum x2 -> x0, blocking collectives: 22.8 us -> none  [the longest x1 11.7 us: per_device(): square_sum = lax.psum(jnp.sum(hidden_f * hidden_f, axis=-1), 'adapter')]
    all_to_all x5 -> x0, starting transfers between devices: 21.4 us -> none  [the longest x1 6.32 us: per_device(): lax.all_to_all(send_voice, 'adapter', split_axis=0, concat_axis=0, tiled=...]
    all_to_all x5 -> x0, waiting for transfers between devices: 16.6 us -> none  [the longest x1 10.1 us: per_device(): lax.all_to_all(outgoing, 'adapter', split_axis=0, concat_axis=0, tiled=True)]
    all_gather x1 -> x0, blocking collectives: 14 us -> none  [per_device(): lax.all_gather(attended, 'adapter', axis=0, tiled=True)]
  transfers between devices with their start and end apart: 8 -> 40, of which waited for: 6 -> 16; matrix products, arithmetic and copies ran while one was open for 10% -> 24% of each run, Pallas kernels for 0% -> 0%
where the time goes in v1:
time: 155 us; the launch traced here: 154 us
  starting transfers between devices  57.8 us (37%)
  waiting for transfers between devices  36.4 us (23%)
  matrix products  24.3 us (16%)
  local copies, waits for them, and re-layouts  18 us (12%)
  other arithmetic  14 us (9%)
  between operations  3.85 us (2%)
    ppermute x39, starting transfers between devices, swap(): return lax.ppermute(value, axis, [(i, i ^ distance) for i in range(size)])  56.2 us
    ppermute x39, waiting for transfers between devices, swap(): return lax.ppermute(value, axis, [(i, i ^ distance) for i in range(size)])  36.4 us
    dot_general x4, matrix products, per_device_four(): jnp.dot(final_normed, codebook_weight[:, p * width:(p + 1) * width], pref...  11.9 us
    ppermute x3, local copies, waits for them, and re-layouts, swap(): return lax.ppermute(value, axis, [(i, i ^ distance) for i in range(size)])  5.09 us
    slice x3, local copies, waits for them, and re-layouts, per_device_four(): sent_rows[k * slot_cap:(k + 1) * slot_cap]  4.63 us
    dot_general x3, matrix products, per_device_four(): jnp.dot(norm_cols, weight, preferred_element_type=jnp.float32)  3.52 us
    dynamic_slice x6, local copies, waits for them, and re-layouts, take_block(): return lax.dynamic_slice_in_dim(array, index * size, size, axis)  3.23 us
  transfers between devices with their start and end apart: 40, of which 16 were waited for; matrix products, arithmetic and copies ran while one was open for 24% of the time, Pallas kernels for 0%

profile of v1, /device:TPU:0, one launch (start us, length us, event | category | flops | bytes accessed | tf_op | source)
XLA Modules:
  0.0 154.4 jit_solution(3017769860746144813)
XLA Ops:
  0.7 1.4 fusion.29
  2.1 1.2 fusion.31
  3.3 0.8 fusion.112
  4.2 3.0 %collective-permute-start.1 = (bf16[16,2048]{1,0:T(8,128)(2,1)}, bf16[16,2048]{1,0:T(8,128)(2,1)S(1)}, u32[]{:S(2)}, u32[]{:S(2)}) collective-permute-start(bf16[16,2048]{1,0:T(8,128)(2,1)} %get-tuple-element.29), channel_id=1, source_target_pairs={{0,4},{4,0},{8,12},{12,8},{1,5},{5,1},{9,13},{13,9},{2,6},{6,2},{1... | collective-permute-start | bytes 196616 | tf_op jit(solution)/shard_map/ppermute | solution.py:34
  7.2 2.6 %collective-permute-start.2 = (bf16[16,2048]{1,0:T(8,128)(2,1)}, bf16[16,2048]{1,0:T(8,128)(2,1)S(1)}, u32[]{:S(2)}, u32[]{:S(2)}) collective-permute-start(bf16[16,2048]{1,0:T(8,128)(2,1)} %get-tuple-element.31), channel_id=1, source_target_pairs={{0,8},{4,12},{8,0},{12,4},{1,9},{5,13},{9,1},{13,5},{2,10},{6,14},... | collective-permute-start | bytes 196616 | tf_op jit(solution)/shard_map/ppermute | solution.py:34
  9.8 0.7 and_select_fusion.1
  11.1 1.6 %fusion.111 = (bf16[16,2176]{0,1:T(8,128)(2,1)S(1)}, bf16[16,2176]{0,1:T(8,128)(2,1)S(1)}, bf16[16,2176]{0,1:T(8,128)(2,1)}, bf16[16,2176]{0,1:T(8,128)(2,1)}) fusion(bf16[64,2176]{0,1:T(8,128)(2,1)S(1)} %convolution_convert_fusion), kind=kLoop, calls=%fused_computation.193 | loop fusion | bytes 557056 | tf_op jit(solution)/shard_map/slice | solution.py:93
  12.6 1.9 %copy.37 = bf16[16,2176]{1,0:T(8,128)(2,1)} copy(bf16[16,2176]{0,1:T(8,128)(2,1)} %get-tuple-element.14) | data formatting | bytes 139264 | tf_op jit(solution)/shard_map/slice | solution.py:94
  15.0 1.9 %copy.38 = bf16[16,2176]{1,0:T(8,128)(2,1)} copy(bf16[16,2176]{0,1:T(8,128)(2,1)} %get-tuple-element.13) | data formatting | bytes 139264 | tf_op jit(solution)/shard_map/slice | solution.py:94
  16.9 0.8 copy.39
  17.7 3.9 %collective-permute-start.10 = (bf16[16,2176]{1,0:T(8,128)(2,1)}, bf16[16,2176]{1,0:T(8,128)(2,1)}, u32[]{:S(2)}, u32[]{:S(2)}) collective-permute-start(bf16[16,2176]{1,0:T(8,128)(2,1)} %copy.39), channel_id=1, source_target_pairs={{0,12},{4,8},{8,4},{12,0},{1,13},{5,9},{9,5},{13,1},{2,14},{6,10},... | collective-permute-start | bytes 208904 | tf_op jit(solution)/shard_map/ppermute | solution.py:34
  21.7 0.7 convert_element_type.169
  22.3 0.7 multiply_cosine_fusion.1
  23.7 1.2 copy.40
  25.3 2.0 %copy.41 = bf16[16,2176]{0,1:T(8,128)(2,1)} copy(bf16[16,2176]{1,0:T(8,128)(2,1)} %collective-permute-done.9) | data formatting | bytes 139264 | tf_op jit(solution)/shard_map/ppermute | solution.py:34
  27.2 1.9 %copy.42 = bf16[16,2176]{0,1:T(8,128)(2,1)} copy(bf16[16,2176]{1,0:T(8,128)(2,1)} %collective-permute-done.10) | data formatting | bytes 139264 | tf_op jit(solution)/shard_map/ppermute | solution.py:34
  29.2 0.9 fusion.109
  30.1 1.9 %fusion.34 = bf16[64,2048,1]{0,1,2:T(8,128)(2,1)S(1)} fusion(bf16[16,2176]{0,1:T(8,128)(2,1)} %copy.42, bf16[16,2176]{0,1:T(8,128)(2,1)} %copy.41, bf16[16,2176]{0,1:T(8,128)(2,1)S(1)} %copy.40, bf16[16,2176]{0,1:T(8,128)(2,1)S(1)} %get-tuple-element.11), kind=kLoop, calls=%fused_computation.36 | loop fusion | flops 1048576 | bytes 540672 | tf_op jit(solution)/shard_map/slice | solution.py:117
  32.0 1.0 fusion.23
  33.1 1.0 fusion.20
  34.3 1.1 collective-permute-done.11
  35.5 1.5 collective-permute-start.12
  37.1 2.3 %collective-permute-done.12 = f32[64,128]{1,0:T(8,128)S(1)} collective-permute-done((f32[64,128]{1,0:T(8,128)S(1)}, f32[64,128]{1,0:T(8,128)S(1)}, u32[]{:S(2)}, u32[]{:S(2)}) %collective-permute-start.12) | collective-permute-done | bytes 32800 | tf_op jit(solution)/shard_map/ppermute | solution.py:34
  39.8 1.7 %fusion.19 = bf16[64,1024]{1,0:T(8,128)(2,1)S(1)} fusion(bf16[8,64,1024]{2,1,0:T(8,128)(2,1)} %param.24, bf16[64,64]{1,0:T(8,128)(2,1)S(1)} %get-tuple-element.46, bf16[64,8]{0,1:T(8,128)(2,1)S(1)} %get-tuple-element.5), kind=kOutput, calls=%fused_computation.19 | convolution fusion | flops 67272704 | bytes 1188864 | tf_op jit(solution)/shard_map/dot_general | solution.py:132
  41.6 4.0 %collective-permute-start.14 = (bf16[16,1152]{1,0:T(8,128)(2,1)S(1)}, bf16[16,1152]{1,0:T(8,128)(2,1)S(1)}, u32[]{:S(2)}, u32[]{:S(2)}) collective-permute-start(bf16[16,1152]{1,0:T(8,128)(2,1)S(1)} %get-tuple-element.41), channel_id=1, source_target_pairs={{0,8},{4,12},{8,0},{12,4},{1,9},{5,13},{9,1},{13,5},{2,10},{6,14},... | collective-permute-start | bytes 110600 | tf_op jit(solution)/shard_map/ppermute | solution.py:34
  46.0 2.9 %fusion.50 = f32[128,1024]{1,0:T(8,128)S(1)} fusion(bf16[2048,1024]{1,0:T(8,128)(2,1)} %param.20, bf16[96,2048]{1,0:T(8,128)(2,1)S(1)} %bitcast.86, bf16[32,2048]{1,0:T(8,128)(2,1)S(1)} %get-tuple-element.27), kind=kOutput, calls=%fused_computation.70 | convolution fusion | flops 537919488 | bytes 5242880 | tf_op jit(solution)/shard_map/dot_general | solution.py:105
  50.0 3.8 %collective-permute-start.6 = (f32[32,1280]{1,0:T(8,128)S(1)}, f32[32,1280]{1,0:T(8,128)S(1)}, u32[]{:S(2)}, u32[]{:S(2)}) collective-permute-start(f32[32,1280]{1,0:T(8,128)S(1)} %get-tuple-element.10), channel_id=1, source_target_pairs={{0,8},{4,12},{8,0},{12,4},{1,9},{5,13},{9,1},{13,5},{2,10},{6,14},... | collective-permute-start | bytes 491528 | tf_op jit(solution)/shard_map/ppermute | solution.py:34
  54.4 2.1 %collective-permute-done.5 = f32[32,1280]{1,0:T(8,128)S(1)} collective-permute-done((f32[32,1280]{1,0:T(8,128)S(1)}, f32[32,1280]{1,0:T(8,128)S(1)}, u32[]{:S(2)}, u32[]{:S(2)}) %collective-permute-start.5) | collective-permute-done | bytes 163872 | tf_op jit(solution)/shard_map/ppermute | solution.py:34
  56.5 8.4 %collective-permute-done.6 = f32[32,1280]{1,0:T(8,128)S(1)} collective-permute-done((f32[32,1280]{1,0:T(8,128)S(1)}, f32[32,1280]{1,0:T(8,128)S(1)}, u32[]{:S(2)}, u32[]{:S(2)}) %collective-permute-start.6) | collective-permute-done | bytes 163872 | tf_op jit(solution)/shard_map/ppermute | solution.py:34
  65.6 0.8 select_reduce_fusion
  67.1 2.4 %collective-permute-start.16 = (bf16[32,1024]{1,0:T(8,128)(2,1)S(1)}, bf16[32,1024]{1,0:T(8,128)(2,1)S(1)}, u32[]{:S(2)}, u32[]{:S(2)}) collective-permute-start(bf16[32,1024]{1,0:T(8,128)(2,1)S(1)} %bitcast.90), channel_id=1, source_target_pairs={{0,4},{4,0},{8,12},{12,8},{1,5},{5,1},{9,13},{13,9},{2,6},{6,2},{1... | collective-permute-start | bytes 196616 | tf_op jit(solution)/shard_map/ppermute | solution.py:34
  69.5 1.1 collective-permute-start.17
  70.5 1.4 collective-permute-start.18
  71.9 3.4 %collective-permute-done.17 = bf16[32,1024]{1,0:T(8,128)(2,1)S(1)} collective-permute-done((bf16[32,1024]{1,0:T(8,128)(2,1)S(1)}, bf16[32,1024]{1,0:T(8,128)(2,1)S(1)}, u32[]{:S(2)}, u32[]{:S(2)}) %collective-permute-start.17) | collective-permute-done | bytes 65568 | tf_op jit(solution)/shard_map/ppermute | solution.py:34
  75.3 1.4 collective-permute-done.18
  76.7 2.9 %fusion.38 = f32[128,2048]{1,0:T(8,128)S(1)} fusion(bf16[1024,2048]{1,0:T(8,128)(2,1)} %param.31, bf16[32,1024]{1,0:T(8,128)(2,1)S(1)} %collective-permute-done.18, bf16[32,1024]{1,0:T(8,128)(2,1)S(1)} %collective-permute-done.17, bf16[32,1024]{1,0:T(8,128)(2,1)S(1)} %collective-permute-done.16, bf16[32,1024]{1,0:T(8,128)(2,1)S(1)} %bitcast.93), kind=kOutput, calls=%fused_computation.48 | convolution fusion | flops 537919488 | bytes 5505024 | tf_op jit(solution)/shard_map/dot_general | solution.py:195
  79.7 0.8 pad_maximum_fusion.5
  80.5 2.2 %collective-permute-done.19 = f32[64,2048]{1,0:T(8,128)} collective-permute-done((f32[64,2048]{1,0:T(8,128)}, f32[64,2048]{1,0:T(8,128)}, u32[]{:S(2)}, u32[]{:S(2)}) %collective-permute-start.19) | collective-permute-done | bytes 524320 | tf_op jit(solution)/shard_map/ppermute | solution.py:34
  82.7 1.7 %slice_add_fusion = f32[32,2048]{1,0:T(8,128)} fusion(f32[64,2048]{1,0:T(8,128)} %collective-permute-done.19, f32[128,2048]{1,0:T(8,128)S(1)} %fusion.38, s32[]{:T(128)S(6)} %select_n.151), kind=kLoop, calls=%fused_computation.43 | loop fusion | flops 65536 | bytes 786436 | tf_op jit(solution)/shard_map/add | solution.py:204
  84.4 1.5 collective-permute-start.20
  85.9 1.6 %constant_dynamic-slice_fusion.4 = bf16[32,2048]{1,0:T(8,128)(2,1)} fusion(bf16[32,8192]{1,0:T(8,128)(2,1)} %param.18, s32[]{:T(128)S(6)} %select_n.130), kind=kLoop, calls=%fused_computation.167 | loop fusion | bytes 262148 | tf_op jit(solution)/shard_map/dynamic_slice | solution.py:38
  87.5 1.6 %collective-permute-start = (bf16[32,2048]{1,0:T(8,128)(2,1)}, bf16[32,2048]{1,0:T(8,128)(2,1)S(1)}, u32[]{:S(2)}, u32[]{:S(2)}) collective-permute-start(bf16[32,2048]{1,0:T(8,128)(2,1)} %constant_dynamic-slice_fusion.4), channel_id=1, source_target_pairs={{0,0},{1,4},{2,8},{3,12},{4,1},{5,5},{6,9},{7,13},{8,2},{9,6},{10,... | collective-permute-start | bytes 393224 | tf_op jit(solution)/shard_map/ppermute | solution.py:187
  89.8 3.2 %collective-permute-done.20 = f32[32,2048]{1,0:T(8,128)S(1)} collective-permute-done((f32[32,2048]{1,0:T(8,128)}, f32[32,2048]{1,0:T(8,128)S(1)}, u32[]{:S(2)}, u32[]{:S(2)}) %collective-permute-start.20) | collective-permute-done | bytes 262176 | tf_op jit(solution)/shard_map/ppermute | solution.py:34
  93.0 1.1 multiply_reduce_fusion
  94.1 7.6 %collective-permute-start.21 = (bf16[32,2048]{1,0:T(8,128)(2,1)S(1)}, bf16[32,2048]{1,0:T(8,128)(2,1)S(1)}, u32[]{:S(2)}, u32[]{:S(2)}) collective-permute-start(bf16[32,2048]{1,0:T(8,128)(2,1)S(1)} %get-tuple-element.3), channel_id=1, source_target_pairs={{0,2},{1,3},{2,0},{3,1},{4,6},{5,7},{6,4},{7,5},{8,10},{9,11},{10,... | collective-permute-start | bytes 393224 | tf_op jit(solution)/shard_map/ppermute | solution.py:34
  101.8 0.7 fusion.114
  105.1 3.5 %collective-permute-done.23 = f32[32]{0:T(128)S(1)} collective-permute-done((f32[32]{0:T(128)S(1)}, f32[32]{0:T(128)S(1)}, u32[]{:S(2)}, u32[]{:S(2)}) %collective-permute-start.23) | collective-permute-done | bytes 160 | tf_op jit(solution)/shard_map/ppermute | solution.py:34
  110.0 4.3 %collective-permute-start.27 = (f32[128]{0:T(128)S(1)}, f32[128]{0:T(128)S(1)}, u32[]{:S(2)}, u32[]{:S(2)}) collective-permute-start(f32[128]{0:T(128)S(1)} %reshape.338), channel_id=1, source_target_pairs={{0,12},{4,8},{8,4},{12,0},{1,13},{5,9},{9,5},{13,1},{2,14},{6,10},... | collective-permute-start | bytes 1544 | tf_op jit(solution)/shard_map/ppermute | solution.py:34
  114.3 0.7 dynamic_slice.119
  115.1 0.7 collective-permute-done.27
  115.9 0.7 copy-done.14
  116.6 2.9 %fusion.6 = f32[128,1024]{1,0:T(8,128)S(1)} fusion(bf16[2048,4096]{1,0:T(8,128)(2,1)} %param.33, bf16[64,2048]{1,0:T(8,128)(2,1)S(1)} %collective-permute-done.22, bf16[32,2048]{1,0:T(8,128)(2,1)S(1)} %collective-permute-done.21, bf16[32,2048]{1,0:T(8,128)(2,1)S(1)} %get-tuple-element.3, f32[2048]{0:T(1024)S(1)} %dynamic_slice.119, f32[128]{0:T(128)S(1)} %add_rsqrt_fusion), kind=kOutput, calls=%fused_computation.6 | convolution fusion | flops 539230208 | bytes 5251584 | tf_op jit(solution)/shard_map/dot_general | solution.py:232
  120.2 3.8 %collective-permute-start.29 = (f16[32,1024]{1,0:T(8,128)(2,1)S(1)}, f16[32,1024]{1,0:T(8,128)(2,1)S(1)}, u32[]{:S(2)}, u32[]{:S(2)}) collective-permute-start(f16[32,1024]{1,0:T(8,128)(2,1)S(1)} %get-tuple-element.17), channel_id=1, source_target_pairs={{0,8},{4,12},{8,0},{12,4},{1,9},{5,13},{9,1},{13,5},{2,10},{6,14},... | collective-permute-start | bytes 196616 | tf_op jit(solution)/shard_map/ppermute | solution.py:34
  124.1 3.0 %fusion.4 = f32[128,1024]{1,0:T(8,128)S(1)} fusion(bf16[2048,4096]{1,0:T(8,128)(2,1)} %param.33, bf16[64,2048]{1,0:T(8,128)(2,1)} %copy-done.14, bf16[32,2048]{1,0:T(8,128)(2,1)S(1)} %collective-permute-done.21, bf16[32,2048]{1,0:T(8,128)(2,1)S(1)} %get-tuple-element.3, f32[2048]{0:T(1024)S(1)} %dynamic_slice.119, f32[128]{0:T(128)S(1)} %add_rsqrt_fusion), kind=kOutput, calls=%fused_computation.4 | convolution fusion | flops 539230208 | bytes 5251584 | tf_op jit(solution)/shard_map/dot_general | solution.py:232
  127.8 3.8 %collective-permute-start.32 = (f16[32,1024]{1,0:T(8,128)(2,1)S(1)}, f16[32,1024]{1,0:T(8,128)(2,1)S(1)}, u32[]{:S(2)}, u32[]{:S(2)}) collective-permute-start(f16[32,1024]{1,0:T(8,128)(2,1)S(1)} %get-tuple-element.20), channel_id=1, source_target_pairs={{0,8},{4,12},{8,0},{12,4},{1,9},{5,13},{9,1},{13,5},{2,10},{6,14},... | collective-permute-start | bytes 196616 | tf_op jit(solution)/shard_map/ppermute | solution.py:34
  131.6 3.0 %fusion.2 = f32[128,1024]{1,0:T(8,128)S(1)} fusion(bf16[2048,4096]{1,0:T(8,128)(2,1)} %param.33, bf16[64,2048]{1,0:T(8,128)(2,1)S(1)} %copy-done.15, bf16[32,2048]{1,0:T(8,128)(2,1)S(1)} %collective-permute-done.21, bf16[32,2048]{1,0:T(8,128)(2,1)S(1)} %get-tuple-element.3, f32[2048]{0:T(1024)S(1)} %dynamic_slice.119, f32[128]{0:T(128)S(1)} %add_rsqrt_fusion), kind=kOutput, calls=%fused_computation.2 | convolution fusion | flops 539230208 | bytes 5251584 | tf_op jit(solution)/shard_map/dot_general | solution.py:232
  134.6 3.0 %fusion = f32[128,1024]{1,0:T(8,128)S(1)} fusion(bf16[2048,4096]{1,0:T(8,128)(2,1)} %param.33, bf16[64,2048]{1,0:T(8,128)(2,1)S(1)} %copy-done.15, bf16[32,2048]{1,0:T(8,128)(2,1)S(1)} %collective-permute-done.21, bf16[32,2048]{1,0:T(8,128)(2,1)S(1)} %get-tuple-element.3, f32[2048]{0:T(1024)S(1)} %dynamic_slice.119, f32[128]{0:T(128)S(1)} %add_rsqrt_fusion), kind=kOutput, calls=%fused_computation | convolution fusion | flops 539230208 | bytes 5251584 | tf_op jit(solution)/shard_map/dot_general | solution.py:232
  138.3 3.8 %collective-permute-start.35 = (f16[32,1024]{1,0:T(8,128)(2,1)S(1)}, f16[32,1024]{1,0:T(8,128)(2,1)S(1)}, u32[]{:S(2)}, u32[]{:S(2)}) collective-permute-start(f16[32,1024]{1,0:T(8,128)(2,1)S(1)} %get-tuple-element.23), channel_id=1, source_target_pairs={{0,8},{4,12},{8,0},{12,4},{1,9},{5,13},{9,1},{13,5},{2,10},{6,14},... | collective-permute-start | bytes 196616 | tf_op jit(solution)/shard_map/ppermute | solution.py:34
  142.8 1.7 %collective-permute-done.33 = f16[32,1024]{1,0:T(8,128)(2,1)S(1)} collective-permute-done((f16[32,1024]{1,0:T(8,128)(2,1)S(1)}, f16[32,1024]{1,0:T(8,128)(2,1)S(1)}, u32[]{:S(2)}, u32[]{:S(2)}) %collective-permute-start.33) | collective-permute-done | bytes 65568 | tf_op jit(solution)/shard_map/ppermute | solution.py:34
  144.5 2.2 %collective-permute-start.38 = (f16[32,1024]{1,0:T(8,128)(2,1)S(1)}, f16[32,1024]{1,0:T(8,128)(2,1)S(1)}, u32[]{:S(2)}, u32[]{:S(2)}) collective-permute-start(f16[32,1024]{1,0:T(8,128)(2,1)S(1)} %get-tuple-element.26), channel_id=1, source_target_pairs={{0,8},{4,12},{8,0},{12,4},{1,9},{5,13},{9,1},{13,5},{2,10},{6,14},... | collective-permute-start | bytes 196616 | tf_op jit(solution)/shard_map/ppermute | solution.py:34
  147.4 1.3 collective-permute-done.36
  148.7 2.6 %collective-permute-done.38 = f16[32,1024]{1,0:T(8,128)(2,1)S(1)} collective-permute-done((f16[32,1024]{1,0:T(8,128)(2,1)S(1)}, f16[32,1024]{1,0:T(8,128)(2,1)S(1)}, u32[]{:S(2)}, u32[]{:S(2)}) %collective-permute-start.38) | collective-permute-done | bytes 65568 | tf_op jit(solution)/shard_map/ppermute | solution.py:34
  151.3 1.5 collective-permute-done.39
  153.4 1.0 broadcast_multiply_fusion
  (138 shorter events, 12.7 us)
Async XLA Ops:
  0.6 31.4 %copy-start = (bf16[2048,8,64]{0,2,1:T(8,128)(2,1)S(1)}, bf16[2048,8,64]{0,2,1:T(8,128)(2,1)}, u32[]{:S(2)}) copy-start(bf16[2048,8,64]{0,2,1:T(8,128)(2,1)} %param.23) | copy-start | bytes 6291460
  4.2 32.8 %collective-permute-start.1 = (bf16[16,2048]{1,0:T(8,128)(2,1)}, bf16[16,2048]{1,0:T(8,128)(2,1)S(1)}, u32[]{:S(2)}, u32[]{:S(2)}) collective-permute-start(bf16[16,2048]{1,0:T(8,128)(2,1)} %get-tuple-element.29), channel_id=1, source_target_pairs={{0,4},{4,0},{8,12},{12,8},{1,5},{5,1},{9,13},{13,9},{2,6},{6,2},{1... | collective-permute-start | bytes 196616 | tf_op jit(solution)/shard_map/ppermute | solution.py:34
  7.2 29.8 %collective-permute-start.2 = (bf16[16,2048]{1,0:T(8,128)(2,1)}, bf16[16,2048]{1,0:T(8,128)(2,1)S(1)}, u32[]{:S(2)}, u32[]{:S(2)}) collective-permute-start(bf16[16,2048]{1,0:T(8,128)(2,1)} %get-tuple-element.31), channel_id=1, source_target_pairs={{0,8},{4,12},{8,0},{12,4},{1,9},{5,13},{9,1},{13,5},{2,10},{6,14},... | collective-permute-start | bytes 196616 | tf_op jit(solution)/shard_map/ppermute | solution.py:34
  14.5 8.6 %collective-permute-start.8 = (bf16[16,2176]{1,0:T(8,128)(2,1)}, bf16[16,2176]{1,0:T(8,128)(2,1)S(1)}, u32[]{:S(2)}, u32[]{:S(2)}) collective-permute-start(bf16[16,2176]{1,0:T(8,128)(2,1)} %copy.37), channel_id=1, source_target_pairs={{0,4},{4,0},{8,12},{12,8},{1,5},{5,1},{9,13},{13,9},{2,6},{6,2},{1... | collective-permute-start | bytes 208904 | tf_op jit(solution)/shard_map/ppermute | solution.py:34
  16.9 8.4 %collective-permute-start.9 = (bf16[16,2176]{1,0:T(8,128)(2,1)}, bf16[16,2176]{1,0:T(8,128)(2,1)}, u32[]{:S(2)}, u32[]{:S(2)}) collective-permute-start(bf16[16,2176]{1,0:T(8,128)(2,1)} %copy.38), channel_id=1, source_target_pairs={{0,8},{4,12},{8,0},{12,4},{1,9},{5,13},{9,1},{13,5},{2,10},{6,14},... | collective-permute-start | bytes 208904 | tf_op jit(solution)/shard_map/ppermute | solution.py:34
  17.7 9.5 %collective-permute-start.10 = (bf16[16,2176]{1,0:T(8,128)(2,1)}, bf16[16,2176]{1,0:T(8,128)(2,1)}, u32[]{:S(2)}, u32[]{:S(2)}) collective-permute-start(bf16[16,2176]{1,0:T(8,128)(2,1)} %copy.39), channel_id=1, source_target_pairs={{0,12},{4,8},{8,4},{12,0},{1,13},{5,9},{9,5},{13,1},{2,14},{6,10},... | collective-permute-start | bytes 208904 | tf_op jit(solution)/shard_map/ppermute | solution.py:34
  23.1 0.6 copy-start.5
  23.7 13.2 %collective-permute-start.3 = (bf16[16,2048]{1,0:T(8,128)(2,1)}, bf16[16,2048]{1,0:T(8,128)(2,1)S(1)}, u32[]{:S(2)}, u32[]{:S(2)}) collective-permute-start(bf16[16,2048]{1,0:T(8,128)(2,1)} %get-tuple-element.30), channel_id=1, source_target_pairs={{0,12},{4,8},{8,4},{12,0},{1,13},{5,9},{9,5},{13,1},{2,14},{6,10},... | collective-permute-start | bytes 196616 | tf_op jit(solution)/shard_map/ppermute | solution.py:34
  29.2 3.9 %copy-start.1 = (bf16[2048,8,64]{0,2,1:T(8,128)(2,1)S(1)}, bf16[2048,8,64]{0,2,1:T(8,128)(2,1)}, u32[]{:S(2)}) copy-start(bf16[2048,8,64]{0,2,1:T(8,128)(2,1)} %param.25) | copy-start | bytes 6291460
  30.1 4.1 %copy-start.9 = (s32[32]{0:T(128)S(1)}, s32[32]{0:T(128)}, u32[]{:S(2)}) copy-start(s32[32]{0:T(128)} %param.30) | copy-start | bytes 388
  32.0 7.5 %copy-start.16 = (bf16[8,64,128]{2,1,0:T(8,128)(2,1)S(1)}, bf16[8,64,128]{2,1,0:T(8,128)(2,1)}, u32[]{:S(2)}) copy-start(bf16[8,64,128]{2,1,0:T(8,128)(2,1)} %param.26) | copy-start | bytes 393220
  34.2 1.2 collective-permute-start.11
  35.5 3.9 %collective-permute-start.12 = (f32[64,128]{1,0:T(8,128)S(1)}, f32[64,128]{1,0:T(8,128)S(1)}, u32[]{:S(2)}, u32[]{:S(2)}) collective-permute-start(f32[64,128]{1,0:T(8,128)S(1)} %fusion.123), channel_id=1, source_target_pairs={{0,2},{1,3},{2,0},{3,1},{4,6},{5,7},{6,4},{7,5},{8,10},{9,11},{10,... | collective-permute-start | bytes 98312 | tf_op jit(solution)/shard_map/ppermute | solution.py:34
  37.0 9.0 %collective-permute-start.4 = (bf16[3,16,2048]{2,1,0:T(8,128)(2,1)S(1)}, bf16[3,16,2048]{2,1,0:T(8,128)(2,1)S(1)}, u32[]{:S(2)}, u32[]{:S(2)}) collective-permute-start(bf16[3,16,2048]{2,1,0:T(8,128)(2,1)S(1)} %pad_maximum_fusion.9), channel_id=1, source_target_pairs={{0,1},{1,0},{2,3},{3,2},{4,5},{5,4},{6,7},{7,6},{8,9},{9,8},{10,11... | collective-permute-start | bytes 589832 | tf_op jit(solution)/shard_map/ppermute | solution.py:34
  39.8 9.2 %copy-start.12 = (bf16[2048,128]{1,0:T(8,128)(2,1)S(1)}, bf16[2048,128]{1,0:T(8,128)(2,1)}, u32[]{:S(2)}) copy-start(bf16[2048,128]{1,0:T(8,128)(2,1)} %param.21) | copy-start | bytes 1572868
  41.5 7.9 %copy-start.13 = (bf16[2048,128]{1,0:T(8,128)(2,1)S(1)}, bf16[2048,128]{1,0:T(8,128)(2,1)}, u32[]{:S(2)}) copy-start(bf16[2048,128]{1,0:T(8,128)(2,1)} %param.22) | copy-start | bytes 1572868
  41.5 12.3 %collective-permute-start.13 = (bf16[16,1152]{1,0:T(8,128)(2,1)S(1)}, bf16[16,1152]{1,0:T(8,128)(2,1)S(1)}, u32[]{:S(2)}, u32[]{:S(2)}) collective-permute-start(bf16[16,1152]{1,0:T(8,128)(2,1)S(1)} %get-tuple-element.39), channel_id=1, source_target_pairs={{0,4},{4,0},{8,12},{12,8},{1,5},{5,1},{9,13},{13,9},{2,6},{6,2},{1... | collective-permute-start | bytes 110600 | tf_op jit(solution)/shard_map/ppermute | solution.py:34
  41.6 12.6 %collective-permute-start.14 = (bf16[16,1152]{1,0:T(8,128)(2,1)S(1)}, bf16[16,1152]{1,0:T(8,128)(2,1)S(1)}, u32[]{:S(2)}, u32[]{:S(2)}) collective-permute-start(bf16[16,1152]{1,0:T(8,128)(2,1)S(1)} %get-tuple-element.41), channel_id=1, source_target_pairs={{0,8},{4,12},{8,0},{12,4},{1,9},{5,13},{9,1},{13,5},{2,10},{6,14},... | collective-permute-start | bytes 110600 | tf_op jit(solution)/shard_map/ppermute | solution.py:34
  45.6 8.6 %collective-permute-start.15 = (bf16[16,1152]{1,0:T(8,128)(2,1)S(1)}, bf16[16,1152]{1,0:T(8,128)(2,1)S(1)}, u32[]{:S(2)}, u32[]{:S(2)}) collective-permute-start(bf16[16,1152]{1,0:T(8,128)(2,1)S(1)} %get-tuple-element.40), channel_id=1, source_target_pairs={{0,12},{4,8},{8,4},{12,0},{1,13},{5,9},{9,5},{13,1},{2,14},{6,10},... | collective-permute-start | bytes 110600 | tf_op jit(solution)/shard_map/ppermute | solution.py:34
  49.0 16.2 %copy-start.6 = (f32[32,64]{1,0:T(8,128)S(1)}, f32[32,64]{1,0:T(8,128)}, u32[]{:S(2)}) copy-start(f32[32,64]{1,0:T(8,128)} %get-tuple-element.48) | copy-start | bytes 24580
  49.0 16.2 %copy-start.7 = (f32[32,64]{1,0:T(8,128)S(1)}, f32[32,64]{1,0:T(8,128)}, u32[]{:S(2)}) copy-start(f32[32,64]{1,0:T(8,128)} %get-tuple-element.49) | copy-start | bytes 24580
  49.0 16.6 %copy-start.2 = (bf16[32,1,128,128]{3,2,1,0:T(8,128)(2,1)S(1)}, bf16[32,1,128,128]{3,2,1,0:T(8,128)(2,1)}, u32[]{:S(2)}) copy-start(bf16[32,1,128,128]{3,2,1,0:T(8,128)(2,1)} %param.27) | copy-start | bytes 3145732
  49.3 17.3 %copy-start.11 = (bf16[32,1,128,128]{3,2,1,0:T(8,128)(2,1)S(1)}, bf16[32,1,128,128]{3,2,1,0:T(8,128)(2,1)}, u32[]{:S(2)}) copy-start(bf16[32,1,128,128]{3,2,1,0:T(8,128)(2,1)} %param.28) | copy-start | bytes 3145732
  49.8 6.7 %collective-permute-start.5 = (f32[32,1280]{1,0:T(8,128)S(1)}, f32[32,1280]{1,0:T(8,128)S(1)}, u32[]{:S(2)}, u32[]{:S(2)}) collective-permute-start(f32[32,1280]{1,0:T(8,128)S(1)} %get-tuple-element.8), channel_id=1, source_target_pairs={{0,4},{4,0},{8,12},{12,8},{1,5},{5,1},{9,13},{13,9},{2,6},{6,2},{1... | collective-permute-start | bytes 491528 | tf_op jit(solution)/shard_map/ppermute | solution.py:34
  50.0 14.9 %collective-permute-start.6 = (f32[32,1280]{1,0:T(8,128)S(1)}, f32[32,1280]{1,0:T(8,128)S(1)}, u32[]{:S(2)}, u32[]{:S(2)}) collective-permute-start(f32[32,1280]{1,0:T(8,128)S(1)} %get-tuple-element.10), channel_id=1, source_target_pairs={{0,8},{4,12},{8,0},{12,4},{1,9},{5,13},{9,1},{13,5},{2,10},{6,14},... | collective-permute-start | bytes 491528 | tf_op jit(solution)/shard_map/ppermute | solution.py:34
  53.8 11.1 %collective-permute-start.7 = (f32[32,1280]{1,0:T(8,128)S(1)}, f32[32,1280]{1,0:T(8,128)S(1)}, u32[]{:S(2)}, u32[]{:S(2)}) collective-permute-start(f32[32,1280]{1,0:T(8,128)S(1)} %get-tuple-element.9), channel_id=1, source_target_pairs={{0,12},{4,8},{8,4},{12,0},{1,13},{5,9},{9,5},{13,1},{2,14},{6,10},... | collective-permute-start | bytes 491528 | tf_op jit(solution)/shard_map/ppermute | solution.py:34
  67.1 4.8 %collective-permute-start.16 = (bf16[32,1024]{1,0:T(8,128)(2,1)S(1)}, bf16[32,1024]{1,0:T(8,128)(2,1)S(1)}, u32[]{:S(2)}, u32[]{:S(2)}) collective-permute-start(bf16[32,1024]{1,0:T(8,128)(2,1)S(1)} %bitcast.90), channel_id=1, source_target_pairs={{0,4},{4,0},{8,12},{12,8},{1,5},{5,1},{9,13},{13,9},{2,6},{6,2},{1... | collective-permute-start | bytes 196616 | tf_op jit(solution)/shard_map/ppermute | solution.py:34
  69.5 5.9 %collective-permute-start.17 = (bf16[32,1024]{1,0:T(8,128)(2,1)S(1)}, bf16[32,1024]{1,0:T(8,128)(2,1)S(1)}, u32[]{:S(2)}, u32[]{:S(2)}) collective-permute-start(bf16[32,1024]{1,0:T(8,128)(2,1)S(1)} %bitcast.91), channel_id=1, source_target_pairs={{0,8},{4,12},{8,0},{12,4},{1,9},{5,13},{9,1},{13,5},{2,10},{6,14},... | collective-permute-start | bytes 196616 | tf_op jit(solution)/shard_map/ppermute | solution.py:34
  70.5 6.2 %collective-permute-start.18 = (bf16[32,1024]{1,0:T(8,128)(2,1)S(1)}, bf16[32,1024]{1,0:T(8,128)(2,1)S(1)}, u32[]{:S(2)}, u32[]{:S(2)}) collective-permute-start(bf16[32,1024]{1,0:T(8,128)(2,1)S(1)} %bitcast.92), channel_id=1, source_target_pairs={{0,12},{4,8},{8,4},{12,0},{1,13},{5,9},{9,5},{13,1},{2,14},{6,10},... | collective-permute-start | bytes 196616 | tf_op jit(solution)/shard_map/ppermute | solution.py:34
  71.9 17.1 %copy-start.17 = (s32[8]{0:T(128)S(1)}, s32[8]{0:T(128)}, u32[]{:S(2)}) copy-start(s32[8]{0:T(128)} %param.34) | copy-start | bytes 100
  71.9 29.8 %copy-start.10 = (s32[32]{0:T(128)S(1)}, s32[32]{0:T(128)}, u32[]{:S(2)}) copy-start(s32[32]{0:T(128)} %param.30) | copy-start | bytes 388
  71.9 29.9 %copy-start.8 = (s32[4]{0:T(128)S(1)}, s32[4]{0:T(128)}, u32[]{:S(2)}) copy-start(s32[4]{0:T(128)} %constant.128.clone) | copy-start | bytes 52
  80.5 2.3 %collective-permute-start.19 = (f32[64,2048]{1,0:T(8,128)}, f32[64,2048]{1,0:T(8,128)}, u32[]{:S(2)}, u32[]{:S(2)}) collective-permute-start(f32[64,2048]{1,0:T(8,128)} %pad_maximum_fusion.5), channel_id=1, source_target_pairs={{0,1},{1,0},{2,3},{3,2},{4,5},{5,4},{6,7},{7,6},{8,9},{9,8},{10,11... | collective-permute-start | bytes 1572872 | tf_op jit(solution)/shard_map/ppermute | solution.py:34
  84.4 8.6 %collective-permute-start.20 = (f32[32,2048]{1,0:T(8,128)}, f32[32,2048]{1,0:T(8,128)S(1)}, u32[]{:S(2)}, u32[]{:S(2)}) collective-permute-start(f32[32,2048]{1,0:T(8,128)} %slice_add_fusion), channel_id=1, source_target_pairs={{0,2},{1,3},{2,0},{3,1},{4,6},{5,7},{6,4},{7,5},{8,10},{9,11},{10,... | collective-permute-start | bytes 786440 | tf_op jit(solution)/shard_map/ppermute | solution.py:34
  87.5 1.6 %collective-permute-start = (bf16[32,2048]{1,0:T(8,128)(2,1)}, bf16[32,2048]{1,0:T(8,128)(2,1)S(1)}, u32[]{:S(2)}, u32[]{:S(2)}) collective-permute-start(bf16[32,2048]{1,0:T(8,128)(2,1)} %constant_dynamic-slice_fusion.4), channel_id=1, source_target_pairs={{0,0},{1,4},{2,8},{3,12},{4,1},{5,5},{6,9},{7,13},{8,2},{9,6},{10,... | collective-permute-start | bytes 393224 | tf_op jit(solution)/shard_map/ppermute | solution.py:187
  89.1 0.7 copy-start.4
  94.1 40.5 %copy-start.3 = (bf16[32,2048]{1,0:T(8,128)(2,1)}, bf16[32,2048]{1,0:T(8,128)(2,1)S(1)}, u32[]{:S(2)}) copy-start(bf16[32,2048]{1,0:T(8,128)(2,1)S(1)} %get-tuple-element.3) | copy-start | bytes 393220
  94.1 14.6 %collective-permute-start.21 = (bf16[32,2048]{1,0:T(8,128)(2,1)S(1)}, bf16[32,2048]{1,0:T(8,128)(2,1)S(1)}, u32[]{:S(2)}, u32[]{:S(2)}) collective-permute-start(bf16[32,2048]{1,0:T(8,128)(2,1)S(1)} %get-tuple-element.3), channel_id=1, source_target_pairs={{0,2},{1,3},{2,0},{3,1},{4,6},{5,7},{6,4},{7,5},{8,10},{9,11},{10,... | collective-permute-start | bytes 393224 | tf_op jit(solution)/shard_map/ppermute | solution.py:34
  105.0 3.6 %collective-permute-start.23 = (f32[32]{0:T(128)S(1)}, f32[32]{0:T(128)S(1)}, u32[]{:S(2)}, u32[]{:S(2)}) collective-permute-start(f32[32]{0:T(128)S(1)} %get-tuple-element.2), channel_id=1, source_target_pairs={{0,2},{1,3},{2,0},{3,1},{4,6},{5,7},{6,4},{7,5},{8,10},{9,11},{10,... | collective-permute-start | bytes 392 | tf_op jit(solution)/shard_map/ppermute | solution.py:34
  108.7 1.2 collective-permute-start.24
  108.8 7.1 %collective-permute-start.22 = (bf16[64,2048]{1,0:T(8,128)(2,1)S(1)}, bf16[64,2048]{1,0:T(8,128)(2,1)S(1)}, u32[]{:S(2)}, u32[]{:S(2)}) collective-permute-start(bf16[64,2048]{1,0:T(8,128)(2,1)S(1)} %pad_maximum_fusion.8), channel_id=1, source_target_pairs={{0,1},{1,0},{2,3},{3,2},{4,5},{5,4},{6,7},{7,6},{8,9},{9,8},{10,11... | collective-permute-start | bytes 786440 | tf_op jit(solution)/shard_map/ppermute | solution.py:34
  110.0 5.2 %collective-permute-start.25 = (f32[128]{0:T(128)S(1)}, f32[128]{0:T(128)S(1)}, u32[]{:S(2)}, u32[]{:S(2)}) collective-permute-start(f32[128]{0:T(128)S(1)} %reshape.338), channel_id=1, source_target_pairs={{0,4},{4,0},{8,12},{12,8},{1,5},{5,1},{9,13},{13,9},{2,6},{6,2},{1... | collective-permute-start | bytes 1544 | tf_op jit(solution)/shard_map/ppermute | solution.py:34
  110.0 5.1 %collective-permute-start.26 = (f32[128]{0:T(128)S(1)}, f32[128]{0:T(128)S(1)}, u32[]{:S(2)}, u32[]{:S(2)}) collective-permute-start(f32[128]{0:T(128)S(1)} %reshape.338), channel_id=1, source_target_pairs={{0,8},{4,12},{8,0},{12,4},{1,9},{5,13},{9,1},{13,5},{2,10},{6,14},... | collective-permute-start | bytes 1544 | tf_op jit(solution)/shard_map/ppermute | solution.py:34
  110.0 5.8 %collective-permute-start.27 = (f32[128]{0:T(128)S(1)}, f32[128]{0:T(128)S(1)}, u32[]{:S(2)}, u32[]{:S(2)}) collective-permute-start(f32[128]{0:T(128)S(1)} %reshape.338), channel_id=1, source_target_pairs={{0,12},{4,8},{8,4},{12,0},{1,13},{5,9},{9,5},{13,1},{2,14},{6,10},... | collective-permute-start | bytes 1544 | tf_op jit(solution)/shard_map/ppermute | solution.py:34
  115.9 0.7 copy-start.14
  119.6 12.0 %copy-start.15 = (bf16[64,2048]{1,0:T(8,128)(2,1)S(1)}, bf16[64,2048]{1,0:T(8,128)(2,1)}, u32[]{:S(2)}) copy-start(bf16[64,2048]{1,0:T(8,128)(2,1)} %copy-done.14) | copy-start | bytes 786436
  119.6 18.1 %collective-permute-start.28 = (f16[32,1024]{1,0:T(8,128)(2,1)S(1)}, f16[32,1024]{1,0:T(8,128)(2,1)S(1)}, u32[]{:S(2)}, u32[]{:S(2)}) collective-permute-start(f16[32,1024]{1,0:T(8,128)(2,1)S(1)} %get-tuple-element.15), channel_id=1, source_target_pairs={{0,4},{4,0},{8,12},{12,8},{1,5},{5,1},{9,13},{13,9},{2,6},{6,2},{1... | collective-permute-start | bytes 196616 | tf_op jit(solution)/shard_map/ppermute | solution.py:34
  120.2 17.5 %collective-permute-start.29 = (f16[32,1024]{1,0:T(8,128)(2,1)S(1)}, f16[32,1024]{1,0:T(8,128)(2,1)S(1)}, u32[]{:S(2)}, u32[]{:S(2)}) collective-permute-start(f16[32,1024]{1,0:T(8,128)(2,1)S(1)} %get-tuple-element.17), channel_id=1, source_target_pairs={{0,8},{4,12},{8,0},{12,4},{1,9},{5,13},{9,1},{13,5},{2,10},{6,14},... | collective-permute-start | bytes 196616 | tf_op jit(solution)/shard_map/ppermute | solution.py:34
  124.1 14.3 %collective-permute-start.30 = (f16[32,1024]{1,0:T(8,128)(2,1)S(1)}, f16[32,1024]{1,0:T(8,128)(2,1)S(1)}, u32[]{:S(2)}, u32[]{:S(2)}) collective-permute-start(f16[32,1024]{1,0:T(8,128)(2,1)S(1)} %get-tuple-element.16), channel_id=1, source_target_pairs={{0,12},{4,8},{8,4},{12,0},{1,13},{5,9},{9,5},{13,1},{2,14},{6,10},... | collective-permute-start | bytes 196616 | tf_op jit(solution)/shard_map/ppermute | solution.py:34
  127.2 15.0 %collective-permute-start.31 = (f16[32,1024]{1,0:T(8,128)(2,1)S(1)}, f16[32,1024]{1,0:T(8,128)(2,1)S(1)}, u32[]{:S(2)}, u32[]{:S(2)}) collective-permute-start(f16[32,1024]{1,0:T(8,128)(2,1)S(1)} %get-tuple-element.18), channel_id=1, source_target_pairs={{0,4},{4,0},{8,12},{12,8},{1,5},{5,1},{9,13},{13,9},{2,6},{6,2},{1... | collective-permute-start | bytes 196616 | tf_op jit(solution)/shard_map/ppermute | solution.py:34
  127.8 14.6 %collective-permute-start.32 = (f16[32,1024]{1,0:T(8,128)(2,1)S(1)}, f16[32,1024]{1,0:T(8,128)(2,1)S(1)}, u32[]{:S(2)}, u32[]{:S(2)}) collective-permute-start(f16[32,1024]{1,0:T(8,128)(2,1)S(1)} %get-tuple-element.20), channel_id=1, source_target_pairs={{0,8},{4,12},{8,0},{12,4},{1,9},{5,13},{9,1},{13,5},{2,10},{6,14},... | collective-permute-start | bytes 196616 | tf_op jit(solution)/shard_map/ppermute | solution.py:34
  137.7 6.8 %collective-permute-start.33 = (f16[32,1024]{1,0:T(8,128)(2,1)S(1)}, f16[32,1024]{1,0:T(8,128)(2,1)S(1)}, u32[]{:S(2)}, u32[]{:S(2)}) collective-permute-start(f16[32,1024]{1,0:T(8,128)(2,1)S(1)} %get-tuple-element.19), channel_id=1, source_target_pairs={{0,12},{4,8},{8,4},{12,0},{1,13},{5,9},{9,5},{13,1},{2,14},{6,10},... | collective-permute-start | bytes 196616 | tf_op jit(solution)/shard_map/ppermute | solution.py:34
  137.8 8.9 %collective-permute-start.34 = (f16[32,1024]{1,0:T(8,128)(2,1)S(1)}, f16[32,1024]{1,0:T(8,128)(2,1)S(1)}, u32[]{:S(2)}, u32[]{:S(2)}) collective-permute-start(f16[32,1024]{1,0:T(8,128)(2,1)S(1)} %get-tuple-element.21), channel_id=1, source_target_pairs={{0,4},{4,0},{8,12},{12,8},{1,5},{5,1},{9,13},{13,9},{2,6},{6,2},{1... | collective-permute-start | bytes 196616 | tf_op jit(solution)/shard_map/ppermute | solution.py:34
  138.3 9.0 %collective-permute-start.35 = (f16[32,1024]{1,0:T(8,128)(2,1)S(1)}, f16[32,1024]{1,0:T(8,128)(2,1)S(1)}, u32[]{:S(2)}, u32[]{:S(2)}) collective-permute-start(f16[32,1024]{1,0:T(8,128)(2,1)S(1)} %get-tuple-element.23), channel_id=1, source_target_pairs={{0,8},{4,12},{8,0},{12,4},{1,9},{5,13},{9,1},{13,5},{2,10},{6,14},... | collective-permute-start | bytes 196616 | tf_op jit(solution)/shard_map/ppermute | solution.py:34
  142.2 6.4 %collective-permute-start.36 = (f16[32,1024]{1,0:T(8,128)(2,1)S(1)}, f16[32,1024]{1,0:T(8,128)(2,1)S(1)}, u32[]{:S(2)}, u32[]{:S(2)}) collective-permute-start(f16[32,1024]{1,0:T(8,128)(2,1)S(1)} %get-tuple-element.22), channel_id=1, source_target_pairs={{0,12},{4,8},{8,4},{12,0},{1,13},{5,9},{9,5},{13,1},{2,14},{6,10},... | collective-permute-start | bytes 196616 | tf_op jit(solution)/shard_map/ppermute | solution.py:34
  142.3 6.3 %collective-permute-start.37 = (f16[32,1024]{1,0:T(8,128)(2,1)S(1)}, f16[32,1024]{1,0:T(8,128)(2,1)S(1)}, u32[]{:S(2)}, u32[]{:S(2)}) collective-permute-start(f16[32,1024]{1,0:T(8,128)(2,1)S(1)} %get-tuple-element.24), channel_id=1, source_target_pairs={{0,4},{4,0},{8,12},{12,8},{1,5},{5,1},{9,13},{13,9},{2,6},{6,2},{1... | collective-permute-start | bytes 196616 | tf_op jit(solution)/shard_map/ppermute | solution.py:34
  144.5 6.8 %collective-permute-start.38 = (f16[32,1024]{1,0:T(8,128)(2,1)S(1)}, f16[32,1024]{1,0:T(8,128)(2,1)S(1)}, u32[]{:S(2)}, u32[]{:S(2)}) collective-permute-start(f16[32,1024]{1,0:T(8,128)(2,1)S(1)} %get-tuple-element.26), channel_id=1, source_target_pairs={{0,8},{4,12},{8,0},{12,4},{1,9},{5,13},{9,1},{13,5},{2,10},{6,14},... | collective-permute-start | bytes 196616 | tf_op jit(solution)/shard_map/ppermute | solution.py:34
  146.7 6.1 %collective-permute-start.39 = (f16[32,1024]{1,0:T(8,128)(2,1)S(1)}, f16[32,1024]{1,0:T(8,128)(2,1)S(1)}, u32[]{:S(2)}, u32[]{:S(2)}) collective-permute-start(f16[32,1024]{1,0:T(8,128)(2,1)S(1)} %get-tuple-element.25), channel_id=1, source_target_pairs={{0,12},{4,8},{8,4},{12,0},{1,13},{5,9},{9,5},{13,1},{2,14},{6,10},... | collective-permute-start | bytes 196616 | tf_op jit(solution)/shard_map/ppermute | solution.py:34

commit v2 on v1

--- a/solution.py
+++ b/solution.py
@@ -1,6 +1,10 @@
+import functools
+
 import jax
 import jax.numpy as jnp
 from jax import lax
+from jax.experimental import pallas as pl
+from jax.experimental.pallas import tpu as pltpu
 from jax.sharding import PartitionSpec as P
 
 CB = 8
@@ -10,7 +14,7 @@
 ROPE_BASE = 500000.0
 NORM_EPS = 1e-05
 ADAPTER_SCALE = 0.5
-LOGIT_PARTS = 4
+LOGIT_PARTS = 2
 
 
 def rotate(values, positions):
@@ -36,6 +40,42 @@
 
 def take_block(array, index, size, axis=0):
     return lax.dynamic_slice_in_dim(array, index * size, size, axis)
+
+
+def lowering_kernel(voices, rank, own_ref, in1_ref, in2_ref, in3_ref, question_ref, content_ref, down_ref, onehot_ref):
+    width = question_ref.shape[1]
+    rows = jnp.concatenate([own_ref[...], in1_ref[...], in2_ref[...], in3_ref[...]], axis=0)
+    onehot = rows[:, width:]
+    onehot_ref[...] = onehot
+    onehot = onehot.astype(jnp.float32)
+    left = lax.broadcasted_iota(jnp.int32, (rows.shape[0], 2 * rank), 1) < rank
+    sums = []
+    for weight_ref in (question_ref, content_ref):
+        every = lax.dot_general(
+            rows[:, :width],
+            weight_ref[...],
+            (((1,), (1,)), ((), ())),
+            preferred_element_type=jnp.float32,
+        )
+        kept = 0.0
+        for pair in range(voices // 2):
+            mask = jnp.where(left, onehot[:, 2 * pair : 2 * pair + 1], onehot[:, 2 * pair + 1 : 2 * pair + 2])
+            kept = kept + mask * every[:, 2 * pair * rank : 2 * (pair + 1) * rank]
+        sums.append(kept[:, :rank] + kept[:, rank:])
+    down_ref[...] = jnp.concatenate(sums, axis=1)
+
+
+def lower(pieces, question, content, voices, rank):
+    rows = sum(piece.shape[0] for piece in pieces)
+    return pl.pallas_call(
+        functools.partial(lowering_kernel, voices, rank),
+        out_shape=(
+            jax.ShapeDtypeStruct((rows, 2 * rank), jnp.float32),
+            jax.ShapeDtypeStruct((rows, 128), jnp.bfloat16),
+        ),
+        cost_estimate=pl.CostEstimate(flops=1000, bytes_accessed=1000, transcendentals=0),
+        compiler_params=pltpu.CompilerParams(vmem_limit_bytes=16 << 20),
+    )(*pieces, question, content)
 
 
 def per_device_four(
@@ -107,21 +147,19 @@
         ],
         axis=1,
     )
+
+    base, rows_in = lax.optimization_barrier((base, rows_in))
     projected = base[:str_dev]
     for k in peers:
         projected = projected + swap(base[k * str_dev : (k + 1) * str_dev], "adapter", k)
-
-    rows = jnp.concatenate(rows_in, axis=0)
-    onehot_b = rows[:, d_slice : d_slice + voices]
-    onehot_f = onehot_b.astype(jnp.float32)
-    flat_rows = rows[:, :d_slice]
-    downs = []
-    for lowering in (speaker_question_lowering, speaker_content_lowering):
-        every = jnp.dot(
-            flat_rows, lowering.reshape(d_slice, voices * rank), preferred_element_type=jnp.float32
-        )
-        downs.append(jnp.sum(onehot_f[:, :, None] * every.reshape(-1, voices, rank), axis=1))
-    down = jnp.concatenate(downs, axis=1)
+    down, onehot = lower(
+        rows_in,
+        speaker_question_lowering.transpose(1, 2, 0).reshape(voices * rank, d_slice),
+        speaker_content_lowering.transpose(1, 2, 0).reshape(voices * rank, d_slice),
+        voices,
+        rank,
+    )
+    onehot_b = onehot[:, :voices]
     down = down + swap(down, "tensor", 1)
     down = (down + swap(down, "tensor", 2)).astype(jnp.bfloat16)
     ups = []

time: 155 us -> 130 us (0.84)
  local copies, waits for them, and re-layouts: 18 us -> 3.46 us
  starting transfers between devices: 57.8 us -> 46.8 us
  waiting for transfers between devices: 36.4 us -> 46 us
  other arithmetic: 14 us -> 6.91 us
  matrix products: 24.3 us -> 20.7 us
    ppermute x39 -> x33, starting transfers between devices: 56.2 us -> 46 us  [swap(): return lax.ppermute(value, axis, [(i, i ^ distance) for i in range(size)])]
    ppermute x39 -> x33, waiting for transfers between devices: 36.4 us -> 46 us  [swap(): return lax.ppermute(value, axis, [(i, i ^ distance) for i in range(size)])]
    ppermute x3 -> x0, local copies, waits for them, and re-layouts: 5.09 us -> none  [swap(): return lax.ppermute(value, axis, [(i, i ^ distance) for i in range(size)])]
    slice x3 -> x1, local copies, waits for them, and re-layouts: 4.63 us -> 0.02 us  [per_device_four(): sent_rows[k * slot_cap:(k + 1) * slot_cap]]
    dot_general x4 -> x2, matrix products: 11.9 us -> 9.4 us  [per_device_four(): jnp.dot(final_normed, codebook_weight[:, p * width:(p + 1) * width], pref...]
    dot_general x3, matrix products: 3.52 us -> 5.8 us  [per_device_four(): jnp.dot(norm_cols, weight, preferred_element_type=jnp.float32)]
    dot_general x2 -> x0, matrix products: 2.03 us -> none  [per_device_four(): jnp.dot(flat_rows, lowering.reshape(d_slice, voices * rank), preferred_el...]
    unnamed x38 -> x22, local copies, waits for them, and re-layouts: 2.1 us -> 0.1 us
  transfers between devices with their start and end apart: 40 -> 34, of which waited for: 16 -> 16; matrix products, arithmetic and copies ran while one was open for 24% -> 12% of each run, Pallas kernels for 0% -> 0%
where the time goes in v2:
time: 130 us; the launch traced here: 129 us
  starting transfers between devices  46.8 us (36%)
  waiting for transfers between devices  46 us (35%)
  matrix products  20.7 us (16%)
  other arithmetic  6.91 us (5%)
  between operations  3.77 us (3%)
  local copies, waits for them, and re-layouts  3.46 us (3%)
  Pallas kernels  1.52 us (1%)
    ppermute x33, starting transfers between devices, swap(): return lax.ppermute(value, axis, [(i, i ^ distance) for i in range(size)])  46 us
    ppermute x33, waiting for transfers between devices, swap(): return lax.ppermute(value, axis, [(i, i ^ distance) for i in range(size)])  46 us
    dot_general x2, matrix products, per_device_four(): jnp.dot(final_normed, codebook_weight[:, p * width:(p + 1) * width], pref...  9.4 us
    dot_general x3, matrix products, per_device_four(): jnp.dot(norm_cols, weight, preferred_element_type=jnp.float32)  5.8 us
    dot_general x1, matrix products, per_device_four(): jnp.dot(gathered, output_weight, preferred_element_type=jnp.float32)  2.9 us
  transfers between devices with their start and end apart: 34, of which 16 were waited for; matrix products, arithmetic and copies ran while one was open for 12% of the time, Pallas kernels for 0%

profile of v2, /device:TPU:0, one launch (start us, length us, event | category | flops | bytes accessed | tf_op | source)
XLA Modules:
  0.0 129.1 jit_solution(2816169119122407197)
XLA Ops:
  0.7 1.3 %fusion.9 = f32[32]{0:T(128)S(1)} fusion(bf16[32,8192]{1,0:T(8,128)(2,1)} %param.18), kind=kLoop, calls=%fused_computation.16 | loop fusion | flops 786400 | bytes 524416 | tf_op jit(solution)/shard_map/reduce_sum | solution.py:113
  2.0 1.2 fusion.11
  3.4 3.1 %collective-permute-start.1 = (bf16[16,2048]{1,0:T(8,128)(2,1)S(1)}, bf16[16,2048]{1,0:T(8,128)(2,1)S(1)}, u32[]{:S(2)}, u32[]{:S(2)}) collective-permute-start(bf16[16,2048]{1,0:T(8,128)(2,1)S(1)} %get-tuple-element.31), channel_id=1, source_target_pairs={{0,4},{4,0},{8,12},{12,8},{1,5},{5,1},{9,13},{13,9},{2,6},{6,2},{1... | collective-permute-start | bytes 196616 | tf_op jit(solution)/shard_map/ppermute | solution.py:38
  6.5 2.6 %collective-permute-start.2 = (bf16[16,2048]{1,0:T(8,128)(2,1)S(1)}, bf16[16,2048]{1,0:T(8,128)(2,1)S(1)}, u32[]{:S(2)}, u32[]{:S(2)}) collective-permute-start(bf16[16,2048]{1,0:T(8,128)(2,1)S(1)} %get-tuple-element.33), channel_id=1, source_target_pairs={{0,8},{4,12},{8,0},{12,4},{1,9},{5,13},{9,1},{13,5},{2,10},{6,14},... | collective-permute-start | bytes 196616 | tf_op jit(solution)/shard_map/ppermute | solution.py:38
  9.1 0.7 and_select_fusion.1
  9.8 0.2 convert_reduce_fusion
  10.1 0.2 convolution_convert_fusion
  10.3 3.5 %collective-permute-done.2 = bf16[16,2048]{1,0:T(8,128)(2,1)S(1)} collective-permute-done((bf16[16,2048]{1,0:T(8,128)(2,1)S(1)}, bf16[16,2048]{1,0:T(8,128)(2,1)S(1)}, u32[]{:S(2)}, u32[]{:S(2)}) %collective-permute-start.2) | collective-permute-done | bytes 65568 | tf_op jit(solution)/shard_map/ppermute | solution.py:38
  13.8 1.4 %collective-permute-done.3 = bf16[16,2048]{1,0:T(8,128)(2,1)S(1)} collective-permute-done((bf16[16,2048]{1,0:T(8,128)(2,1)S(1)}, bf16[16,2048]{1,0:T(8,128)(2,1)S(1)}, u32[]{:S(2)}, u32[]{:S(2)}) %collective-permute-start.3) | collective-permute-done | bytes 65568 | tf_op jit(solution)/shard_map/ppermute | solution.py:38
  15.4 2.3 %collective-permute-start.6 = (bf16[16,2176]{1,0:T(8,128)(2,1)S(1)}, bf16[16,2176]{1,0:T(8,128)(2,1)S(1)}, u32[]{:S(2)}, u32[]{:S(2)}) collective-permute-start(bf16[16,2176]{1,0:T(8,128)(2,1)S(1)} %get-tuple-element.37), channel_id=1, source_target_pairs={{0,8},{4,12},{8,0},{12,4},{1,9},{5,13},{9,1},{13,5},{2,10},{6,14},... | collective-permute-start | bytes 208904 | tf_op jit(solution)/shard_map/ppermute | solution.py:38
  17.7 2.0 %collective-permute-start.7 = (bf16[16,2176]{1,0:T(8,128)(2,1)S(1)}, bf16[16,2176]{1,0:T(8,128)(2,1)S(1)}, u32[]{:S(2)}, u32[]{:S(2)}) collective-permute-start(bf16[16,2176]{1,0:T(8,128)(2,1)S(1)} %get-tuple-element.36), channel_id=1, source_target_pairs={{0,12},{4,8},{8,4},{12,0},{1,13},{5,9},{9,5},{13,1},{2,14},{6,10},... | collective-permute-start | bytes 208904 | tf_op jit(solution)/shard_map/ppermute | solution.py:38
  19.8 0.7 convert_element_type.129
  20.5 3.1 %fusion.27 = f32[128,1024]{1,0:T(8,128)S(1)} fusion(bf16[2048,1024]{1,0:T(8,128)(2,1)} %param.20, bf16[96,2048]{1,0:T(8,128)(2,1)S(1)} %bitcast.69, bf16[32,2048]{1,0:T(8,128)(2,1)S(1)} %get-tuple-element.30), kind=kOutput, calls=%fused_computation.60 | convolution fusion | flops 537919488 | bytes 5242880 | tf_op jit(solution)/shard_map/dot_general | solution.py:145
  23.7 1.4 %fusion.26 = f32[128,128]{1,0:T(8,128)S(1)} fusion(bf16[2048,128]{1,0:T(8,128)(2,1)} %param.21, bf16[96,2048]{1,0:T(8,128)(2,1)S(1)} %bitcast.70, bf16[32,2048]{1,0:T(8,128)(2,1)S(1)} %get-tuple-element.30), kind=kOutput, calls=%fused_computation.59 | convolution fusion | flops 68157440 | bytes 1114112 | tf_op jit(solution)/shard_map/dot_general | solution.py:145
  25.0 1.3 %fusion.25 = f32[128,128]{1,0:T(8,128)S(1)} fusion(bf16[2048,128]{1,0:T(8,128)(2,1)} %param.22, bf16[96,2048]{1,0:T(8,128)(2,1)S(1)} %bitcast.71, bf16[32,2048]{1,0:T(8,128)(2,1)S(1)} %get-tuple-element.30), kind=kOutput, calls=%fused_computation.58 | convolution fusion | flops 68157440 | bytes 1114112 | tf_op jit(solution)/shard_map/dot_general | solution.py:145
  26.5 1.5 %shard_map.185 = (f32[64,128]{1,0:T(8,128)S(1)}, bf16[64,128]{1,0:T(8,128)(2,1)S(1)}) custom-call(bf16[16,2176]{1,0:T(8,128)(2,1)S(1)} %get-tuple-element.10.own_ref, bf16[16,2176]{1,0:T(8,128)(2,1)S(1)} %collective-permute-done.5.in1_ref, bf16[16,2176]{1,0:T(8,128)(2,1)S(1)} %collective-permute-done.6.in2_ref, ...), custom_call_target="tpu_custom_call" | custom-call | flops 1000 | bytes 1000 | tf_op jit(solution)/shard_map/pallas_call | solution.py:70
  28.3 1.1 collective-permute-done.11
  29.3 1.5 %collective-permute-start.12 = (f32[64,128]{1,0:T(8,128)S(1)}, f32[64,128]{1,0:T(8,128)S(1)}, u32[]{:S(2)}, u32[]{:S(2)}) collective-permute-start(f32[64,128]{1,0:T(8,128)S(1)} %add.192), channel_id=1, source_target_pairs={{0,2},{1,3},{2,0},{3,1},{4,6},{5,7},{6,4},{7,5},{8,10},{9,11},{10,... | collective-permute-start | bytes 98312 | tf_op jit(solution)/shard_map/ppermute | solution.py:38
  31.0 2.3 %collective-permute-done.12 = f32[64,128]{1,0:T(8,128)S(1)} collective-permute-done((f32[64,128]{1,0:T(8,128)S(1)}, f32[64,128]{1,0:T(8,128)S(1)}, u32[]{:S(2)}, u32[]{:S(2)}) %collective-permute-start.12) | collective-permute-done | bytes 32800 | tf_op jit(solution)/shard_map/ppermute | solution.py:38
  33.3 0.3 fusion.8
  33.6 0.4 fusion.5
  34.1 2.3 %collective-permute-start.14 = (bf16[16,1152]{1,0:T(8,128)(2,1)S(1)}, bf16[16,1152]{1,0:T(8,128)(2,1)S(1)}, u32[]{:S(2)}, u32[]{:S(2)}) collective-permute-start(bf16[16,1152]{1,0:T(8,128)(2,1)S(1)} %get-tuple-element.47), channel_id=1, source_target_pairs={{0,8},{4,12},{8,0},{12,4},{1,9},{5,13},{9,1},{13,5},{2,10},{6,14},... | collective-permute-start | bytes 110600 | tf_op jit(solution)/shard_map/ppermute | solution.py:38
  36.5 2.0 %collective-permute-start.15 = (bf16[16,1152]{1,0:T(8,128)(2,1)S(1)}, bf16[16,1152]{1,0:T(8,128)(2,1)S(1)}, u32[]{:S(2)}, u32[]{:S(2)}) collective-permute-start(bf16[16,1152]{1,0:T(8,128)(2,1)S(1)} %get-tuple-element.46), channel_id=1, source_target_pairs={{0,12},{4,8},{8,4},{12,0},{1,13},{5,9},{9,5},{13,1},{2,14},{6,10},... | collective-permute-start | bytes 110600 | tf_op jit(solution)/shard_map/ppermute | solution.py:38
  38.6 1.8 %collective-permute-start.10 = (f32[32,1280]{1,0:T(8,128)S(1)}, f32[32,1280]{1,0:T(8,128)S(1)}, u32[]{:S(2)}, u32[]{:S(2)}) collective-permute-start(f32[32,1280]{1,0:T(8,128)S(1)} %get-tuple-element.27), channel_id=1, source_target_pairs={{0,12},{4,8},{8,4},{12,0},{1,13},{5,9},{9,5},{13,1},{2,14},{6,10},... | collective-permute-start | bytes 491528 | tf_op jit(solution)/shard_map/ppermute | solution.py:38
  40.4 2.6 %collective-permute-start.9 = (f32[32,1280]{1,0:T(8,128)S(1)}, f32[32,1280]{1,0:T(8,128)S(1)}, u32[]{:S(2)}, u32[]{:S(2)}) collective-permute-start(f32[32,1280]{1,0:T(8,128)S(1)} %get-tuple-element.28), channel_id=1, source_target_pairs={{0,8},{4,12},{8,0},{12,4},{1,9},{5,13},{9,1},{13,5},{2,10},{6,14},... | collective-permute-start | bytes 491528 | tf_op jit(solution)/shard_map/ppermute | solution.py:38
  43.0 0.2 fusion.28
  43.2 4.4 %collective-permute-done.10 = f32[32,1280]{1,0:T(8,128)S(1)} collective-permute-done((f32[32,1280]{1,0:T(8,128)S(1)}, f32[32,1280]{1,0:T(8,128)S(1)}, u32[]{:S(2)}, u32[]{:S(2)}) %collective-permute-start.10) | collective-permute-done | bytes 163872 | tf_op jit(solution)/shard_map/ppermute | solution.py:38
  47.7 1.2 collective-permute-done.8
  48.9 5.6 %collective-permute-done.9 = f32[32,1280]{1,0:T(8,128)S(1)} collective-permute-done((f32[32,1280]{1,0:T(8,128)S(1)}, f32[32,1280]{1,0:T(8,128)S(1)}, u32[]{:S(2)}, u32[]{:S(2)}) %collective-permute-start.9) | collective-permute-done | bytes 163872 | tf_op jit(solution)/shard_map/ppermute | solution.py:38
  54.9 0.2 fusion.67
  55.1 0.8 select_reduce_fusion
  55.9 0.2 fusion.42
  56.2 0.4 fusion.6
  56.7 2.3 %collective-permute-start.17 = (bf16[32,1024]{1,0:T(8,128)(2,1)S(1)}, bf16[32,1024]{1,0:T(8,128)(2,1)S(1)}, u32[]{:S(2)}, u32[]{:S(2)}) collective-permute-start(bf16[32,1024]{1,0:T(8,128)(2,1)S(1)} %bitcast.74), channel_id=1, source_target_pairs={{0,8},{4,12},{8,0},{12,4},{1,9},{5,13},{9,1},{13,5},{2,10},{6,14},... | collective-permute-start | bytes 196616 | tf_op jit(solution)/shard_map/ppermute | solution.py:38
  59.0 2.0 %collective-permute-start.18 = (bf16[32,1024]{1,0:T(8,128)(2,1)S(1)}, bf16[32,1024]{1,0:T(8,128)(2,1)S(1)}, u32[]{:S(2)}, u32[]{:S(2)}) collective-permute-start(bf16[32,1024]{1,0:T(8,128)(2,1)S(1)} %bitcast.75), channel_id=1, source_target_pairs={{0,12},{4,8},{8,4},{12,0},{1,13},{5,9},{9,5},{13,1},{2,14},{6,10},... | collective-permute-start | bytes 196616 | tf_op jit(solution)/shard_map/ppermute | solution.py:38
  61.1 2.5 %collective-permute-done.17 = bf16[32,1024]{1,0:T(8,128)(2,1)S(1)} collective-permute-done((bf16[32,1024]{1,0:T(8,128)(2,1)S(1)}, bf16[32,1024]{1,0:T(8,128)(2,1)S(1)}, u32[]{:S(2)}, u32[]{:S(2)}) %collective-permute-start.17) | collective-permute-done | bytes 65568 | tf_op jit(solution)/shard_map/ppermute | solution.py:38
  63.6 1.5 %collective-permute-done.18 = bf16[32,1024]{1,0:T(8,128)(2,1)S(1)} collective-permute-done((bf16[32,1024]{1,0:T(8,128)(2,1)S(1)}, bf16[32,1024]{1,0:T(8,128)(2,1)S(1)}, u32[]{:S(2)}, u32[]{:S(2)}) %collective-permute-start.18) | collective-permute-done | bytes 65568 | tf_op jit(solution)/shard_map/ppermute | solution.py:38
  65.1 2.9 %fusion.17 = f32[128,2048]{1,0:T(8,128)S(1)} fusion(bf16[1024,2048]{1,0:T(8,128)(2,1)} %param.31, bf16[32,1024]{1,0:T(8,128)(2,1)S(1)} %collective-permute-done.18, bf16[32,1024]{1,0:T(8,128)(2,1)S(1)} %collective-permute-done.17, bf16[32,1024]{1,0:T(8,128)(2,1)S(1)} %collective-permute-done.16, bf16[32,1024]{1,0:T(8,128)(2,1)S(1)} %bitcast.76), kind=kOutput, calls=%fused_computation.32 | convolution fusion | flops 537919488 | bytes 5505024 | tf_op jit(solution)/shard_map/dot_general | solution.py:233
  68.2 1.9 %collective-permute-done.19 = f32[64,2048]{1,0:T(8,128)S(1)} collective-permute-done((f32[64,2048]{1,0:T(8,128)S(1)}, f32[64,2048]{1,0:T(8,128)S(1)}, u32[]{:S(2)}, u32[]{:S(2)}) %collective-permute-start.19) | collective-permute-done | bytes 524320 | tf_op jit(solution)/shard_map/ppermute | solution.py:38
  70.1 1.6 %collective-permute-start.20 = (f32[32,2048]{1,0:T(8,128)S(1)}, f32[32,2048]{1,0:T(8,128)S(1)}, u32[]{:S(2)}, u32[]{:S(2)}) collective-permute-start(f32[32,2048]{1,0:T(8,128)S(1)} %slice_add_fusion), channel_id=1, source_target_pairs={{0,2},{1,3},{2,0},{3,1},{4,6},{5,7},{6,4},{7,5},{8,10},{9,11},{10,... | collective-permute-start | bytes 786440 | tf_op jit(solution)/shard_map/ppermute | solution.py:38
  71.7 0.9 constant_dynamic-slice_fusion.4
  72.6 0.8 collective-permute-start
  73.6 5.0 %collective-permute-done.20 = f32[32,2048]{1,0:T(8,128)S(1)} collective-permute-done((f32[32,2048]{1,0:T(8,128)S(1)}, f32[32,2048]{1,0:T(8,128)S(1)}, u32[]{:S(2)}, u32[]{:S(2)}) %collective-permute-start.20) | collective-permute-done | bytes 262176 | tf_op jit(solution)/shard_map/ppermute | solution.py:38
  78.5 0.2 multiply_reduce_fusion
  78.7 5.3 %collective-permute-start.21 = (bf16[32,2048]{1,0:T(8,128)(2,1)S(1)}, bf16[32,2048]{1,0:T(8,128)(2,1)S(1)}, u32[]{:S(2)}, u32[]{:S(2)}) collective-permute-start(bf16[32,2048]{1,0:T(8,128)(2,1)S(1)} %get-tuple-element.17), channel_id=1, source_target_pairs={{0,2},{1,3},{2,0},{3,1},{4,6},{5,7},{6,4},{7,5},{8,10},{9,11},{10,... | collective-permute-start | bytes 393224 | tf_op jit(solution)/shard_map/ppermute | solution.py:38
  84.1 0.6 fusion.90
  87.3 3.5 %collective-permute-done.23 = f32[32]{0:T(128)S(1)} collective-permute-done((f32[32]{0:T(128)S(1)}, f32[32]{0:T(128)S(1)}, u32[]{:S(2)}, u32[]{:S(2)}) %collective-permute-start.23) | collective-permute-done | bytes 160 | tf_op jit(solution)/shard_map/ppermute | solution.py:38
  91.0 0.5 collective-permute-start.22
  91.5 0.5 collective-permute-done.24
  92.2 0.7 collective-permute-start.26
  92.9 3.7 %collective-permute-start.27 = (f32[128]{0:T(128)S(1)}, f32[128]{0:T(128)S(1)}, u32[]{:S(2)}, u32[]{:S(2)}) collective-permute-start(f32[128]{0:T(128)S(1)} %reshape.333), channel_id=1, source_target_pairs={{0,12},{4,8},{8,4},{12,0},{1,13},{5,9},{9,5},{13,1},{2,14},{6,10},... | collective-permute-start | bytes 1544 | tf_op jit(solution)/shard_map/ppermute | solution.py:38
  96.6 0.7 dynamic_slice.87
  97.3 0.9 collective-permute-done.27
  98.2 4.7 %fusion.2 = f32[128,2048]{1,0:T(8,128)S(1)} fusion(bf16[2048,4096]{1,0:T(8,128)(2,1)} %param.33, bf16[64,2048]{1,0:T(8,128)(2,1)S(1)} %collective-permute-done.22, bf16[32,2048]{1,0:T(8,128)(2,1)S(1)} %collective-permute-done.21, bf16[32,2048]{1,0:T(8,128)(2,1)S(1)} %get-tuple-element.17, f32[2048]{0:T(1024)S(1)} %dynamic_slice.87, f32[128]{0:T(128)S(1)} %add_rsqrt_fusion), kind=kOutput, calls=%fused_computation.2 | convolution fusion | flops 1076101120 | bytes 9970176 | tf_op jit(solution)/shard_map/dot_general | solution.py:270
  103.0 0.5 collective-permute-start.28
  103.5 3.8 %collective-permute-start.29 = (f16[32,2048]{1,0:T(8,128)(2,1)S(1)}, f16[32,2048]{1,0:T(8,128)(2,1)S(1)}, u32[]{:S(2)}, u32[]{:S(2)}) collective-permute-start(f16[32,2048]{1,0:T(8,128)(2,1)S(1)} %get-tuple-element.20), channel_id=1, source_target_pairs={{0,8},{4,12},{8,0},{12,4},{1,9},{5,13},{9,1},{13,5},{2,10},{6,14},... | collective-permute-start | bytes 393224 | tf_op jit(solution)/shard_map/ppermute | solution.py:38
  107.5 4.7 %fusion = f32[128,2048]{1,0:T(8,128)S(1)} fusion(bf16[2048,4096]{1,0:T(8,128)(2,1)} %param.33, bf16[64,2048]{1,0:T(8,128)(2,1)S(1)} %collective-permute-done.22, bf16[32,2048]{1,0:T(8,128)(2,1)S(1)} %collective-permute-done.21, bf16[32,2048]{1,0:T(8,128)(2,1)S(1)} %get-tuple-element.17, f32[2048]{0:T(1024)S(1)} %dynamic_slice.87, f32[128]{0:T(128)S(1)} %add_rsqrt_fusion), kind=kOutput, calls=%fused_computation | convolution fusion | flops 1076101120 | bytes 9970176 | tf_op jit(solution)/shard_map/dot_general | solution.py:270
  112.3 0.5 collective-permute-start.31
  112.8 3.8 %collective-permute-start.32 = (f16[32,2048]{1,0:T(8,128)(2,1)S(1)}, f16[32,2048]{1,0:T(8,128)(2,1)S(1)}, u32[]{:S(2)}, u32[]{:S(2)}) collective-permute-start(f16[32,2048]{1,0:T(8,128)(2,1)S(1)} %get-tuple-element.23), channel_id=1, source_target_pairs={{0,8},{4,12},{8,0},{12,4},{1,9},{5,13},{9,1},{13,5},{2,10},{6,14},... | collective-permute-start | bytes 393224 | tf_op jit(solution)/shard_map/ppermute | solution.py:38
  116.6 0.2 collective-permute-start.33
  116.7 1.0 collective-permute-done.29
  117.9 9.6 %collective-permute-done.32 = f16[32,2048]{1,0:T(8,128)(2,1)S(1)} collective-permute-done((f16[32,2048]{1,0:T(8,128)(2,1)S(1)}, f16[32,2048]{1,0:T(8,128)(2,1)S(1)}, u32[]{:S(2)}, u32[]{:S(2)}) %collective-permute-start.32) | collective-permute-done | bytes 131104 | tf_op jit(solution)/shard_map/ppermute | solution.py:38
  127.6 0.4 reshape.334
  128.1 1.0 broadcast_multiply_fusion
  (95 shorter events, 3.0 us)
Async XLA Ops:
  0.6 33.0 %copy-start = (bf16[8,64,1024]{2,1,0:T(8,128)(2,1)S(1)}, bf16[8,64,1024]{2,1,0:T(8,128)(2,1)}, u32[]{:S(2)}) copy-start(bf16[8,64,1024]{2,1,0:T(8,128)(2,1)} %param.24) | copy-start | bytes 3145732
  3.4 6.9 %collective-permute-start.1 = (bf16[16,2048]{1,0:T(8,128)(2,1)S(1)}, bf16[16,2048]{1,0:T(8,128)(2,1)S(1)}, u32[]{:S(2)}, u32[]{:S(2)}) collective-permute-start(bf16[16,2048]{1,0:T(8,128)(2,1)S(1)} %get-tuple-element.31), channel_id=1, source_target_pairs={{0,4},{4,0},{8,12},{12,8},{1,5},{5,1},{9,13},{13,9},{2,6},{6,2},{1... | collective-permute-start | bytes 196616 | tf_op jit(solution)/shard_map/ppermute | solution.py:38
  6.5 7.3 %collective-permute-start.2 = (bf16[16,2048]{1,0:T(8,128)(2,1)S(1)}, bf16[16,2048]{1,0:T(8,128)(2,1)S(1)}, u32[]{:S(2)}, u32[]{:S(2)}) collective-permute-start(bf16[16,2048]{1,0:T(8,128)(2,1)S(1)} %get-tuple-element.33), channel_id=1, source_target_pairs={{0,8},{4,12},{8,0},{12,4},{1,9},{5,13},{9,1},{13,5},{2,10},{6,14},... | collective-permute-start | bytes 196616 | tf_op jit(solution)/shard_map/ppermute | solution.py:38
  9.1 6.1 %collective-permute-start.3 = (bf16[16,2048]{1,0:T(8,128)(2,1)S(1)}, bf16[16,2048]{1,0:T(8,128)(2,1)S(1)}, u32[]{:S(2)}, u32[]{:S(2)}) collective-permute-start(bf16[16,2048]{1,0:T(8,128)(2,1)S(1)} %get-tuple-element.32), channel_id=1, source_target_pairs={{0,12},{4,8},{8,4},{12,0},{1,13},{5,9},{9,5},{13,1},{2,14},{6,10},... | collective-permute-start | bytes 196616 | tf_op jit(solution)/shard_map/ppermute | solution.py:38
  15.2 5.2 %collective-permute-start.4 = (bf16[3,16,2048]{2,1,0:T(8,128)(2,1)S(1)}, bf16[3,16,2048]{2,1,0:T(8,128)(2,1)S(1)}, u32[]{:S(2)}, u32[]{:S(2)}) collective-permute-start(bf16[3,16,2048]{2,1,0:T(8,128)(2,1)S(1)} %pad_maximum_fusion.6), channel_id=1, source_target_pairs={{0,1},{1,0},{2,3},{3,2},{4,5},{5,4},{6,7},{7,6},{8,9},{9,8},{10,11... | collective-permute-start | bytes 589832 | tf_op jit(solution)/shard_map/ppermute | solution.py:38
  15.3 11.1 %collective-permute-start.5 = (bf16[16,2176]{1,0:T(8,128)(2,1)S(1)}, bf16[16,2176]{1,0:T(8,128)(2,1)S(1)}, u32[]{:S(2)}, u32[]{:S(2)}) collective-permute-start(bf16[16,2176]{1,0:T(8,128)(2,1)S(1)} %get-tuple-element.38), channel_id=1, source_target_pairs={{0,4},{4,0},{8,12},{12,8},{1,5},{5,1},{9,13},{13,9},{2,6},{6,2},{1... | collective-permute-start | bytes 208904 | tf_op jit(solution)/shard_map/ppermute | solution.py:38
  15.4 11.1 %collective-permute-start.6 = (bf16[16,2176]{1,0:T(8,128)(2,1)S(1)}, bf16[16,2176]{1,0:T(8,128)(2,1)S(1)}, u32[]{:S(2)}, u32[]{:S(2)}) collective-permute-start(bf16[16,2176]{1,0:T(8,128)(2,1)S(1)} %get-tuple-element.37), channel_id=1, source_target_pairs={{0,8},{4,12},{8,0},{12,4},{1,9},{5,13},{9,1},{13,5},{2,10},{6,14},... | collective-permute-start | bytes 208904 | tf_op jit(solution)/shard_map/ppermute | solution.py:38
  17.7 8.7 %collective-permute-start.7 = (bf16[16,2176]{1,0:T(8,128)(2,1)S(1)}, bf16[16,2176]{1,0:T(8,128)(2,1)S(1)}, u32[]{:S(2)}, u32[]{:S(2)}) collective-permute-start(bf16[16,2176]{1,0:T(8,128)(2,1)S(1)} %get-tuple-element.36), channel_id=1, source_target_pairs={{0,12},{4,8},{8,4},{12,0},{1,13},{5,9},{9,5},{13,1},{2,14},{6,10},... | collective-permute-start | bytes 208904 | tf_op jit(solution)/shard_map/ppermute | solution.py:38
  20.5 6.0 %copy-start.1 = (bf16[2048,8,64]{0,2,1:T(8,128)(2,1)S(1)}, bf16[2048,8,64]{0,2,1:T(8,128)(2,1)}, u32[]{:S(2)}) copy-start(bf16[2048,8,64]{0,2,1:T(8,128)(2,1)} %param.23) | copy-start | bytes 6291460
  20.5 6.0 %copy-start.2 = (bf16[2048,8,64]{0,2,1:T(8,128)(2,1)S(1)}, bf16[2048,8,64]{0,2,1:T(8,128)(2,1)}, u32[]{:S(2)}) copy-start(bf16[2048,8,64]{0,2,1:T(8,128)(2,1)} %param.25) | copy-start | bytes 6291460
  23.6 7.2 %copy-start.6 = (s32[32]{0:T(128)S(1)}, s32[32]{0:T(128)}, u32[]{:S(2)}) copy-start(s32[32]{0:T(128)} %param.30) | copy-start | bytes 388
  23.7 9.7 %copy-start.8 = (bf16[8,64,128]{2,1,0:T(8,128)(2,1)S(1)}, bf16[8,64,128]{2,1,0:T(8,128)(2,1)}, u32[]{:S(2)}) copy-start(bf16[8,64,128]{2,1,0:T(8,128)(2,1)} %param.26) | copy-start | bytes 393220
  26.5 28.6 %copy-start.3 = (bf16[32,1,128,128]{3,2,1,0:T(8,128)(2,1)S(1)}, bf16[32,1,128,128]{3,2,1,0:T(8,128)(2,1)}, u32[]{:S(2)}) copy-start(bf16[32,1,128,128]{3,2,1,0:T(8,128)(2,1)} %param.27) | copy-start | bytes 3145732
  28.0 1.3 collective-permute-start.11
  29.3 3.9 %collective-permute-start.12 = (f32[64,128]{1,0:T(8,128)S(1)}, f32[64,128]{1,0:T(8,128)S(1)}, u32[]{:S(2)}, u32[]{:S(2)}) collective-permute-start(f32[64,128]{1,0:T(8,128)S(1)} %add.192), channel_id=1, source_target_pairs={{0,2},{1,3},{2,0},{3,1},{4,6},{5,7},{6,4},{7,5},{8,10},{9,11},{10,... | collective-permute-start | bytes 98312 | tf_op jit(solution)/shard_map/ppermute | solution.py:38
  30.9 25.2 %copy-start.7 = (bf16[32,1,128,128]{3,2,1,0:T(8,128)(2,1)S(1)}, bf16[32,1,128,128]{3,2,1,0:T(8,128)(2,1)}, u32[]{:S(2)}) copy-start(bf16[32,1,128,128]{3,2,1,0:T(8,128)(2,1)} %param.28) | copy-start | bytes 3145732
  34.1 6.3 %collective-permute-start.13 = (bf16[16,1152]{1,0:T(8,128)(2,1)S(1)}, bf16[16,1152]{1,0:T(8,128)(2,1)S(1)}, u32[]{:S(2)}, u32[]{:S(2)}) collective-permute-start(bf16[16,1152]{1,0:T(8,128)(2,1)S(1)} %get-tuple-element.45), channel_id=1, source_target_pairs={{0,4},{4,0},{8,12},{12,8},{1,5},{5,1},{9,13},{13,9},{2,6},{6,2},{1... | collective-permute-start | bytes 110600 | tf_op jit(solution)/shard_map/ppermute | solution.py:38
  34.1 8.9 %collective-permute-start.14 = (bf16[16,1152]{1,0:T(8,128)(2,1)S(1)}, bf16[16,1152]{1,0:T(8,128)(2,1)S(1)}, u32[]{:S(2)}, u32[]{:S(2)}) collective-permute-start(bf16[16,1152]{1,0:T(8,128)(2,1)S(1)} %get-tuple-element.47), channel_id=1, source_target_pairs={{0,8},{4,12},{8,0},{12,4},{1,9},{5,13},{9,1},{13,5},{2,10},{6,14},... | collective-permute-start | bytes 110600 | tf_op jit(solution)/shard_map/ppermute | solution.py:38
  36.5 6.5 %collective-permute-start.15 = (bf16[16,1152]{1,0:T(8,128)(2,1)S(1)}, bf16[16,1152]{1,0:T(8,128)(2,1)S(1)}, u32[]{:S(2)}, u32[]{:S(2)}) collective-permute-start(bf16[16,1152]{1,0:T(8,128)(2,1)S(1)} %get-tuple-element.46), channel_id=1, source_target_pairs={{0,12},{4,8},{8,4},{12,0},{1,13},{5,9},{9,5},{13,1},{2,14},{6,10},... | collective-permute-start | bytes 110600 | tf_op jit(solution)/shard_map/ppermute | solution.py:38
  38.6 9.1 %collective-permute-start.10 = (f32[32,1280]{1,0:T(8,128)S(1)}, f32[32,1280]{1,0:T(8,128)S(1)}, u32[]{:S(2)}, u32[]{:S(2)}) collective-permute-start(f32[32,1280]{1,0:T(8,128)S(1)} %get-tuple-element.27), channel_id=1, source_target_pairs={{0,12},{4,8},{8,4},{12,0},{1,13},{5,9},{9,5},{13,1},{2,14},{6,10},... | collective-permute-start | bytes 491528 | tf_op jit(solution)/shard_map/ppermute | solution.py:38
  40.4 8.5 %collective-permute-start.8 = (f32[32,1280]{1,0:T(8,128)S(1)}, f32[32,1280]{1,0:T(8,128)S(1)}, u32[]{:S(2)}, u32[]{:S(2)}) collective-permute-start(f32[32,1280]{1,0:T(8,128)S(1)} %get-tuple-element.26), channel_id=1, source_target_pairs={{0,4},{4,0},{8,12},{12,8},{1,5},{5,1},{9,13},{13,9},{2,6},{6,2},{1... | collective-permute-start | bytes 491528 | tf_op jit(solution)/shard_map/ppermute | solution.py:38
  40.4 14.1 %collective-permute-start.9 = (f32[32,1280]{1,0:T(8,128)S(1)}, f32[32,1280]{1,0:T(8,128)S(1)}, u32[]{:S(2)}, u32[]{:S(2)}) collective-permute-start(f32[32,1280]{1,0:T(8,128)S(1)} %get-tuple-element.28), channel_id=1, source_target_pairs={{0,8},{4,12},{8,0},{12,4},{1,9},{5,13},{9,1},{13,5},{2,10},{6,14},... | collective-permute-start | bytes 491528 | tf_op jit(solution)/shard_map/ppermute | solution.py:38
  56.6 4.5 %collective-permute-start.16 = (bf16[32,1024]{1,0:T(8,128)(2,1)S(1)}, bf16[32,1024]{1,0:T(8,128)(2,1)S(1)}, u32[]{:S(2)}, u32[]{:S(2)}) collective-permute-start(bf16[32,1024]{1,0:T(8,128)(2,1)S(1)} %bitcast.73), channel_id=1, source_target_pairs={{0,4},{4,0},{8,12},{12,8},{1,5},{5,1},{9,13},{13,9},{2,6},{6,2},{1... | collective-permute-start | bytes 196616 | tf_op jit(solution)/shard_map/ppermute | solution.py:38
  56.7 6.9 %collective-permute-start.17 = (bf16[32,1024]{1,0:T(8,128)(2,1)S(1)}, bf16[32,1024]{1,0:T(8,128)(2,1)S(1)}, u32[]{:S(2)}, u32[]{:S(2)}) collective-permute-start(bf16[32,1024]{1,0:T(8,128)(2,1)S(1)} %bitcast.74), channel_id=1, source_target_pairs={{0,8},{4,12},{8,0},{12,4},{1,9},{5,13},{9,1},{13,5},{2,10},{6,14},... | collective-permute-start | bytes 196616 | tf_op jit(solution)/shard_map/ppermute | solution.py:38
  59.0 6.1 %collective-permute-start.18 = (bf16[32,1024]{1,0:T(8,128)(2,1)S(1)}, bf16[32,1024]{1,0:T(8,128)(2,1)S(1)}, u32[]{:S(2)}, u32[]{:S(2)}) collective-permute-start(bf16[32,1024]{1,0:T(8,128)(2,1)S(1)} %bitcast.75), channel_id=1, source_target_pairs={{0,12},{4,8},{8,4},{12,0},{1,13},{5,9},{9,5},{13,1},{2,14},{6,10},... | collective-permute-start | bytes 196616 | tf_op jit(solution)/shard_map/ppermute | solution.py:38
  61.1 12.4 %copy-start.9 = (s32[8]{0:T(128)S(1)}, s32[8]{0:T(128)}, u32[]{:S(2)}) copy-start(s32[8]{0:T(128)} %param.34) | copy-start | bytes 100
  61.1 23.0 %copy-start.5 = (s32[4]{0:T(128)S(1)}, s32[4]{0:T(128)}, u32[]{:S(2)}) copy-start(s32[4]{0:T(128)} %constant.128.clone) | copy-start | bytes 52
  68.1 2.0 %collective-permute-start.19 = (f32[64,2048]{1,0:T(8,128)S(1)}, f32[64,2048]{1,0:T(8,128)S(1)}, u32[]{:S(2)}, u32[]{:S(2)}) collective-permute-start(f32[64,2048]{1,0:T(8,128)S(1)} %pad_maximum_fusion.2), channel_id=1, source_target_pairs={{0,1},{1,0},{2,3},{3,2},{4,5},{5,4},{6,7},{7,6},{8,9},{9,8},{10,11... | collective-permute-start | bytes 1572872 | tf_op jit(solution)/shard_map/ppermute | solution.py:38
  70.1 8.4 %collective-permute-start.20 = (f32[32,2048]{1,0:T(8,128)S(1)}, f32[32,2048]{1,0:T(8,128)S(1)}, u32[]{:S(2)}, u32[]{:S(2)}) collective-permute-start(f32[32,2048]{1,0:T(8,128)S(1)} %slice_add_fusion), channel_id=1, source_target_pairs={{0,2},{1,3},{2,0},{3,1},{4,6},{5,7},{6,4},{7,5},{8,10},{9,11},{10,... | collective-permute-start | bytes 786440 | tf_op jit(solution)/shard_map/ppermute | solution.py:38
  72.6 1.0 collective-permute-start
  78.7 28.8 %copy-start.4 = (bf16[32,2048]{1,0:T(8,128)(2,1)}, bf16[32,2048]{1,0:T(8,128)(2,1)S(1)}, u32[]{:S(2)}) copy-start(bf16[32,2048]{1,0:T(8,128)(2,1)S(1)} %get-tuple-element.17) | copy-start | bytes 393220
  78.7 12.2 %collective-permute-start.21 = (bf16[32,2048]{1,0:T(8,128)(2,1)S(1)}, bf16[32,2048]{1,0:T(8,128)(2,1)S(1)}, u32[]{:S(2)}, u32[]{:S(2)}) collective-permute-start(bf16[32,2048]{1,0:T(8,128)(2,1)S(1)} %get-tuple-element.17), channel_id=1, source_target_pairs={{0,2},{1,3},{2,0},{3,1},{4,6},{5,7},{6,4},{7,5},{8,10},{9,11},{10,... | collective-permute-start | bytes 393224 | tf_op jit(solution)/shard_map/ppermute | solution.py:38
  87.3 3.6 %collective-permute-start.23 = (f32[32]{0:T(128)S(1)}, f32[32]{0:T(128)S(1)}, u32[]{:S(2)}, u32[]{:S(2)}) collective-permute-start(f32[32]{0:T(128)S(1)} %get-tuple-element.16), channel_id=1, source_target_pairs={{0,2},{1,3},{2,0},{3,1},{4,6},{5,7},{6,4},{7,5},{8,10},{9,11},{10,... | collective-permute-start | bytes 392 | tf_op jit(solution)/shard_map/ppermute | solution.py:38
  90.9 1.2 collective-permute-start.24
  91.0 7.3 %collective-permute-start.22 = (bf16[64,2048]{1,0:T(8,128)(2,1)S(1)}, bf16[64,2048]{1,0:T(8,128)(2,1)S(1)}, u32[]{:S(2)}, u32[]{:S(2)}) collective-permute-start(bf16[64,2048]{1,0:T(8,128)(2,1)S(1)} %pad_maximum_fusion.5), channel_id=1, source_target_pairs={{0,1},{1,0},{2,3},{3,2},{4,5},{5,4},{6,7},{7,6},{8,9},{9,8},{10,11... | collective-permute-start | bytes 786440 | tf_op jit(solution)/shard_map/ppermute | solution.py:38
  92.2 5.2 %collective-permute-start.25 = (f32[128]{0:T(128)S(1)}, f32[128]{0:T(128)S(1)}, u32[]{:S(2)}, u32[]{:S(2)}) collective-permute-start(f32[128]{0:T(128)S(1)} %reshape.333), channel_id=1, source_target_pairs={{0,4},{4,0},{8,12},{12,8},{1,5},{5,1},{9,13},{13,9},{2,6},{6,2},{1... | collective-permute-start | bytes 1544 | tf_op jit(solution)/shard_map/ppermute | solution.py:38
  92.2 5.2 %collective-permute-start.26 = (f32[128]{0:T(128)S(1)}, f32[128]{0:T(128)S(1)}, u32[]{:S(2)}, u32[]{:S(2)}) collective-permute-start(f32[128]{0:T(128)S(1)} %reshape.333), channel_id=1, source_target_pairs={{0,8},{4,12},{8,0},{12,4},{1,9},{5,13},{9,1},{13,5},{2,10},{6,14},... | collective-permute-start | bytes 1544 | tf_op jit(solution)/shard_map/ppermute | solution.py:38
  92.9 5.3 %collective-permute-start.27 = (f32[128]{0:T(128)S(1)}, f32[128]{0:T(128)S(1)}, u32[]{:S(2)}, u32[]{:S(2)}) collective-permute-start(f32[128]{0:T(128)S(1)} %reshape.333), channel_id=1, source_target_pairs={{0,12},{4,8},{8,4},{12,0},{1,13},{5,9},{9,5},{13,1},{2,14},{6,10},... | collective-permute-start | bytes 1544 | tf_op jit(solution)/shard_map/ppermute | solution.py:38
  103.0 13.5 %collective-permute-start.28 = (f16[32,2048]{1,0:T(8,128)(2,1)S(1)}, f16[32,2048]{1,0:T(8,128)(2,1)S(1)}, u32[]{:S(2)}, u32[]{:S(2)}) collective-permute-start(f16[32,2048]{1,0:T(8,128)(2,1)S(1)} %get-tuple-element.18), channel_id=1, source_target_pairs={{0,4},{4,0},{8,12},{12,8},{1,5},{5,1},{9,13},{13,9},{2,6},{6,2},{1... | collective-permute-start | bytes 393224 | tf_op jit(solution)/shard_map/ppermute | solution.py:38
  103.5 14.3 %collective-permute-start.29 = (f16[32,2048]{1,0:T(8,128)(2,1)S(1)}, f16[32,2048]{1,0:T(8,128)(2,1)S(1)}, u32[]{:S(2)}, u32[]{:S(2)}) collective-permute-start(f16[32,2048]{1,0:T(8,128)(2,1)S(1)} %get-tuple-element.20), channel_id=1, source_target_pairs={{0,8},{4,12},{8,0},{12,4},{1,9},{5,13},{9,1},{13,5},{2,10},{6,14},... | collective-permute-start | bytes 393224 | tf_op jit(solution)/shard_map/ppermute | solution.py:38
  107.3 10.5 %collective-permute-start.30 = (f16[32,2048]{1,0:T(8,128)(2,1)S(1)}, f16[32,2048]{1,0:T(8,128)(2,1)S(1)}, u32[]{:S(2)}, u32[]{:S(2)}) collective-permute-start(f16[32,2048]{1,0:T(8,128)(2,1)S(1)} %get-tuple-element.19), channel_id=1, source_target_pairs={{0,12},{4,8},{8,4},{12,0},{1,13},{5,9},{9,5},{13,1},{2,14},{6,10},... | collective-permute-start | bytes 393224 | tf_op jit(solution)/shard_map/ppermute | solution.py:38
  112.3 5.6 %collective-permute-start.31 = (f16[32,2048]{1,0:T(8,128)(2,1)S(1)}, f16[32,2048]{1,0:T(8,128)(2,1)S(1)}, u32[]{:S(2)}, u32[]{:S(2)}) collective-permute-start(f16[32,2048]{1,0:T(8,128)(2,1)S(1)} %get-tuple-element.21), channel_id=1, source_target_pairs={{0,4},{4,0},{8,12},{12,8},{1,5},{5,1},{9,13},{13,9},{2,6},{6,2},{1... | collective-permute-start | bytes 393224 | tf_op jit(solution)/shard_map/ppermute | solution.py:38
  112.8 14.7 %collective-permute-start.32 = (f16[32,2048]{1,0:T(8,128)(2,1)S(1)}, f16[32,2048]{1,0:T(8,128)(2,1)S(1)}, u32[]{:S(2)}, u32[]{:S(2)}) collective-permute-start(f16[32,2048]{1,0:T(8,128)(2,1)S(1)} %get-tuple-element.23), channel_id=1, source_target_pairs={{0,8},{4,12},{8,0},{12,4},{1,9},{5,13},{9,1},{13,5},{2,10},{6,14},... | collective-permute-start | bytes 393224 | tf_op jit(solution)/shard_map/ppermute | solution.py:38
  116.6 10.9 %collective-permute-start.33 = (f16[32,2048]{1,0:T(8,128)(2,1)S(1)}, f16[32,2048]{1,0:T(8,128)(2,1)S(1)}, u32[]{:S(2)}, u32[]{:S(2)}) collective-permute-start(f16[32,2048]{1,0:T(8,128)(2,1)S(1)} %get-tuple-element.22), channel_id=1, source_target_pairs={{0,12},{4,8},{8,4},{12,0},{1,13},{5,9},{9,5},{13,1},{2,14},{6,10},... | collective-permute-start | bytes 393224 | tf_op jit(solution)/shard_map/ppermute | solution.py:38

commit v3 on v2

--- a/solution.py
+++ b/solution.py
@@ -15,6 +15,7 @@
 NORM_EPS = 1e-05
 ADAPTER_SCALE = 0.5
 LOGIT_PARTS = 2
+KERNEL_VMEM = 8 << 20
 
 
 def rotate(values, positions):
@@ -42,9 +43,121 @@
     return lax.dynamic_slice_in_dim(array, index * size, size, axis)
 
 
-def lowering_kernel(voices, rank, own_ref, in1_ref, in2_ref, in3_ref, question_ref, content_ref, down_ref, onehot_ref):
+def full_spec():
+    return pl.BlockSpec(memory_space=pltpu.VMEM)
+
+
+def call(kernel, outs, operands, scalars=(), scratch=(), resident=(), hbm=()):
+    hbm = [pltpu.with_memory_space_constraint(array, pltpu.HBM) for array in hbm]
+    resident = [pltpu.with_memory_space_constraint(array, pltpu.VMEM) for array in resident]
+    specs = [pl.BlockSpec(memory_space=pl.ANY)] * len(hbm)
+    specs += [full_spec()] * (len(operands) + len(resident))
+    arrays = [*hbm, *operands, *resident]
+    specs = [pl.BlockSpec(memory_space=pltpu.SMEM)] * len(scalars) + specs
+    arrays = [*scalars, *arrays]
+    return pl.pallas_call(
+        kernel,
+        out_shape=tuple(outs),
+        in_specs=specs,
+        out_specs=tuple(full_spec() for _ in outs),
+        scratch_shapes=scratch,
+        cost_estimate=pl.CostEstimate(flops=1000, bytes_accessed=1000, transcendentals=0),
+        compiler_params=pltpu.CompilerParams(vmem_limit_bytes=KERNEL_VMEM),
+    )(*arrays)
+
+
+def shaped(shape, dtype):
+    return jax.ShapeDtypeStruct(shape, dtype)
+
+
+def norm_kernel(
+    n_adapter, voices, books, place_ref, delays_ref, tokens_hbm, gain_hbm, label_hbm, lengths_hbm, closing_hbm,
+    own_ref, rows_ref, out1_ref, out2_ref, out3_ref, placing_ref, raw_ref, active_ref, closing_ref,
+    normed_ref, tokens_ref, gain_ref, label_ref, lengths_ref, sems,
+):
+    a, t = place_ref[0], place_ref[1]
+    streams, model_width = tokens_ref.shape
+    d_slice = own_ref.shape[1]
+    closing_part = closing_hbm.at[:, pl.ds(pl.multiple_of(a * d_slice, d_slice), d_slice)]
+    copies = [
+        pltpu.make_async_copy(source, target, sems.at[i])
+        for i, (source, target) in enumerate(
+            (
+                (tokens_hbm, tokens_ref),
+                (gain_hbm, gain_ref),
+                (label_hbm, label_ref),
+                (lengths_hbm, lengths_ref),
+                (closing_part, closing_ref),
+            )
+        )
+    ]
+    for copy in copies:
+        copy.start()
+    for copy in copies:
+        copy.wait()
+    half = streams // 2
+    cap = rows_ref.shape[0]
+    tok = tokens_ref[...].astype(jnp.float32)
+    mean = jnp.sum(tok * tok, axis=-1, keepdims=True) * (1.0 / model_width)
+    normed_ref[...] = (tok * lax.rsqrt(mean + NORM_EPS) * gain_ref[...]).astype(jnp.bfloat16)
+
+    def owner_of(label):
+        return sum((label >= j * voices).astype(jnp.int32) for j in range(1, n_adapter))
+
+    square = (streams, streams)
+    row_index = lax.broadcasted_iota(jnp.int32, square, 0)
+    col_index = lax.broadcasted_iota(jnp.int32, square, 1)
+
+    def column(row):
+        picked = jnp.where(row_index == col_index, row.astype(jnp.float32), 0.0)
+        return jnp.sum(picked, axis=1, keepdims=True).astype(jnp.int32)
+
+    label_row = label_ref[...]
+    label_col = column(label_row)
+    owner_row, owner_col = owner_of(label_row), owner_of(label_col)
+    voice = label_col - owner_col * voices
+    earlier = (owner_col == owner_row) & (row_index < col_index)
+    rank = jnp.sum(earlier.astype(jnp.float32), axis=0, keepdims=True).astype(jnp.int32)
+    slot = jnp.bitwise_xor(owner_row, a) * cap + rank
+    slots = (n_adapter * cap, streams)
+    placing = (lax.broadcasted_iota(jnp.int32, slots, 0) == slot).astype(jnp.float32).astype(jnp.bfloat16)
+    placing_ref[...] = placing
+    lanes = (streams, 128)
+    onehot = (lax.broadcasted_iota(jnp.int32, lanes, 1) == voice).astype(jnp.float32).astype(jnp.bfloat16)
+    mine = normed_ref[:, pl.ds(pl.multiple_of(t * d_slice, d_slice), d_slice)]
+    rows = jnp.dot(placing, mine, preferred_element_type=jnp.float32).astype(jnp.bfloat16)
+    kinds = jnp.dot(placing, onehot, preferred_element_type=jnp.float32).astype(jnp.bfloat16)
+    own_ref[...] = normed_ref[:, pl.ds(pl.multiple_of(a * d_slice, d_slice), d_slice)]
+    rows_ref[:, :d_slice] = rows[:cap]
+    rows_ref[:, d_slice:] = kinds[:cap]
+    first = pl.multiple_of(lax.rem(t, 2) * half, half)
+    length_col = column(lengths_ref[...])
+    lane = lax.broadcasted_iota(jnp.int32, active_ref.shape, 1)
+    active = jnp.zeros(active_ref.shape, jnp.float32)
+    for p in range(books):
+        started = (length_col >= delays_ref[t * books + p]).astype(jnp.float32)
+        active = jnp.where(lane == p, started, active)
+    active_ref[...] = active
+    quarter = raw_ref.shape[2]
+    for k in range(n_adapter):
+        first_raw = pl.multiple_of(jnp.bitwise_xor(a, k) * d_slice + t * quarter, quarter)
+        raw_ref[k] = tokens_ref[:, pl.ds(first_raw, quarter)]
+    for k, out_ref in enumerate((out1_ref, out2_ref, out3_ref), 1):
+        start = pl.multiple_of(jnp.bitwise_xor(a, k) * d_slice, d_slice)
+        out_ref[:half, :d_slice] = normed_ref[pl.ds(first, half), pl.ds(start, d_slice)]
+        out_ref[:half, d_slice:] = jnp.zeros((half, 128), jnp.bfloat16)
+        out_ref[half:, :d_slice] = rows[k * cap : (k + 1) * cap]
+        out_ref[half:, d_slice:] = kinds[k * cap : (k + 1) * cap]
+
+
+def lowering_kernel(
+    voices, rank, own_ref, in1_ref, in2_ref, in3_ref, question_ref, content_ref, down_ref, onehot_ref
+):
     width = question_ref.shape[1]
-    rows = jnp.concatenate([own_ref[...], in1_ref[...], in2_ref[...], in3_ref[...]], axis=0)
+    cap = own_ref.shape[0]
+    rows = jnp.concatenate(
+        [own_ref[...], in1_ref[cap:, :], in2_ref[cap:, :], in3_ref[cap:, :]], axis=0
+    )
     onehot = rows[:, width:]
     onehot_ref[...] = onehot
     onehot = onehot.astype(jnp.float32)
@@ -65,17 +178,105 @@
     down_ref[...] = jnp.concatenate(sums, axis=1)
 
 
-def lower(pieces, question, content, voices, rank):
-    rows = sum(piece.shape[0] for piece in pieces)
-    return pl.pallas_call(
-        functools.partial(lowering_kernel, voices, rank),
-        out_shape=(
-            jax.ShapeDtypeStruct((rows, 2 * rank), jnp.float32),
-            jax.ShapeDtypeStruct((rows, 128), jnp.bfloat16),
-        ),
-        cost_estimate=pl.CostEstimate(flops=1000, bytes_accessed=1000, transcendentals=0),
-        compiler_params=pltpu.CompilerParams(vmem_limit_bytes=16 << 20),
-    )(*pieces, question, content)
+def raising_kernel(
+    voices, rank, near_ref, far_ref, onehot_ref, question_ref, content_ref,
+    own_ref, out1_ref, out2_ref, out3_ref,
+):
+    down = (near_ref[...] + far_ref[...]).astype(jnp.bfloat16).astype(jnp.float32)
+    onehot = onehot_ref[...].astype(jnp.float32)
+    left = lax.broadcasted_iota(jnp.int32, (down.shape[0], 2 * rank), 1) < rank
+    first = 0
+    for i, weight_ref in enumerate((question_ref, content_ref)):
+        part = down[:, i * rank : (i + 1) * rank]
+        twice = jnp.concatenate([part, part], axis=1)
+        spread = jnp.concatenate(
+            [
+                jnp.where(left, onehot[:, 2 * pair : 2 * pair + 1], onehot[:, 2 * pair + 1 : 2 * pair + 2])
+                * twice
+                for pair in range(voices // 2)
+            ],
+            axis=1,
+        ).astype(jnp.bfloat16)
+        up = jnp.dot(spread, weight_ref[...], preferred_element_type=jnp.float32) * ADAPTER_SCALE
+        up = up.astype(jnp.bfloat16)
+        last = first + weight_ref.shape[1]
+        cap = own_ref.shape[0]
+        for k, out_ref in enumerate((own_ref, out1_ref, out2_ref, out3_ref)):
+            out_ref[:, first:last] = up[k * cap : (k + 1) * cap]
+        first = last
+
+
+def base_kernel(
+    place_ref, own_ref, in1_ref, in2_ref, in3_ref, other_ref, query_ref, key_ref, value_ref,
+    keep_ref, send_ref, rows_ref,
+):
+    core = lax.rem(place_ref[1], 2)
+    streams, width = own_ref.shape
+    half = streams // 2
+    rows_ref[:streams, :] = own_ref[...]
+    for k, in_ref in enumerate((in1_ref, in2_ref, in3_ref), 1):
+        mine = pl.multiple_of(k * streams + core * half, half)
+        theirs = pl.multiple_of(k * streams + (1 - core) * half, half)
+        rows_ref[pl.ds(mine, half), :] = in_ref[:half, :width]
+        rows_ref[pl.ds(theirs, half), :] = other_ref[(k - 1) * half : k * half, :]
+    first = 0
+    for weight_ref in (query_ref, key_ref, value_ref):
+        last = first + weight_ref.shape[1]
+        out = jnp.dot(rows_ref[...], weight_ref[...], preferred_element_type=jnp.float32)
+        for k in range(4):
+            out_ref = send_ref if k % 2 else keep_ref
+            out_ref[k // 2 * streams : (k // 2 + 1) * streams, first:last] = out[
+                k * streams : (k + 1) * streams
+            ]
+        first = last
+
+
+def out_kernel(
+    place_ref, own_ref, in1_ref, in2_ref, in3_ref, weight_ref, keep_ref, send_ref, rows_ref
+):
+    turn = jnp.bitwise_xor(place_ref[0], place_ref[1])
+    streams = own_ref.shape[0]
+    for k, in_ref in enumerate((own_ref, in1_ref, in2_ref, in3_ref)):
+        first = pl.multiple_of(jnp.bitwise_xor(turn, k) * streams, streams)
+        rows_ref[pl.ds(first, streams), :] = in_ref[...]
+    depth = weight_ref.shape[0]
+    quarter = rows_ref.shape[1] - depth
+    column = pl.ds(pl.multiple_of(place_ref[1] * quarter, quarter), quarter)
+    out = jnp.dot(rows_ref[:, :depth], weight_ref[...], preferred_element_type=jnp.float32)
+    for m in range(4):
+        out_ref = send_ref if m % 2 else keep_ref
+        to, block = pl.ds(m // 2 * streams, streams), slice(m * streams, (m + 1) * streams)
+        out_ref[to, :] = out[block]
+        out_ref[to, column] += rows_ref[block, depth:].astype(jnp.float32)
+
+
+def head_kernel(
+    first, place_ref, own_ref, across_ref, pair_ref, scale_ref, gain_ref, weight_ref, out_ref, rows_ref
+):
+    turn = jnp.bitwise_xor(place_ref[0], place_ref[1])
+    streams = own_ref.shape[0]
+    diagonal = lax.broadcasted_iota(jnp.int32, (streams, streams), 0) == lax.broadcasted_iota(
+        jnp.int32, (streams, streams), 1
+    )
+    pieces = (
+        own_ref[...],
+        pair_ref[:streams, :],
+        across_ref[...],
+        pair_ref[streams:, :],
+    )
+    for m, piece in enumerate(pieces):
+        row = (0, 2, 1, 3)[m]
+        scale = jnp.sum(
+            jnp.where(diagonal, scale_ref[row : row + 1, :], 0.0), axis=1, keepdims=True
+        )
+        at = pl.multiple_of(jnp.bitwise_xor(turn, m) * streams, streams)
+        rows_ref[pl.ds(at, streams), :] = (
+            piece.astype(jnp.float32) * scale * gain_ref[...]
+        ).astype(jnp.bfloat16)
+    width = out_ref.shape[1]
+    out_ref[...] = jnp.dot(
+        rows_ref[...], weight_ref[:, first : first + width], preferred_element_type=jnp.float32
+    )
 
 
 def per_device_four(
@@ -101,86 +302,88 @@
     peers = range(1, n_adapter)
     a = lax.axis_index("adapter")
     t = lax.axis_index("tensor")
-    core = t % 2
     str_dev, model_width = tokens.shape
-    half = str_dev // 2
+    place_ids = jnp.stack([a, t]).astype(jnp.int32)
     d_slice = model_width // n_adapter
     voices, rank = speaker_question_raising.shape[:2]
     query_columns = query_weight.shape[1]
     key_value_columns = key_weight.shape[1]
 
-    tok_f = tokens.astype(jnp.float32)
-    inverse = lax.rsqrt(jnp.mean(tok_f * tok_f, axis=-1, keepdims=True) + NORM_EPS)
-    normed = (tok_f * inverse * attention_gain).astype(jnp.bfloat16)
-
-    my_half = take_block(normed, core, half)
-    came = [swap(take_block(my_half, a ^ k, d_slice, 1), "adapter", k) for k in peers]
-
+    bf16 = jnp.bfloat16
     slot_cap = max(2, 2 * str_dev // n_adapter)
-    owner_ids = sequence_speaker_label // voices
-    local_voice = sequence_speaker_label % voices
-    same_owner = owner_ids[:, None] == owner_ids[None, :]
-    earlier = jnp.arange(str_dev)[:, None] > jnp.arange(str_dev)[None, :]
-    owner_rank = jnp.sum((same_owner & earlier).astype(jnp.int32), axis=1)
-    slot_ids = (owner_ids ^ a) * slot_cap + owner_rank
-    placing = (slot_ids[None, :] == jnp.arange(n_adapter * slot_cap)[:, None]).astype(jnp.bfloat16)
-    voice_onehot = (local_voice[:, None] == jnp.arange(128)[None, :]).astype(jnp.bfloat16)
-    sent_rows = jnp.dot(
-        placing,
-        jnp.concatenate([take_block(normed, t, d_slice, 1), voice_onehot], axis=1),
-        preferred_element_type=jnp.float32,
-    ).astype(jnp.bfloat16)
-    rows_in = [sent_rows[:slot_cap]] + [
-        swap(sent_rows[k * slot_cap : (k + 1) * slot_cap], "adapter", k) for k in peers
-    ]
-
-    came = jnp.stack(came)
-    other = swap(came, "tensor", 1)
-    first = jnp.where(core == 0, came, other)
-    second = jnp.where(core == 0, other, came)
-    arrived = jnp.concatenate([first, second], axis=1).reshape(-1, d_slice)
-    norm_cols = jnp.concatenate([take_block(normed, a, d_slice, 1), arrived], axis=0)
-    base = jnp.concatenate(
+    half = str_dev // 2
+    n_tensor = lax.axis_size("tensor")
+    quarter = d_slice // n_tensor
+    books_local = CB // n_tensor
+    own_cols, own_rows, *outgoing, placing, raw, active, final_slice = call(
+        functools.partial(norm_kernel, n_adapter, voices, books_local),
+        [shaped((str_dev, d_slice), bf16), shaped((slot_cap, d_slice + 128), bf16)]
+        + [shaped((half + slot_cap, d_slice + 128), bf16)] * 3
+        + [
+            shaped((n_adapter * slot_cap, str_dev), bf16),
+            shaped((n_adapter, str_dev, quarter), bf16),
+            shaped((str_dev, 128), jnp.float32),
+            shaped((1, d_slice), jnp.float32),
+        ],
+        [],
+        [place_ids, delays],
         [
-            jnp.dot(norm_cols, weight, preferred_element_type=jnp.float32)
-            for weight in (query_weight, key_weight, value_weight)
+            pltpu.VMEM((str_dev, model_width), bf16),
+            pltpu.VMEM((str_dev, model_width), bf16),
+            pltpu.VMEM((1, model_width), jnp.float32),
+            pltpu.VMEM((1, str_dev), jnp.int32),
+            pltpu.VMEM((1, str_dev), jnp.int32),
+            pltpu.SemaphoreType.DMA((5,)),
         ],
-        axis=1,
-    )
-
-    base, rows_in = lax.optimization_barrier((base, rows_in))
-    projected = base[:str_dev]
-    for k in peers:
-        projected = projected + swap(base[k * str_dev : (k + 1) * str_dev], "adapter", k)
-    down, onehot = lower(
-        rows_in,
-        speaker_question_lowering.transpose(1, 2, 0).reshape(voices * rank, d_slice),
-        speaker_content_lowering.transpose(1, 2, 0).reshape(voices * rank, d_slice),
-        voices,
-        rank,
-    )
-    onehot_b = onehot[:, :voices]
+        hbm=[
+            tokens,
+            attention_gain[None],
+            sequence_speaker_label[None],
+            lengths[None],
+            closing_gain[None],
+        ],
+    )
+    came = [swap(payload, "adapter", k) for k, payload in zip(peers, outgoing)]
+    other = swap(jnp.concatenate([piece[:half, :d_slice] for piece in came]), "tensor", 1)
+
+    down, onehot = call(
+        functools.partial(lowering_kernel, voices, rank),
+        [shaped((n_adapter * slot_cap, 2 * rank), jnp.float32), shaped((n_adapter * slot_cap, 128), bf16)],
+        [own_rows, *came],
+        resident=[
+            speaker_question_lowering.transpose(1, 2, 0).reshape(voices * rank, d_slice),
+            speaker_content_lowering.transpose(1, 2, 0).reshape(voices * rank, d_slice),
+        ],
+    )
+    other, down = lax.optimization_barrier((other, down))
+    kept, sent = call(
+        base_kernel,
+        [shaped((2 * str_dev, query_columns + 2 * key_value_columns), jnp.float32)] * 2,
+        [own_cols, *came, other],
+        [place_ids],
+        [pltpu.VMEM((n_adapter * str_dev, d_slice), bf16)],
+        resident=[query_weight, key_weight, value_weight],
+    )
     down = down + swap(down, "tensor", 1)
-    down = (down + swap(down, "tensor", 2)).astype(jnp.bfloat16)
-    ups = []
-    for i, raising in enumerate((speaker_question_raising, speaker_content_raising)):
-        spread = (
-            onehot_b[:, :, None] * down[:, None, i * rank : (i + 1) * rank]
-        ).reshape(-1, voices * rank)
-        up = jnp.dot(
-            spread, raising.reshape(voices * rank, -1), preferred_element_type=jnp.float32
-        )
-        ups.append((up * ADAPTER_SCALE).astype(jnp.bfloat16))
-    outgoing = jnp.concatenate(ups, axis=1)
+    summed = kept + swap(sent, "adapter", 1)
+    raised = call(
+        functools.partial(raising_kernel, voices, rank),
+        [shaped((slot_cap, query_columns + key_value_columns), bf16)] * n_adapter,
+        [down, swap(down, "tensor", 2), onehot],
+        resident=[
+            speaker_question_raising.reshape(voices * rank, query_columns),
+            speaker_content_raising.reshape(voices * rank, key_value_columns),
+        ],
+    )
     returned = jnp.concatenate(
-        [outgoing[:slot_cap]]
-        + [swap(outgoing[k * slot_cap : (k + 1) * slot_cap], "adapter", k) for k in peers],
-        axis=0,
+        [raised[0]] + [swap(raised[k], "adapter", k) for k in peers], axis=0
     )
     adapter_summands = jnp.einsum(
         "ms,mc->sc", placing, returned, preferred_element_type=jnp.float32
     )
 
+    far = swap(summed[str_dev:], "adapter", 2)
+    projected = summed[:str_dev] + far
     kv_local, ctx_len, head_dim = rotated_key_cache.shape[1:]
     group_size = query_columns // (kv_local * head_dim)
     query = rotate(
@@ -222,64 +425,55 @@
     )
     attended = mixed.astype(jnp.bfloat16).reshape(str_dev, query_columns)
 
-    raw = lax.ppermute(
-        take_block(tokens, t, d_slice, 1),
-        ("adapter", "tensor"),
-        [(i * n_adapter + j, j * n_adapter + i) for i in range(n_adapter) for j in range(n_adapter)],
-    )
-    gathered = jnp.concatenate(
-        [attended] + [swap(attended, "adapter", k) for k in peers], axis=0
-    )
-    partial_out = jnp.dot(gathered, output_weight, preferred_element_type=jnp.float32)
-    turn = a ^ t
-    near = swap(
-        jnp.concatenate(
-            [take_block(partial_out, turn ^ 1, str_dev), take_block(partial_out, turn ^ 3, str_dev)]
-        ),
-        "tensor",
-        1,
-    )
-    far = take_block(partial_out, turn ^ 2, str_dev) + near[str_dev:]
-    summed_out = take_block(partial_out, turn, str_dev) + near[:str_dev] + swap(far, "tensor", 2)
-    hidden_out = (raw.astype(jnp.float32) + summed_out).astype(jnp.bfloat16)
+    def with_raw(k):
+        return jnp.concatenate([attended, raw[k]], axis=1)
+
+    kept, sent = call(
+        out_kernel,
+        [shaped((2 * str_dev, d_slice), jnp.float32)] * 2,
+        [with_raw(0)] + [swap(with_raw(k), "adapter", k) for k in peers],
+        [place_ids],
+        [pltpu.VMEM((n_adapter * str_dev, query_columns + quarter), bf16)],
+        resident=[output_weight],
+    )
+    pair = kept + swap(sent, "tensor", 1)
+    summed_out = pair[:str_dev] + swap(pair[str_dev:], "tensor", 2)
+    hidden_out = summed_out.astype(jnp.bfloat16)
 
     hidden_f = hidden_out.astype(jnp.float32)
     square = jnp.sum(hidden_f * hidden_f, axis=-1)
-    square_pair = jnp.stack([square, swap(square, "tensor", 2)])
-    squares = jnp.concatenate([square_pair, swap(square_pair, "tensor", 1)]).reshape(-1)
-    square_sum = squares
+    square_sum = square
     for k in peers:
-        square_sum = square_sum + swap(squares, "adapter", k)
-    hidden_pair = jnp.concatenate([hidden_out, swap(hidden_out, "tensor", 2)])
-    hidden_all = jnp.concatenate([hidden_pair, swap(hidden_pair, "tensor", 1)])
-    final_slice = take_block(closing_gain, a, d_slice)
-    final_normed = (
-        hidden_all.astype(jnp.float32)
-        * lax.rsqrt(square_sum / model_width + NORM_EPS)[:, None]
-        * final_slice
-    ).astype(jnp.bfloat16)
-
-    books_local = CB // lax.axis_size("tensor")
-    book_delays = take_block(delays, t, books_local)
-    active = (lengths[:, None] >= book_delays[None, :]).astype(jnp.float32)
-    place = jnp.array([0, 2, 1, 3], jnp.int32)
-    parts = LOGIT_PARTS
-    width = codebook_weight.shape[1] // parts
+        square_sum = square_sum + swap(square, "adapter", k)
+    scale = lax.rsqrt(square_sum / model_width + NORM_EPS)[None]
+    across = swap(hidden_out, "tensor", 2)
+    hidden_pair = swap(jnp.concatenate([hidden_out, across]), "tensor", 1)
+    scale = jnp.concatenate([scale, swap(scale, "tensor", 2)])
+    scale = jnp.concatenate([scale, swap(scale, "tensor", 1)])
+
+    width = codebook_weight.shape[1] // LOGIT_PARTS
     outs = []
-    for p in range(parts):
-        partial = jnp.dot(
-            final_normed,
-            codebook_weight[:, p * width : (p + 1) * width],
-            preferred_element_type=jnp.float32,
-        )
-        total_p = take_block(partial, place[turn], str_dev)
+    for p in range(LOGIT_PARTS):
+        partial = call(
+            functools.partial(head_kernel, p * width),
+            [shaped((n_adapter * str_dev, width), jnp.float32)],
+            [hidden_out, across, hidden_pair, scale, final_slice],
+            [place_ids],
+            [pltpu.VMEM((n_adapter * str_dev, d_slice), bf16)],
+            resident=[codebook_weight],
+        )[0]
+        total_p = partial[:str_dev]
         for k in peers:
-            block = take_block(partial, place[turn ^ k], str_dev)
+            block = partial[k * str_dev : (k + 1) * str_dev]
             total_p = total_p + swap(
                 (block * 32.0).astype(jnp.float16), "adapter", k
             ).astype(jnp.float32) * (1.0 / 32.0)
         outs.append(total_p)
-    logits = jnp.concatenate(outs, axis=1).reshape(str_dev, books_local, VOC) * active[:, :, None]
+    if width == VOC:
+        logits = jnp.stack([out * active[:, p : p + 1] for p, out in enumerate(outs)], axis=1)
+    else:
+        logits = jnp.concatenate(outs, axis=1).reshape(str_dev, books_local, VOC)
+        logits = logits * active[:, :books_local, None]
     return (hidden_out, logits)
 
 

time: 130 us -> 115 us (0.88)
  matrix products: 20.7 us -> 1.62 us
  Pallas kernels: 1.52 us -> 11.1 us
  waiting for transfers between devices: 46 us -> 55.3 us
  starting transfers between devices: 46.8 us -> 38.7 us
  other arithmetic: 6.91 us -> 1.66 us
  between operations: 3.77 us -> 1.03 us
  local copies, waits for them, and re-layouts: 3.46 us -> 5.51 us
    dot_general x9 -> x0, matrix products: 19 us -> none  [the longest x2 9.4 us: per_device_four(): jnp.dot(final_normed, codebook_weight[:, p * width:(p + 1) * width], pref...]
    pallas_call x1 -> x7, Pallas kernels: 1.52 us -> 11.1 us  [call(): pl.pallas_call(kernel, out_shape=tuple(outs), in_specs=specs, out_specs=t...]
    ppermute x33 -> x29, waiting for transfers between devices: 46 us -> 55.3 us  [swap(): return lax.ppermute(value, axis, [(i, i ^ distance) for i in range(size)])]
    ppermute x33 -> x29, starting transfers between devices: 46 us -> 38.7 us  [swap(): return lax.ppermute(value, axis, [(i, i ^ distance) for i in range(size)])]
    unnamed x22 -> x31, local copies, waits for them, and re-layouts: 0.1 us -> 5.28 us
    dynamic_slice x7 -> x0, local copies, waits for them, and re-layouts: 2.54 us -> none  [the longest x6 1.9 us: take_block(): return lax.dynamic_slice_in_dim(array, index * size, size, axis)]
    reduce_sum x2 -> x0, other arithmetic: 1.51 us -> none  [the longest x1 1.33 us: per_device_four(): jnp.mean(tok_f * tok_f, axis=-1, keepdims=True) + NORM_EPS]
    convert_element_type x4 -> x0, other arithmetic: 1.39 us -> none  [the longest x1 1.24 us: per_device_four(): normed = (tok_f * inverse * attention_gain).astype(jnp.bfloat16)]
  transfers between devices with their start and end apart: 34 -> 29, of which waited for: 16 -> 18; matrix products, arithmetic and copies ran while one was open for 12% -> 1% of each run, Pallas kernels for 0% -> 5%
where the time goes in v3:
time: 115 us
  waiting for transfers between devices  55.3 us (48%)
  starting transfers between devices  38.7 us (34%)
  Pallas kernels  11.1 us (10%)
  local copies, waits for them, and re-layouts  5.51 us (5%)
  other arithmetic  1.66 us (1%)
  matrix products  1.62 us (1%)
    ppermute x29, waiting for transfers between devices, swap(): return lax.ppermute(value, axis, [(i, i ^ distance) for i in range(size)])  55.3 us
    ppermute x29, starting transfers between devices, swap(): return lax.ppermute(value, axis, [(i, i ^ distance) for i in range(size)])  38.7 us
    pallas_call x7, Pallas kernels, call(): pl.pallas_call(kernel, out_shape=tuple(outs), in_specs=specs, out_specs=t...  11.1 us
    unnamed x31, local copies, waits for them, and re-layouts  5.28 us
  transfers between devices with their start and end apart: 29, of which 18 were waited for; matrix products, arithmetic and copies ran while one was open for 1% of the time, Pallas kernels for 5%

profile of v3, /device:TPU:0, one launch (start us, length us, event | category | flops | bytes accessed | tf_op | source)
XLA Modules:
  0.0 114.9 jit_solution(9870949669833967746)
XLA Ops:
  0.7 0.8 copy-done.11
  1.6 2.2 %shard_map.176 = (bf16[32,2048]{1,0:T(8,128)(2,1)S(1)}, bf16[16,2176]{1,0:T(8,128)(2,1)S(1)}, bf16[32,2176]{1,0:T(8,128)(2,1)S(1)}, bf16[32,2176]{1,0:T(8,128)(2...) custom-call(s32[2]{0:T(128)S(1)} %pad_add_fusion.place_ref, ...), custom_call_target="tpu_custom_call" | custom-call | flops 1000 | bytes 1000 | tf_op jit(solution)/shard_map/pallas_call | solution.py:58
  3.8 3.1 %collective-permute-start = (bf16[32,2176]{1,0:T(8,128)(2,1)S(1)}, bf16[32,2176]{1,0:T(8,128)(2,1)S(1)}, u32[]{:S(2)}, u32[]{:S(2)}) collective-permute-start(bf16[32,2176]{1,0:T(8,128)(2,1)S(1)} %get-tuple-element.24), channel_id=1, source_target_pairs={{0,4},{4,0},{8,12},{12,8},{1,5},{5,1},{9,13},{13,9},{2,6},{6,2},{1... | collective-permute-start | bytes 417800 | tf_op jit(solution)/shard_map/ppermute | solution.py:39
  6.9 2.6 %collective-permute-start.1 = (bf16[32,2176]{1,0:T(8,128)(2,1)S(1)}, bf16[32,2176]{1,0:T(8,128)(2,1)S(1)}, u32[]{:S(2)}, u32[]{:S(2)}) collective-permute-start(bf16[32,2176]{1,0:T(8,128)(2,1)S(1)} %get-tuple-element.25), channel_id=1, source_target_pairs={{0,8},{4,12},{8,0},{12,4},{1,9},{5,13},{9,1},{13,5},{2,10},{6,14},... | collective-permute-start | bytes 417800 | tf_op jit(solution)/shard_map/ppermute | solution.py:39
  9.5 2.8 %collective-permute-done.in1_ref = bf16[32,2176]{1,0:T(8,128)(2,1)S(1)} collective-permute-done((bf16[32,2176]{1,0:T(8,128)(2,1)S(1)}, bf16[32,2176]{1,0:T(8,128)(2,1)S(1)}, u32[]{:S(2)}, u32[]{:S(2)}) %collective-permute-start) | collective-permute-done | bytes 139296 | tf_op jit(solution)/shard_map/ppermute | solution.py:39
  12.3 8.0 %collective-permute-done.1.in2_ref = bf16[32,2176]{1,0:T(8,128)(2,1)S(1)} collective-permute-done((bf16[32,2176]{1,0:T(8,128)(2,1)S(1)}, bf16[32,2176]{1,0:T(8,128)(2,1)S(1)}, u32[]{:S(2)}, u32[]{:S(2)}) %collective-permute-start.1) | collective-permute-done | bytes 139296 | tf_op jit(solution)/shard_map/ppermute | solution.py:39
  20.5 1.6 %copy-done.4 = bf16[2048,8,64]{0,2,1:T(8,128)(2,1)S(1)} copy-done((bf16[2048,8,64]{0,2,1:T(8,128)(2,1)S(1)}, bf16[2048,8,64]{0,2,1:T(8,128)(2,1)}, u32[]{:S(2)}) %copy-start.4) | copy-done | bytes 2097176
  22.1 1.6 %copy-done.5 = bf16[2048,8,64]{0,2,1:T(8,128)(2,1)S(1)} copy-done((bf16[2048,8,64]{0,2,1:T(8,128)(2,1)S(1)}, bf16[2048,8,64]{0,2,1:T(8,128)(2,1)}, u32[]{:S(2)}) %copy-start.5) | copy-done | bytes 2097176
  23.7 1.5 %shard_map.177 = (f32[64,128]{1,0:T(8,128)S(1)}, bf16[64,128]{1,0:T(8,128)(2,1)S(1)}) custom-call(bf16[16,2176]{1,0:T(8,128)(2,1)S(1)} %get-tuple-element.27.own_ref, bf16[32,2176]{1,0:T(8,128)(2,1)S(1)} %collective-permute-done.in1_ref, bf16[32,2176]{1,0:T(8,128)(2,1)S(1)} %collective-permute-done.1.in2_ref, ...), custom_call_target="tpu_custom_call" | custom-call | flops 1000 | bytes 1000 | tf_op jit(solution)/shard_map/pallas_call | solution.py:58
  25.2 0.6 collective-permute-start.6
  25.9 1.6 %shard_map.178 = (f32[64,1280]{1,0:T(8,128)S(1)}, f32[64,1280]{1,0:T(8,128)S(1)}) custom-call(s32[2]{0:T(128)S(1)} %pad_add_fusion.place_ref, bf16[32,2048]{1,0:T(8,128)(2,1)S(1)} %get-tuple-element.23.own_ref, bf16[32,2176]{1,0:T(8,128)(2,1)S(1)} %collective-permute-done.in1_ref, bf16[32,2176]{1,0:T(8,128)(2,1)S(1)} %collective-permute-done.1.in2_ref, ...), custom_call_target="tpu_custom_call" | custom-call | flops 1000 | bytes 1000 | tf_op jit(solution)/shard_map/pallas_call | solution.py:58
  27.4 2.2 %collective-permute-start.4 = (f32[64,1280]{1,0:T(8,128)S(1)}, f32[64,1280]{1,0:T(8,128)S(1)}, u32[]{:S(2)}, u32[]{:S(2)}) collective-permute-start(f32[64,1280]{1,0:T(8,128)S(1)} %get-tuple-element.31), channel_id=1, source_target_pairs={{0,4},{4,0},{8,12},{12,8},{1,5},{5,1},{9,13},{13,9},{2,6},{6,2},{1... | collective-permute-start | bytes 983048 | tf_op jit(solution)/shard_map/ppermute | solution.py:39
  29.6 1.6 %collective-permute-start.7 = (f32[64,128]{1,0:T(8,128)S(1)}, f32[64,128]{1,0:T(8,128)S(1)}, u32[]{:S(2)}, u32[]{:S(2)}) collective-permute-start(f32[64,128]{1,0:T(8,128)S(1)} %add.70.near_ref), channel_id=1, source_target_pairs={{0,2},{1,3},{2,0},{3,1},{4,6},{5,7},{6,4},{7,5},{8,10},{9,11},{10,... | collective-permute-start | bytes 98312 | tf_op jit(solution)/shard_map/ppermute | solution.py:39
  31.2 0.1 multiply_cosine_fusion.1
  31.3 2.3 %collective-permute-done.7.far_ref = f32[64,128]{1,0:T(8,128)S(1)} collective-permute-done((f32[64,128]{1,0:T(8,128)S(1)}, f32[64,128]{1,0:T(8,128)S(1)}, u32[]{:S(2)}, u32[]{:S(2)}) %collective-permute-start.7) | collective-permute-done | bytes 32800 | tf_op jit(solution)/shard_map/ppermute | solution.py:39
  33.6 0.4 shard_map.179
  34.0 0.1 collective-permute-start.8
  34.1 3.0 %collective-permute-start.9 = (bf16[16,1152]{1,0:T(8,128)(2,1)S(1)}, bf16[16,1152]{1,0:T(8,128)(2,1)S(1)}, u32[]{:S(2)}, u32[]{:S(2)}) collective-permute-start(bf16[16,1152]{1,0:T(8,128)(2,1)S(1)} %get-tuple-element.37), channel_id=1, source_target_pairs={{0,8},{4,12},{8,0},{12,4},{1,9},{5,13},{9,1},{13,5},{2,10},{6,14},... | collective-permute-start | bytes 110600 | tf_op jit(solution)/shard_map/ppermute | solution.py:39
  37.1 1.3 %collective-permute-start.10 = (bf16[16,1152]{1,0:T(8,128)(2,1)S(1)}, bf16[16,1152]{1,0:T(8,128)(2,1)S(1)}, u32[]{:S(2)}, u32[]{:S(2)}) collective-permute-start(bf16[16,1152]{1,0:T(8,128)(2,1)S(1)} %get-tuple-element.38), channel_id=1, source_target_pairs={{0,12},{4,8},{8,4},{12,0},{1,13},{5,9},{9,5},{13,1},{2,14},{6,10},... | collective-permute-start | bytes 110600 | tf_op jit(solution)/shard_map/ppermute | solution.py:39
  38.6 2.7 %collective-permute-start.5 = (f32[32,1280]{1,0:T(8,128)S(1)}, f32[32,1280]{1,0:T(8,128)S(1)}, u32[]{:S(2)}, u32[]{:S(2)}) collective-permute-start(f32[32,1280]{1,0:T(8,128)S(1)} %slice.124), channel_id=1, source_target_pairs={{0,8},{4,12},{8,0},{12,4},{1,9},{5,13},{9,1},{13,5},{2,10},{6,14},... | collective-permute-start | bytes 491528 | tf_op jit(solution)/shard_map/ppermute | solution.py:39
  41.3 1.9 %collective-permute-done.10 = bf16[16,1152]{1,0:T(8,128)(2,1)S(1)} collective-permute-done((bf16[16,1152]{1,0:T(8,128)(2,1)S(1)}, bf16[16,1152]{1,0:T(8,128)(2,1)S(1)}, u32[]{:S(2)}, u32[]{:S(2)}) %collective-permute-start.10) | collective-permute-done | bytes 36896 | tf_op jit(solution)/shard_map/ppermute | solution.py:39
  43.3 0.2 fusion.18
  43.5 5.5 %collective-permute-done.5 = f32[32,1280]{1,0:T(8,128)S(1)} collective-permute-done((f32[32,1280]{1,0:T(8,128)S(1)}, f32[32,1280]{1,0:T(8,128)S(1)}, u32[]{:S(2)}, u32[]{:S(2)}) %collective-permute-start.5) | collective-permute-done | bytes 163872 | tf_op jit(solution)/shard_map/ppermute | solution.py:39
  49.0 0.1 fusion.48
  49.2 0.1 maximum_bitcast_fusion
  49.2 0.1 fusion.28
  49.4 0.2 fusion.43
  49.6 0.8 select_reduce_fusion
  50.4 0.2 fusion.27
  50.6 0.4 fusion
  51.1 2.1 %collective-permute-start.13 = (bf16[32,1536]{1,0:T(8,128)(2,1)S(1)}, bf16[32,1536]{1,0:T(8,128)(2,1)S(1)}, u32[]{:S(2)}, u32[]{:S(2)}) collective-permute-start(bf16[32,1536]{1,0:T(8,128)(2,1)S(1)} %get-tuple-element.66), channel_id=1, source_target_pairs={{0,12},{4,8},{8,4},{12,0},{1,13},{5,9},{9,5},{13,1},{2,14},{6,10},... | collective-permute-start | bytes 294920 | tf_op jit(solution)/shard_map/ppermute | solution.py:39
  53.2 2.4 %collective-permute-start.12 = (bf16[32,1536]{1,0:T(8,128)(2,1)S(1)}, bf16[32,1536]{1,0:T(8,128)(2,1)S(1)}, u32[]{:S(2)}, u32[]{:S(2)}) collective-permute-start(bf16[32,1536]{1,0:T(8,128)(2,1)S(1)} %get-tuple-element.68), channel_id=1, source_target_pairs={{0,8},{4,12},{8,0},{12,4},{1,9},{5,13},{9,1},{13,5},{2,10},{6,14},... | collective-permute-start | bytes 294920 | tf_op jit(solution)/shard_map/ppermute | solution.py:39
  55.6 3.1 %collective-permute-done.13.in3_ref = bf16[32,1536]{1,0:T(8,128)(2,1)S(1)} collective-permute-done((bf16[32,1536]{1,0:T(8,128)(2,1)S(1)}, bf16[32,1536]{1,0:T(8,128)(2,1)S(1)}, u32[]{:S(2)}, u32[]{:S(2)}) %collective-permute-start.13) | collective-permute-done | bytes 98336 | tf_op jit(solution)/shard_map/ppermute | solution.py:39
  58.7 2.8 %collective-permute-done.11.in1_ref = bf16[32,1536]{1,0:T(8,128)(2,1)S(1)} collective-permute-done((bf16[32,1536]{1,0:T(8,128)(2,1)S(1)}, bf16[32,1536]{1,0:T(8,128)(2,1)S(1)}, u32[]{:S(2)}, u32[]{:S(2)}) %collective-permute-start.11) | collective-permute-done | bytes 98336 | tf_op jit(solution)/shard_map/ppermute | solution.py:39
  61.4 0.4 collective-permute-done.12.in2_ref
  61.8 1.4 %shard_map.180 = (f32[64,2048]{1,0:T(8,128)S(1)}, f32[64,2048]{1,0:T(8,128)S(1)}) custom-call(s32[2]{0:T(128)S(1)} %pad_add_fusion.place_ref, bf16[32,1536]{1,0:T(8,128)(2,1)S(1)} %get-tuple-element.69.own_ref, bf16[32,1536]{1,0:T(8,128)(2,1)S(1)} %collective-permute-done.11.in1_ref, bf16[32,1536]{1,0:T(8,128)(2,1)S(1)} %collective-permute-done.12.in2_ref, ...), custom_call_target="tpu_custom_call" | custom-call | flops 1000 | bytes 1000 | tf_op jit(solution)/shard_map/pallas_call | solution.py:58
  63.3 1.9 %collective-permute-done.14 = f32[64,2048]{1,0:T(8,128)S(1)} collective-permute-done((f32[64,2048]{1,0:T(8,128)S(1)}, f32[64,2048]{1,0:T(8,128)S(1)}, u32[]{:S(2)}, u32[]{:S(2)}) %collective-permute-start.14) | collective-permute-done | bytes 524320 | tf_op jit(solution)/shard_map/ppermute | solution.py:39
  65.2 1.4 %collective-permute-start.15 = (f32[32,2048]{1,0:T(8,128)S(1)}, f32[32,2048]{1,0:T(8,128)S(1)}, u32[]{:S(2)}, u32[]{:S(2)}) collective-permute-start(f32[32,2048]{1,0:T(8,128)S(1)} %slice.135), channel_id=1, source_target_pairs={{0,2},{1,3},{2,0},{3,1},{4,6},{5,7},{6,4},{7,5},{8,10},{9,11},{10,... | collective-permute-start | bytes 786440 | tf_op jit(solution)/shard_map/ppermute | solution.py:39
  66.7 7.0 %collective-permute-done.15 = f32[32,2048]{1,0:T(8,128)S(1)} collective-permute-done((f32[32,2048]{1,0:T(8,128)S(1)}, f32[32,2048]{1,0:T(8,128)S(1)}, u32[]{:S(2)}, u32[]{:S(2)}) %collective-permute-start.15) | collective-permute-done | bytes 262176 | tf_op jit(solution)/shard_map/ppermute | solution.py:39
  73.7 0.1 multiply_reduce_fusion
  73.8 1.9 %collective-permute-start.20 = (f32[32]{0:T(128)S(1)}, f32[32]{0:T(128)S(1)}, u32[]{:S(2)}, u32[]{:S(2)}) collective-permute-start(f32[32]{0:T(128)S(1)} %get-tuple-element.50), channel_id=1, source_target_pairs={{0,12},{4,8},{8,4},{12,0},{1,13},{5,9},{9,5},{13,1},{2,14},{6,10},... | collective-permute-start | bytes 392 | tf_op jit(solution)/shard_map/ppermute | solution.py:39
  75.7 0.2 collective-permute-start.19
  75.8 2.4 %collective-permute-start.18 = (f32[32]{0:T(128)S(1)}, f32[32]{0:T(128)S(1)}, u32[]{:S(2)}, u32[]{:S(2)}) collective-permute-start(f32[32]{0:T(128)S(1)} %get-tuple-element.50), channel_id=1, source_target_pairs={{0,4},{4,0},{8,12},{12,8},{1,5},{5,1},{9,13},{13,9},{2,6},{6,2},{1... | collective-permute-start | bytes 392 | tf_op jit(solution)/shard_map/ppermute | solution.py:39
  78.3 1.4 %collective-permute-start.16 = (bf16[32,2048]{1,0:T(8,128)(2,1)S(1)}, bf16[32,2048]{1,0:T(8,128)(2,1)S(1)}, u32[]{:S(2)}, u32[]{:S(2)}) collective-permute-start(bf16[32,2048]{1,0:T(8,128)(2,1)S(1)} %get-tuple-element.51.own_ref), channel_id=1, source_target_pairs={{0,2},{1,3},{2,0},{3,1},{4,6},{5,7},{6,4},{7,5},{8,10},{9,11},{10,... | collective-permute-start | bytes 393224 | tf_op jit(solution)/shard_map/ppermute | solution.py:39
  79.6 0.5 collective-permute-done.19
  80.1 1.5 %collective-permute-start.21 = (f32[1,32]{1,0:T(1,128)S(1)}, f32[1,32]{1,0:T(1,128)S(1)}, u32[]{:S(2)}, u32[]{:S(2)}) collective-permute-start(f32[1,32]{1,0:T(1,128)S(1)} %rsqrt_bitcast_fusion), channel_id=1, source_target_pairs={{0,2},{1,3},{2,0},{3,1},{4,6},{5,7},{6,4},{7,5},{8,10},{9,11},{10,... | collective-permute-start | bytes 392 | tf_op jit(solution)/shard_map/ppermute | solution.py:39
  81.6 1.6 %collective-permute-done.16.across_ref = bf16[32,2048]{1,0:T(8,128)(2,1)S(1)} collective-permute-done((bf16[32,2048]{1,0:T(8,128)(2,1)S(1)}, bf16[32,2048]{1,0:T(8,128)(2,1)S(1)}, u32[]{:S(2)}, u32[]{:S(2)}) %collective-permute-start.16) | collective-permute-done | bytes 131104 | tf_op jit(solution)/shard_map/ppermute | solution.py:39
  83.3 0.4 collective-permute-done.21
  83.7 0.2 collective-permute-start.22
  83.9 0.2 slice_reduce_fusion.1
  84.1 0.9 collective-permute-done.22
  85.0 2.0 %shard_map.182 = f32[128,2048]{1,0:T(8,128)S(1)} custom-call(s32[2]{0:T(128)S(1)} %pad_add_fusion.place_ref, bf16[32,2048]{1,0:T(8,128)(2,1)S(1)} %get-tuple-element.51.own_ref, bf16[32,2048]{1,0:T(8,128)(2,1)S(1)} %collective-permute-done.16.across_ref, bf16[64,2048]{1,0:T(8,128)(2,1)S(1)} %collective-permute-done.17.pair_ref, ...), custom_call_target="tpu_custom_call" | custom-call | flops 1000 | bytes 1000 | tf_op jit(solution)/shard_map/pallas_call | solution.py:58
  87.1 1.7 %collective-permute-start.26 = (f16[32,2048]{1,0:T(8,128)(2,1)S(1)}, f16[32,2048]{1,0:T(8,128)(2,1)S(1)}, u32[]{:S(2)}, u32[]{:S(2)}) collective-permute-start(f16[32,2048]{1,0:T(8,128)(2,1)S(1)} %get-tuple-element.55), channel_id=1, source_target_pairs={{0,4},{4,0},{8,12},{12,8},{1,5},{5,1},{9,13},{13,9},{2,6},{6,2},{1... | collective-permute-start | bytes 393224 | tf_op jit(solution)/shard_map/ppermute | solution.py:39
  88.7 1.8 %collective-permute-start.28 = (f16[32,2048]{1,0:T(8,128)(2,1)S(1)}, f16[32,2048]{1,0:T(8,128)(2,1)S(1)}, u32[]{:S(2)}, u32[]{:S(2)}) collective-permute-start(f16[32,2048]{1,0:T(8,128)(2,1)S(1)} %get-tuple-element.56), channel_id=1, source_target_pairs={{0,12},{4,8},{8,4},{12,0},{1,13},{5,9},{9,5},{13,1},{2,14},{6,10},... | collective-permute-start | bytes 393224 | tf_op jit(solution)/shard_map/ppermute | solution.py:39
  90.6 2.0 %shard_map.181 = f32[128,2048]{1,0:T(8,128)S(1)} custom-call(s32[2]{0:T(128)S(1)} %pad_add_fusion.place_ref, bf16[32,2048]{1,0:T(8,128)(2,1)S(1)} %get-tuple-element.51.own_ref, bf16[32,2048]{1,0:T(8,128)(2,1)S(1)} %collective-permute-done.16.across_ref, bf16[64,2048]{1,0:T(8,128)(2,1)S(1)} %collective-permute-done.17.pair_ref, ...), custom_call_target="tpu_custom_call" | custom-call | flops 1000 | bytes 1000 | tf_op jit(solution)/shard_map/pallas_call | solution.py:58
  92.7 2.6 %collective-permute-start.23 = (f16[32,2048]{1,0:T(8,128)(2,1)S(1)}, f16[32,2048]{1,0:T(8,128)(2,1)S(1)}, u32[]{:S(2)}, u32[]{:S(2)}) collective-permute-start(f16[32,2048]{1,0:T(8,128)(2,1)S(1)} %get-tuple-element.52), channel_id=1, source_target_pairs={{0,4},{4,0},{8,12},{12,8},{1,5},{5,1},{9,13},{13,9},{2,6},{6,2},{1... | collective-permute-start | bytes 393224 | tf_op jit(solution)/shard_map/ppermute | solution.py:39
  95.3 1.8 %collective-permute-start.25 = (f16[32,2048]{1,0:T(8,128)(2,1)S(1)}, f16[32,2048]{1,0:T(8,128)(2,1)S(1)}, u32[]{:S(2)}, u32[]{:S(2)}) collective-permute-start(f16[32,2048]{1,0:T(8,128)(2,1)S(1)} %get-tuple-element.53), channel_id=1, source_target_pairs={{0,12},{4,8},{8,4},{12,0},{1,13},{5,9},{9,5},{13,1},{2,14},{6,10},... | collective-permute-start | bytes 393224 | tf_op jit(solution)/shard_map/ppermute | solution.py:39
  97.1 0.7 collective-permute-done.28
  97.8 5.6 %collective-permute-done.27 = f16[32,2048]{1,0:T(8,128)(2,1)S(1)} collective-permute-done((f16[32,2048]{1,0:T(8,128)(2,1)S(1)}, f16[32,2048]{1,0:T(8,128)(2,1)S(1)}, u32[]{:S(2)}, u32[]{:S(2)}) %collective-permute-start.27) | collective-permute-done | bytes 131104 | tf_op jit(solution)/shard_map/ppermute | solution.py:39
  103.4 0.1 fusion.9
  103.5 2.7 %collective-permute-done.25 = f16[32,2048]{1,0:T(8,128)(2,1)S(1)} collective-permute-done((f16[32,2048]{1,0:T(8,128)(2,1)S(1)}, f16[32,2048]{1,0:T(8,128)(2,1)S(1)}, u32[]{:S(2)}, u32[]{:S(2)}) %collective-permute-start.25) | collective-permute-done | bytes 131104 | tf_op jit(solution)/shard_map/ppermute | solution.py:39
  106.2 7.3 %collective-permute-done.24 = f16[32,2048]{1,0:T(8,128)(2,1)S(1)} collective-permute-done((f16[32,2048]{1,0:T(8,128)(2,1)S(1)}, f16[32,2048]{1,0:T(8,128)(2,1)S(1)}, u32[]{:S(2)}, u32[]{:S(2)}) %collective-permute-start.24) | collective-permute-done | bytes 131104 | tf_op jit(solution)/shard_map/ppermute | solution.py:39
  113.6 0.1 fusion.16
  113.7 1.2 %copy.20 = f32[32,2,2048]{2,1,0:T(2,128)} copy(f32[32,2,2048]{2,0,1:T(8,128)S(1)} %pad_maximum_fusion) | data formatting | bytes 1048576
  (72 shorter events, 1.1 us)
Async XLA Ops:
  0.6 49.0 %copy-start = (bf16[32,1,128,128]{3,2,1,0:T(8,128)(2,1)S(1)}, bf16[32,1,128,128]{3,2,1,0:T(8,128)(2,1)}, u32[]{:S(2)}) copy-start(bf16[32,1,128,128]{3,2,1,0:T(8,128)(2,1)} %param.26) | copy-start | bytes 3145732
  0.6 25.2 %copy-start.12 = (s32[32]{0:T(128)S(1)}, s32[32]{0:T(128)}, u32[]{:S(2)}) copy-start(s32[32]{0:T(128)} %param.29) | copy-start | bytes 388
  0.7 25.2 %copy-start.2 = (bf16[2048,1024]{1,0:T(8,128)(2,1)S(1)}, bf16[2048,1024]{1,0:T(8,128)(2,1)}, u32[]{:S(2)}) copy-start(bf16[2048,1024]{1,0:T(8,128)(2,1)} %query_ref.1) | copy-start | bytes 12582916
  0.7 0.8 copy-start.11
  3.8 8.5 %collective-permute-start = (bf16[32,2176]{1,0:T(8,128)(2,1)S(1)}, bf16[32,2176]{1,0:T(8,128)(2,1)S(1)}, u32[]{:S(2)}, u32[]{:S(2)}) collective-permute-start(bf16[32,2176]{1,0:T(8,128)(2,1)S(1)} %get-tuple-element.24), channel_id=1, source_target_pairs={{0,4},{4,0},{8,12},{12,8},{1,5},{5,1},{9,13},{13,9},{2,6},{6,2},{1... | collective-permute-start | bytes 417800 | tf_op jit(solution)/shard_map/ppermute | solution.py:39
  6.9 13.5 %collective-permute-start.1 = (bf16[32,2176]{1,0:T(8,128)(2,1)S(1)}, bf16[32,2176]{1,0:T(8,128)(2,1)S(1)}, u32[]{:S(2)}, u32[]{:S(2)}) collective-permute-start(bf16[32,2176]{1,0:T(8,128)(2,1)S(1)} %get-tuple-element.25), channel_id=1, source_target_pairs={{0,8},{4,12},{8,0},{12,4},{1,9},{5,13},{9,1},{13,5},{2,10},{6,14},... | collective-permute-start | bytes 417800 | tf_op jit(solution)/shard_map/ppermute | solution.py:39
  9.5 10.9 %collective-permute-start.2 = (bf16[32,2176]{1,0:T(8,128)(2,1)S(1)}, bf16[32,2176]{1,0:T(8,128)(2,1)S(1)}, u32[]{:S(2)}, u32[]{:S(2)}) collective-permute-start(bf16[32,2176]{1,0:T(8,128)(2,1)S(1)} %get-tuple-element.26), channel_id=1, source_target_pairs={{0,12},{4,8},{8,4},{12,0},{1,13},{5,9},{9,5},{13,1},{2,14},{6,10},... | collective-permute-start | bytes 417800 | tf_op jit(solution)/shard_map/ppermute | solution.py:39
  20.4 4.8 %collective-permute-start.3 = (bf16[48,2048]{1,0:T(8,128)(2,1)S(1)}, bf16[48,2048]{1,0:T(8,128)(2,1)S(1)}, u32[]{:S(2)}, u32[]{:S(2)}) collective-permute-start(bf16[48,2048]{1,0:T(8,128)(2,1)S(1)} %pad_maximum_fusion.2), channel_id=1, source_target_pairs={{0,1},{1,0},{2,3},{3,2},{4,5},{5,4},{6,7},{7,6},{8,9},{9,8},{10,11... | collective-permute-start | bytes 589832 | tf_op jit(solution)/shard_map/ppermute | solution.py:39
  20.5 1.6 %copy-start.4 = (bf16[2048,8,64]{0,2,1:T(8,128)(2,1)S(1)}, bf16[2048,8,64]{0,2,1:T(8,128)(2,1)}, u32[]{:S(2)}) copy-start(bf16[2048,8,64]{0,2,1:T(8,128)(2,1)} %param.22) | copy-start | bytes 6291460
  22.1 1.6 %copy-start.5 = (bf16[2048,8,64]{0,2,1:T(8,128)(2,1)S(1)}, bf16[2048,8,64]{0,2,1:T(8,128)(2,1)}, u32[]{:S(2)}) copy-start(bf16[2048,8,64]{0,2,1:T(8,128)(2,1)} %param.24) | copy-start | bytes 6291460
  23.7 2.2 %copy-start.8 = (bf16[2048,128]{1,0:T(8,128)(2,1)S(1)}, bf16[2048,128]{1,0:T(8,128)(2,1)}, u32[]{:S(2)}) copy-start(bf16[2048,128]{1,0:T(8,128)(2,1)} %key_ref.1) | copy-start | bytes 1572868
  23.7 2.2 %copy-start.9 = (bf16[2048,128]{1,0:T(8,128)(2,1)S(1)}, bf16[2048,128]{1,0:T(8,128)(2,1)}, u32[]{:S(2)}) copy-start(bf16[2048,128]{1,0:T(8,128)(2,1)} %value_ref.1) | copy-start | bytes 1572868
  23.7 26.9 %copy-start.13 = (bf16[32,1,128,128]{3,2,1,0:T(8,128)(2,1)S(1)}, bf16[32,1,128,128]{3,2,1,0:T(8,128)(2,1)}, u32[]{:S(2)}) copy-start(bf16[32,1,128,128]{3,2,1,0:T(8,128)(2,1)} %param.27) | copy-start | bytes 3145732
  25.2 8.4 %copy-start.7 = (bf16[8,64,1024]{2,1,0:T(8,128)(2,1)S(1)}, bf16[8,64,1024]{2,1,0:T(8,128)(2,1)}, u32[]{:S(2)}) copy-start(bf16[8,64,1024]{2,1,0:T(8,128)(2,1)} %param.23) | copy-start | bytes 3145732
  25.2 8.4 %copy-start.10 = (bf16[8,64,128]{2,1,0:T(8,128)(2,1)S(1)}, bf16[8,64,128]{2,1,0:T(8,128)(2,1)}, u32[]{:S(2)}) copy-start(bf16[8,64,128]{2,1,0:T(8,128)(2,1)} %param.25) | copy-start | bytes 393220
  25.2 4.4 %collective-permute-start.6 = (f32[64,128]{1,0:T(8,128)S(1)}, f32[64,128]{1,0:T(8,128)S(1)}, u32[]{:S(2)}, u32[]{:S(2)}) collective-permute-start(f32[64,128]{1,0:T(8,128)S(1)} %get-tuple-element.33), channel_id=1, source_target_pairs={{0,1},{1,0},{2,3},{3,2},{4,5},{5,4},{6,7},{7,6},{8,9},{9,8},{10,11... | collective-permute-start | bytes 98312 | tf_op jit(solution)/shard_map/ppermute | solution.py:39
  25.8 36.0 %copy-start.3 = (bf16[1024,2048]{1,0:T(8,128)(2,1)S(1)}, bf16[1024,2048]{1,0:T(8,128)(2,1)}, u32[]{:S(2)}) copy-start(bf16[1024,2048]{1,0:T(8,128)(2,1)} %weight_ref.3) | copy-start | bytes 12582916
  25.9 59.1 %copy-start.1 = (bf16[2048,4096]{1,0:T(8,128)(2,1)S(1)}, bf16[2048,4096]{1,0:T(8,128)(2,1)}, u32[]{:S(2)}) copy-start(bf16[2048,4096]{1,0:T(8,128)(2,1)} %weight_ref.5) | copy-start | bytes 50331652
  27.4 11.1 %collective-permute-start.4 = (f32[64,1280]{1,0:T(8,128)S(1)}, f32[64,1280]{1,0:T(8,128)S(1)}, u32[]{:S(2)}, u32[]{:S(2)}) collective-permute-start(f32[64,1280]{1,0:T(8,128)S(1)} %get-tuple-element.31), channel_id=1, source_target_pairs={{0,4},{4,0},{8,12},{12,8},{1,5},{5,1},{9,13},{13,9},{2,6},{6,2},{1... | collective-permute-start | bytes 983048 | tf_op jit(solution)/shard_map/ppermute | solution.py:39
  29.6 4.0 %collective-permute-start.7 = (f32[64,128]{1,0:T(8,128)S(1)}, f32[64,128]{1,0:T(8,128)S(1)}, u32[]{:S(2)}, u32[]{:S(2)}) collective-permute-start(f32[64,128]{1,0:T(8,128)S(1)} %add.70.near_ref), channel_id=1, source_target_pairs={{0,2},{1,3},{2,0},{3,1},{4,6},{5,7},{6,4},{7,5},{8,10},{9,11},{10,... | collective-permute-start | bytes 98312 | tf_op jit(solution)/shard_map/ppermute | solution.py:39
  34.0 7.4 %collective-permute-start.8 = (bf16[16,1152]{1,0:T(8,128)(2,1)S(1)}, bf16[16,1152]{1,0:T(8,128)(2,1)S(1)}, u32[]{:S(2)}, u32[]{:S(2)}) collective-permute-start(bf16[16,1152]{1,0:T(8,128)(2,1)S(1)} %get-tuple-element.36), channel_id=1, source_target_pairs={{0,4},{4,0},{8,12},{12,8},{1,5},{5,1},{9,13},{13,9},{2,6},{6,2},{1... | collective-permute-start | bytes 110600 | tf_op jit(solution)/shard_map/ppermute | solution.py:39
  34.1 7.3 %collective-permute-start.9 = (bf16[16,1152]{1,0:T(8,128)(2,1)S(1)}, bf16[16,1152]{1,0:T(8,128)(2,1)S(1)}, u32[]{:S(2)}, u32[]{:S(2)}) collective-permute-start(bf16[16,1152]{1,0:T(8,128)(2,1)S(1)} %get-tuple-element.37), channel_id=1, source_target_pairs={{0,8},{4,12},{8,0},{12,4},{1,9},{5,13},{9,1},{13,5},{2,10},{6,14},... | collective-permute-start | bytes 110600 | tf_op jit(solution)/shard_map/ppermute | solution.py:39
  37.1 6.2 %collective-permute-start.10 = (bf16[16,1152]{1,0:T(8,128)(2,1)S(1)}, bf16[16,1152]{1,0:T(8,128)(2,1)S(1)}, u32[]{:S(2)}, u32[]{:S(2)}) collective-permute-start(bf16[16,1152]{1,0:T(8,128)(2,1)S(1)} %get-tuple-element.38), channel_id=1, source_target_pairs={{0,12},{4,8},{8,4},{12,0},{1,13},{5,9},{9,5},{13,1},{2,14},{6,10},... | collective-permute-start | bytes 110600 | tf_op jit(solution)/shard_map/ppermute | solution.py:39
  38.6 10.3 %collective-permute-start.5 = (f32[32,1280]{1,0:T(8,128)S(1)}, f32[32,1280]{1,0:T(8,128)S(1)}, u32[]{:S(2)}, u32[]{:S(2)}) collective-permute-start(f32[32,1280]{1,0:T(8,128)S(1)} %slice.124), channel_id=1, source_target_pairs={{0,8},{4,12},{8,0},{12,4},{1,9},{5,13},{9,1},{13,5},{2,10},{6,14},... | collective-permute-start | bytes 491528 | tf_op jit(solution)/shard_map/ppermute | solution.py:39
  51.1 7.5 %collective-permute-start.13 = (bf16[32,1536]{1,0:T(8,128)(2,1)S(1)}, bf16[32,1536]{1,0:T(8,128)(2,1)S(1)}, u32[]{:S(2)}, u32[]{:S(2)}) collective-permute-start(bf16[32,1536]{1,0:T(8,128)(2,1)S(1)} %get-tuple-element.66), channel_id=1, source_target_pairs={{0,12},{4,8},{8,4},{12,0},{1,13},{5,9},{9,5},{13,1},{2,14},{6,10},... | collective-permute-start | bytes 294920 | tf_op jit(solution)/shard_map/ppermute | solution.py:39
  53.2 8.2 %collective-permute-start.11 = (bf16[32,1536]{1,0:T(8,128)(2,1)S(1)}, bf16[32,1536]{1,0:T(8,128)(2,1)S(1)}, u32[]{:S(2)}, u32[]{:S(2)}) collective-permute-start(bf16[32,1536]{1,0:T(8,128)(2,1)S(1)} %get-tuple-element.67), channel_id=1, source_target_pairs={{0,4},{4,0},{8,12},{12,8},{1,5},{5,1},{9,13},{13,9},{2,6},{6,2},{1... | collective-permute-start | bytes 294920 | tf_op jit(solution)/shard_map/ppermute | solution.py:39
  53.2 8.6 %collective-permute-start.12 = (bf16[32,1536]{1,0:T(8,128)(2,1)S(1)}, bf16[32,1536]{1,0:T(8,128)(2,1)S(1)}, u32[]{:S(2)}, u32[]{:S(2)}) collective-permute-start(bf16[32,1536]{1,0:T(8,128)(2,1)S(1)} %get-tuple-element.68), channel_id=1, source_target_pairs={{0,8},{4,12},{8,0},{12,4},{1,9},{5,13},{9,1},{13,5},{2,10},{6,14},... | collective-permute-start | bytes 294920 | tf_op jit(solution)/shard_map/ppermute | solution.py:39
  63.2 2.0 %collective-permute-start.14 = (f32[64,2048]{1,0:T(8,128)S(1)}, f32[64,2048]{1,0:T(8,128)S(1)}, u32[]{:S(2)}, u32[]{:S(2)}) collective-permute-start(f32[64,2048]{1,0:T(8,128)S(1)} %get-tuple-element.41), channel_id=1, source_target_pairs={{0,1},{1,0},{2,3},{3,2},{4,5},{5,4},{6,7},{7,6},{8,9},{9,8},{10,11... | collective-permute-start | bytes 1572872 | tf_op jit(solution)/shard_map/ppermute | solution.py:39
  65.2 8.4 %collective-permute-start.15 = (f32[32,2048]{1,0:T(8,128)S(1)}, f32[32,2048]{1,0:T(8,128)S(1)}, u32[]{:S(2)}, u32[]{:S(2)}) collective-permute-start(f32[32,2048]{1,0:T(8,128)S(1)} %slice.135), channel_id=1, source_target_pairs={{0,2},{1,3},{2,0},{3,1},{4,6},{5,7},{6,4},{7,5},{8,10},{9,11},{10,... | collective-permute-start | bytes 786440 | tf_op jit(solution)/shard_map/ppermute | solution.py:39
  73.8 16.8 %copy-start.6 = (bf16[32,2048]{1,0:T(8,128)(2,1)}, bf16[32,2048]{1,0:T(8,128)(2,1)S(1)}, u32[]{:S(2)}) copy-start(bf16[32,2048]{1,0:T(8,128)(2,1)S(1)} %get-tuple-element.51.own_ref) | copy-start | bytes 393220
  73.8 5.8 %collective-permute-start.20 = (f32[32]{0:T(128)S(1)}, f32[32]{0:T(128)S(1)}, u32[]{:S(2)}, u32[]{:S(2)}) collective-permute-start(f32[32]{0:T(128)S(1)} %get-tuple-element.50), channel_id=1, source_target_pairs={{0,12},{4,8},{8,4},{12,0},{1,13},{5,9},{9,5},{13,1},{2,14},{6,10},... | collective-permute-start | bytes 392 | tf_op jit(solution)/shard_map/ppermute | solution.py:39
  75.7 4.4 %collective-permute-start.19 = (f32[32]{0:T(128)S(1)}, f32[32]{0:T(128)S(1)}, u32[]{:S(2)}, u32[]{:S(2)}) collective-permute-start(f32[32]{0:T(128)S(1)} %get-tuple-element.50), channel_id=1, source_target_pairs={{0,8},{4,12},{8,0},{12,4},{1,9},{5,13},{9,1},{13,5},{2,10},{6,14},... | collective-permute-start | bytes 392 | tf_op jit(solution)/shard_map/ppermute | solution.py:39
  75.8 4.3 %collective-permute-start.18 = (f32[32]{0:T(128)S(1)}, f32[32]{0:T(128)S(1)}, u32[]{:S(2)}, u32[]{:S(2)}) collective-permute-start(f32[32]{0:T(128)S(1)} %get-tuple-element.50), channel_id=1, source_target_pairs={{0,4},{4,0},{8,12},{12,8},{1,5},{5,1},{9,13},{13,9},{2,6},{6,2},{1... | collective-permute-start | bytes 392 | tf_op jit(solution)/shard_map/ppermute | solution.py:39
  78.3 5.0 %collective-permute-start.16 = (bf16[32,2048]{1,0:T(8,128)(2,1)S(1)}, bf16[32,2048]{1,0:T(8,128)(2,1)S(1)}, u32[]{:S(2)}, u32[]{:S(2)}) collective-permute-start(bf16[32,2048]{1,0:T(8,128)(2,1)S(1)} %get-tuple-element.51.own_ref), channel_id=1, source_target_pairs={{0,2},{1,3},{2,0},{3,1},{4,6},{5,7},{6,4},{7,5},{8,10},{9,11},{10,... | collective-permute-start | bytes 393224 | tf_op jit(solution)/shard_map/ppermute | solution.py:39
  80.1 3.6 %collective-permute-start.21 = (f32[1,32]{1,0:T(1,128)S(1)}, f32[1,32]{1,0:T(1,128)S(1)}, u32[]{:S(2)}, u32[]{:S(2)}) collective-permute-start(f32[1,32]{1,0:T(1,128)S(1)} %rsqrt_bitcast_fusion), channel_id=1, source_target_pairs={{0,2},{1,3},{2,0},{3,1},{4,6},{5,7},{6,4},{7,5},{8,10},{9,11},{10,... | collective-permute-start | bytes 392 | tf_op jit(solution)/shard_map/ppermute | solution.py:39
  83.2 1.7 %collective-permute-start.17 = (bf16[64,2048]{1,0:T(8,128)(2,1)S(1)}, bf16[64,2048]{1,0:T(8,128)(2,1)S(1)}, u32[]{:S(2)}, u32[]{:S(2)}) collective-permute-start(bf16[64,2048]{1,0:T(8,128)(2,1)S(1)} %pad_maximum_fusion.1), channel_id=1, source_target_pairs={{0,1},{1,0},{2,3},{3,2},{4,5},{5,4},{6,7},{7,6},{8,9},{9,8},{10,11... | collective-permute-start | bytes 786440 | tf_op jit(solution)/shard_map/ppermute | solution.py:39
  83.7 1.2 %collective-permute-start.22 = (f32[2,32]{1,0:T(2,128)S(1)}, f32[2,32]{1,0:T(2,128)S(1)}, u32[]{:S(2)}, u32[]{:S(2)}) collective-permute-start(f32[2,32]{1,0:T(2,128)S(1)} %pad_maximum_fusion.11), channel_id=1, source_target_pairs={{0,1},{1,0},{2,3},{3,2},{4,5},{5,4},{6,7},{7,6},{8,9},{9,8},{10,11... | collective-permute-start | bytes 776 | tf_op jit(solution)/shard_map/ppermute | solution.py:39
  87.1 10.0 %collective-permute-start.26 = (f16[32,2048]{1,0:T(8,128)(2,1)S(1)}, f16[32,2048]{1,0:T(8,128)(2,1)S(1)}, u32[]{:S(2)}, u32[]{:S(2)}) collective-permute-start(f16[32,2048]{1,0:T(8,128)(2,1)S(1)} %get-tuple-element.55), channel_id=1, source_target_pairs={{0,4},{4,0},{8,12},{12,8},{1,5},{5,1},{9,13},{13,9},{2,6},{6,2},{1... | collective-permute-start | bytes 393224 | tf_op jit(solution)/shard_map/ppermute | solution.py:39
  88.7 9.0 %collective-permute-start.28 = (f16[32,2048]{1,0:T(8,128)(2,1)S(1)}, f16[32,2048]{1,0:T(8,128)(2,1)S(1)}, u32[]{:S(2)}, u32[]{:S(2)}) collective-permute-start(f16[32,2048]{1,0:T(8,128)(2,1)S(1)} %get-tuple-element.56), channel_id=1, source_target_pairs={{0,12},{4,8},{8,4},{12,0},{1,13},{5,9},{9,5},{13,1},{2,14},{6,10},... | collective-permute-start | bytes 393224 | tf_op jit(solution)/shard_map/ppermute | solution.py:39
  90.6 12.9 %collective-permute-start.27 = (f16[32,2048]{1,0:T(8,128)(2,1)S(1)}, f16[32,2048]{1,0:T(8,128)(2,1)S(1)}, u32[]{:S(2)}, u32[]{:S(2)}) collective-permute-start(f16[32,2048]{1,0:T(8,128)(2,1)S(1)} %get-tuple-element.57), channel_id=1, source_target_pairs={{0,8},{4,12},{8,0},{12,4},{1,9},{5,13},{9,1},{13,5},{2,10},{6,14},... | collective-permute-start | bytes 393224 | tf_op jit(solution)/shard_map/ppermute | solution.py:39
  92.7 10.8 %collective-permute-start.23 = (f16[32,2048]{1,0:T(8,128)(2,1)S(1)}, f16[32,2048]{1,0:T(8,128)(2,1)S(1)}, u32[]{:S(2)}, u32[]{:S(2)}) collective-permute-start(f16[32,2048]{1,0:T(8,128)(2,1)S(1)} %get-tuple-element.52), channel_id=1, source_target_pairs={{0,4},{4,0},{8,12},{12,8},{1,5},{5,1},{9,13},{13,9},{2,6},{6,2},{1... | collective-permute-start | bytes 393224 | tf_op jit(solution)/shard_map/ppermute | solution.py:39
  95.3 10.9 %collective-permute-start.25 = (f16[32,2048]{1,0:T(8,128)(2,1)S(1)}, f16[32,2048]{1,0:T(8,128)(2,1)S(1)}, u32[]{:S(2)}, u32[]{:S(2)}) collective-permute-start(f16[32,2048]{1,0:T(8,128)(2,1)S(1)} %get-tuple-element.53), channel_id=1, source_target_pairs={{0,12},{4,8},{8,4},{12,0},{1,13},{5,9},{9,5},{13,1},{2,14},{6,10},... | collective-permute-start | bytes 393224 | tf_op jit(solution)/shard_map/ppermute | solution.py:39
  97.1 16.5 %collective-permute-start.24 = (f16[32,2048]{1,0:T(8,128)(2,1)S(1)}, f16[32,2048]{1,0:T(8,128)(2,1)S(1)}, u32[]{:S(2)}, u32[]{:S(2)}) collective-permute-start(f16[32,2048]{1,0:T(8,128)(2,1)S(1)} %get-tuple-element.54), channel_id=1, source_target_pairs={{0,8},{4,12},{8,0},{12,4},{1,9},{5,13},{9,1},{13,5},{2,10},{6,14},... | collective-permute-start | bytes 393224 | tf_op jit(solution)/shard_map/ppermute | solution.py:39

commit v4 on v3

--- a/solution.py
+++ b/solution.py
@@ -14,7 +14,6 @@
 ROPE_BASE = 500000.0
 NORM_EPS = 1e-05
 ADAPTER_SCALE = 0.5
-LOGIT_PARTS = 2
 KERNEL_VMEM = 8 << 20
 
 
@@ -47,9 +46,10 @@
     return pl.BlockSpec(memory_space=pltpu.VMEM)
 
 
-def call(kernel, outs, operands, scalars=(), scratch=(), resident=(), hbm=()):
+def call(kernel, outs, operands, scalars=(), scratch=(), resident=(), hbm=(), anywhere=()):
     hbm = [pltpu.with_memory_space_constraint(array, pltpu.HBM) for array in hbm]
     resident = [pltpu.with_memory_space_constraint(array, pltpu.VMEM) for array in resident]
+    hbm += anywhere
     specs = [pl.BlockSpec(memory_space=pl.ANY)] * len(hbm)
     specs += [full_spec()] * (len(operands) + len(resident))
     arrays = [*hbm, *operands, *resident]
@@ -71,9 +71,10 @@
 
 
 def norm_kernel(
-    n_adapter, voices, books, place_ref, delays_ref, tokens_hbm, gain_hbm, label_hbm, lengths_hbm, closing_hbm,
+    n_adapter, voices, books, place_ref,
+    tokens_hbm, gain_hbm, label_hbm, lengths_hbm, closing_hbm, delays_hbm,
     own_ref, rows_ref, out1_ref, out2_ref, out3_ref, placing_ref, raw_ref, active_ref, closing_ref,
-    normed_ref, tokens_ref, gain_ref, label_ref, lengths_ref, sems,
+    normed_ref, tokens_ref, gain_ref, label_ref, lengths_ref, delays_ref, sems,
 ):
     a, t = place_ref[0], place_ref[1]
     streams, model_width = tokens_ref.shape
@@ -88,6 +89,7 @@
                 (label_hbm, label_ref),
                 (lengths_hbm, lengths_ref),
                 (closing_part, closing_ref),
+                (delays_hbm, delays_ref),
             )
         )
     ]
@@ -134,8 +136,12 @@
     length_col = column(lengths_ref[...])
     lane = lax.broadcasted_iota(jnp.int32, active_ref.shape, 1)
     active = jnp.zeros(active_ref.shape, jnp.float32)
+    books_row = delays_ref[...].astype(jnp.float32)
+    book = lax.broadcasted_iota(jnp.int32, books_row.shape, 1)
     for p in range(books):
-        started = (length_col >= delays_ref[t * books + p]).astype(jnp.float32)
+        mine_only = jnp.where(book == t * books + p, books_row, 0.0)
+        delay = jnp.sum(mine_only, axis=1, keepdims=True).astype(jnp.int32)
+        started = (length_col >= delay).astype(jnp.float32)
         active = jnp.where(lane == p, started, active)
     active_ref[...] = active
     quarter = raw_ref.shape[2]
@@ -148,6 +154,21 @@
         out_ref[:half, d_slice:] = jnp.zeros((half, 128), jnp.bfloat16)
         out_ref[half:, :d_slice] = rows[k * cap : (k + 1) * cap]
         out_ref[half:, d_slice:] = kinds[k * cap : (k + 1) * cap]
+
+
+def fetch_kernel(question_hbm, content_hbm, after_hbm, question_ref, content_ref, sems):
+    copies = []
+    for source, target in ((question_hbm, question_ref), (content_hbm, content_ref)):
+        rows = source.shape[0] // 4
+        for i in range(4):
+            part = pl.ds(i * rows, rows)
+            copies.append(
+                pltpu.make_async_copy(source.at[part], target.at[part], sems.at[len(copies)])
+            )
+    for copy in copies:
+        copy.start()
+    for copy in copies:
+        copy.wait()
 
 
 def lowering_kernel(
@@ -251,7 +272,7 @@
 
 
 def head_kernel(
-    first, place_ref, own_ref, across_ref, pair_ref, scale_ref, gain_ref, weight_ref, out_ref, rows_ref
+    first, place_ref, own_ref, across_ref, pair_ref, scale_ref, gain_ref, weight_ref, keep_ref, send_ref, rows_ref
 ):
     turn = jnp.bitwise_xor(place_ref[0], place_ref[1])
     streams = own_ref.shape[0]
@@ -273,10 +294,14 @@
         rows_ref[pl.ds(at, streams), :] = (
             piece.astype(jnp.float32) * scale * gain_ref[...]
         ).astype(jnp.bfloat16)
-    width = out_ref.shape[1]
-    out_ref[...] = jnp.dot(
+    width = keep_ref.shape[1]
+    out = 16.0 * jnp.dot(
         rows_ref[...], weight_ref[:, first : first + width], preferred_element_type=jnp.float32
     )
+    keep_ref[:streams] = out[:streams]
+    send_ref[:streams] = out[streams : 2 * streams]
+    keep_ref[streams:] = out[2 * streams : 3 * streams]
+    send_ref[streams:] = out[3 * streams :]
 
 
 def per_device_four(
@@ -326,14 +351,15 @@
             shaped((1, d_slice), jnp.float32),
         ],
         [],
-        [place_ids, delays],
+        [place_ids],
         [
             pltpu.VMEM((str_dev, model_width), bf16),
             pltpu.VMEM((str_dev, model_width), bf16),
             pltpu.VMEM((1, model_width), jnp.float32),
             pltpu.VMEM((1, str_dev), jnp.int32),
             pltpu.VMEM((1, str_dev), jnp.int32),
-            pltpu.SemaphoreType.DMA((5,)),
+            pltpu.VMEM((1, CB), jnp.int32),
+            pltpu.SemaphoreType.DMA((6,)),
         ],
         hbm=[
             tokens,
@@ -341,19 +367,29 @@
             sequence_speaker_label[None],
             lengths[None],
             closing_gain[None],
+            delays[None],
         ],
     )
     came = [swap(payload, "adapter", k) for k, payload in zip(peers, outgoing)]
+    question_down, content_down = call(
+        fetch_kernel,
+        [pltpu.VMEM((voices * rank, d_slice), bf16)] * 2,
+        [],
+        scratch=[pltpu.SemaphoreType.DMA((8,))],
+        hbm=[
+            speaker_question_lowering.transpose(1, 2, 0).reshape(voices * rank, d_slice),
+            speaker_content_lowering.transpose(1, 2, 0).reshape(voices * rank, d_slice),
+        ],
+        anywhere=[own_cols],
+    )
+    came, question_down = lax.optimization_barrier((came, question_down))
     other = swap(jnp.concatenate([piece[:half, :d_slice] for piece in came]), "tensor", 1)
 
     down, onehot = call(
         functools.partial(lowering_kernel, voices, rank),
         [shaped((n_adapter * slot_cap, 2 * rank), jnp.float32), shaped((n_adapter * slot_cap, 128), bf16)],
         [own_rows, *came],
-        resident=[
-            speaker_question_lowering.transpose(1, 2, 0).reshape(voices * rank, d_slice),
-            speaker_content_lowering.transpose(1, 2, 0).reshape(voices * rank, d_slice),
-        ],
+        resident=[question_down, content_down],
     )
     other, down = lax.optimization_barrier((other, down))
     kept, sent = call(
@@ -437,7 +473,14 @@
         resident=[output_weight],
     )
     pair = kept + swap(sent, "tensor", 1)
-    summed_out = pair[:str_dev] + swap(pair[str_dev:], "tensor", 2)
+    leaving = pair[str_dev:]
+    largest = jnp.max(jnp.abs(leaving), axis=1, keepdims=True)
+    row_scale = jnp.minimum(16384.0 / jnp.maximum(largest, 1e-30), 32768.0).astype(jnp.float16)
+    coded = (leaving * row_scale.astype(jnp.float32)).astype(jnp.float16)
+    coded = jnp.concatenate([coded, jnp.broadcast_to(row_scale, (str_dev, 128))], axis=1)
+    coded = swap(coded, "tensor", 2)
+    arrived = coded[:, :d_slice].astype(jnp.float32) / coded[:, d_slice : d_slice + 1].astype(jnp.float32)
+    summed_out = pair[:str_dev] + arrived
     hidden_out = summed_out.astype(jnp.bfloat16)
 
     hidden_f = hidden_out.astype(jnp.float32)
@@ -451,24 +494,34 @@
     scale = jnp.concatenate([scale, swap(scale, "tensor", 2)])
     scale = jnp.concatenate([scale, swap(scale, "tensor", 1)])
 
-    width = codebook_weight.shape[1] // LOGIT_PARTS
+    width = codebook_weight.shape[1] // 2
     outs = []
-    for p in range(LOGIT_PARTS):
-        partial = call(
-            functools.partial(head_kernel, p * width),
-            [shaped((n_adapter * str_dev, width), jnp.float32)],
+
+    def head(first, ids):
+        return call(
+            functools.partial(head_kernel, first),
+            [shaped((2 * str_dev, width), jnp.float32)] * 2,
             [hidden_out, across, hidden_pair, scale, final_slice],
-            [place_ids],
+            [ids],
             [pltpu.VMEM((n_adapter * str_dev, d_slice), bf16)],
             resident=[codebook_weight],
-        )[0]
-        total_p = partial[:str_dev]
-        for k in peers:
-            block = partial[k * str_dev : (k + 1) * str_dev]
-            total_p = total_p + swap(
-                (block * 32.0).astype(jnp.float16), "adapter", k
-            ).astype(jnp.float32) * (1.0 / 32.0)
-        outs.append(total_p)
+        )
+
+    def moved(block, k):
+        return swap(block.astype(jnp.float16), "adapter", k).astype(jnp.float32)
+
+    kept, sent = head(0, place_ids)
+    kept, place_ids = lax.optimization_barrier((kept, place_ids))
+    kept_far, sent_far = head(width, place_ids)
+    kept = kept + moved(sent, 1)
+    first_total = kept[:str_dev] + moved(kept[str_dev:], 2)
+    second_total = (
+        kept_far[:str_dev]
+        + moved(sent_far[:str_dev], 1)
+        + moved(kept_far[str_dev:], 2)
+        + moved(sent_far[str_dev:], 3)
+    )
+    outs = [first_total * (1.0 / 16.0), second_total * (1.0 / 16.0)]
     if width == VOC:
         logits = jnp.stack([out * active[:, p : p + 1] for p, out in enumerate(outs)], axis=1)
     else:

time: 115 us -> 107 us (0.930)
  waiting for transfers between devices: 55.3 us -> 48.7 us
  local copies, waits for them, and re-layouts: 5.51 us -> 1.74 us
  Pallas kernels: 11.1 us -> 13.3 us
    ppermute x29 -> x28, waiting for transfers between devices: 55.3 us -> 48.7 us  [swap(): return lax.ppermute(value, axis, [(i, i ^ distance) for i in range(size)])]
    unnamed x31, local copies, waits for them, and re-layouts: 5.28 us -> 1.58 us
    pallas_call x7 -> x8, Pallas kernels: 11.1 us -> 13.3 us  [call(): pl.pallas_call(kernel, out_shape=tuple(outs), in_specs=specs, out_specs=t...]
    ppermute x29 -> x28, starting transfers between devices: 38.7 us -> 38.4 us  [swap(): return lax.ppermute(value, axis, [(i, i ^ distance) for i in range(size)])]
  transfers between devices with their start and end apart: 29 -> 28, of which waited for: 18 -> 18; matrix products, arithmetic and copies ran while one was open for 1% -> 1% of each run, Pallas kernels for 5% -> 7%
where the time goes in v4:
time: 107 us
  waiting for transfers between devices  48.7 us (46%)
  starting transfers between devices  38.4 us (36%)
  Pallas kernels  13.3 us (12%)
  other arithmetic  2.29 us (2%)
  local copies, waits for them, and re-layouts  1.74 us (2%)
  matrix products  1.62 us (2%)
  between operations  1.1 us (1%)
    ppermute x28, waiting for transfers between devices, swap(): return lax.ppermute(value, axis, [(i, i ^ distance) for i in range(size)])  48.7 us
    ppermute x28, starting transfers between devices, swap(): return lax.ppermute(value, axis, [(i, i ^ distance) for i in range(size)])  38.4 us
    pallas_call x8, Pallas kernels, call(): pl.pallas_call(kernel, out_shape=tuple(outs), in_specs=specs, out_specs=t...  13.3 us
  transfers between devices with their start and end apart: 28, of which 18 were waited for; matrix products, arithmetic and copies ran while one was open for 1% of the time, Pallas kernels for 7%

profile of v4, /device:TPU:0, one launch (start us, length us, event | category | flops | bytes accessed | tf_op | source)
XLA Modules:
  0.0 107.1 jit_solution(15729483593348515048)
XLA Ops:
  0.7 2.2 %shard_map.176 = (bf16[32,2048]{1,0:T(8,128)(2,1)S(1)}, bf16[16,2176]{1,0:T(8,128)(2,1)S(1)}, bf16[32,2176]{1,0:T(8,128)(2,1)S(1)}, bf16[32,2176]{1,0:T(8,128)(2...) custom-call(s32[2]{0:T(128)S(1)} %pad_add_fusion.place_ref, ...), custom_call_target="tpu_custom_call" | custom-call | flops 1000 | bytes 1000 | tf_op jit(solution)/shard_map/pallas_call | solution.py:58
  2.9 3.1 %collective-permute-start = (bf16[32,2176]{1,0:T(8,128)(2,1)S(1)}, bf16[32,2176]{1,0:T(8,128)(2,1)S(1)}, u32[]{:S(2)}, u32[]{:S(2)}) collective-permute-start(bf16[32,2176]{1,0:T(8,128)(2,1)S(1)} %get-tuple-element.36), channel_id=1, source_target_pairs={{0,4},{4,0},{8,12},{12,8},{1,5},{5,1},{9,13},{13,9},{2,6},{6,2},{1... | collective-permute-start | bytes 417800 | tf_op jit(solution)/shard_map/ppermute | solution.py:38
  6.0 2.6 %collective-permute-start.1 = (bf16[32,2176]{1,0:T(8,128)(2,1)S(1)}, bf16[32,2176]{1,0:T(8,128)(2,1)S(1)}, u32[]{:S(2)}, u32[]{:S(2)}) collective-permute-start(bf16[32,2176]{1,0:T(8,128)(2,1)S(1)} %get-tuple-element.37), channel_id=1, source_target_pairs={{0,8},{4,12},{8,0},{12,4},{1,9},{5,13},{9,1},{13,5},{2,10},{6,14},... | collective-permute-start | bytes 417800 | tf_op jit(solution)/shard_map/ppermute | solution.py:38
  8.6 2.4 %shard_map.177 = (bf16[512,2048]{1,0:T(8,128)(2,1)S(1)}, bf16[512,2048]{1,0:T(8,128)(2,1)S(1)}) custom-call(bf16[512,2048]{1,0:T(8,128)(2,1)} %bitcast.65, bf16[512,2048]{1,0:T(8,128)(2,1)} %bitcast.66, bf16[32,2048]{1,0:T(8,128)(2,1)S(1)} %get-tuple-element.35.after_hbm.own_ref), custom_call_target="tpu_custom_call" | custom-call | flops 1000 | bytes 1000 | tf_op jit(solution)/shard_map/pallas_call | solution.py:58
  10.9 0.5 collective-permute-done.in1_ref
  11.4 8.0 %collective-permute-done.1.in2_ref = bf16[32,2176]{1,0:T(8,128)(2,1)S(1)} collective-permute-done((bf16[32,2176]{1,0:T(8,128)(2,1)S(1)}, bf16[32,2176]{1,0:T(8,128)(2,1)S(1)}, u32[]{:S(2)}, u32[]{:S(2)}) %collective-permute-start.1) | collective-permute-done | bytes 139296 | tf_op jit(solution)/shard_map/ppermute | solution.py:38
  19.7 1.5 %shard_map.178 = (f32[64,128]{1,0:T(8,128)S(1)}, bf16[64,128]{1,0:T(8,128)(2,1)S(1)}) custom-call(bf16[16,2176]{1,0:T(8,128)(2,1)S(1)} %get-tuple-element.43.own_ref, bf16[32,2176]{1,0:T(8,128)(2,1)S(1)} %collective-permute-done.in1_ref, bf16[32,2176]{1,0:T(8,128)(2,1)S(1)} %collective-permute-done.1.in2_ref, ...), custom_call_target="tpu_custom_call" | custom-call | flops 1000 | bytes 1000 | tf_op jit(solution)/shard_map/pallas_call | solution.py:58
  21.2 0.5 collective-permute-start.6
  21.8 0.3 copy-done.1
  22.1 1.6 %shard_map.179 = (f32[64,1280]{1,0:T(8,128)S(1)}, f32[64,1280]{1,0:T(8,128)S(1)}) custom-call(s32[2]{0:T(128)S(1)} %pad_add_fusion.place_ref, bf16[32,2048]{1,0:T(8,128)(2,1)S(1)} %get-tuple-element.35.after_hbm.own_ref, bf16[32,2176]{1,0:T(8,128)(2,1)S(1)} %collective-permute-done.in1_ref, bf16[32,2176]{1,0:T(8,128)(2,1)S(1)} %collective-permute-done.1.in2_ref, ...), custom_call_target="tpu_custom_call" | custom-call | flops 1000 | bytes 1000 | tf_op jit(solution)/shard_map/pallas_call | solution.py:58
  23.6 2.2 %collective-permute-start.4 = (f32[64,1280]{1,0:T(8,128)S(1)}, f32[64,1280]{1,0:T(8,128)S(1)}, u32[]{:S(2)}, u32[]{:S(2)}) collective-permute-start(f32[64,1280]{1,0:T(8,128)S(1)} %get-tuple-element.49), channel_id=1, source_target_pairs={{0,4},{4,0},{8,12},{12,8},{1,5},{5,1},{9,13},{13,9},{2,6},{6,2},{1... | collective-permute-start | bytes 983048 | tf_op jit(solution)/shard_map/ppermute | solution.py:38
  25.9 1.5 %collective-permute-start.7 = (f32[64,128]{1,0:T(8,128)S(1)}, f32[64,128]{1,0:T(8,128)S(1)}, u32[]{:S(2)}, u32[]{:S(2)}) collective-permute-start(f32[64,128]{1,0:T(8,128)S(1)} %add.67.near_ref), channel_id=1, source_target_pairs={{0,2},{1,3},{2,0},{3,1},{4,6},{5,7},{6,4},{7,5},{8,10},{9,11},{10,... | collective-permute-start | bytes 98312 | tf_op jit(solution)/shard_map/ppermute | solution.py:38
  27.4 0.1 multiply_cosine_fusion.1
  27.5 2.3 %collective-permute-done.7.far_ref = f32[64,128]{1,0:T(8,128)S(1)} collective-permute-done((f32[64,128]{1,0:T(8,128)S(1)}, f32[64,128]{1,0:T(8,128)S(1)}, u32[]{:S(2)}, u32[]{:S(2)}) %collective-permute-start.7) | collective-permute-done | bytes 32800 | tf_op jit(solution)/shard_map/ppermute | solution.py:38
  29.8 0.4 shard_map.180
  30.2 0.1 collective-permute-start.8
  30.3 3.0 %collective-permute-start.9 = (bf16[16,1152]{1,0:T(8,128)(2,1)S(1)}, bf16[16,1152]{1,0:T(8,128)(2,1)S(1)}, u32[]{:S(2)}, u32[]{:S(2)}) collective-permute-start(bf16[16,1152]{1,0:T(8,128)(2,1)S(1)} %get-tuple-element.55), channel_id=1, source_target_pairs={{0,8},{4,12},{8,0},{12,4},{1,9},{5,13},{9,1},{13,5},{2,10},{6,14},... | collective-permute-start | bytes 110600 | tf_op jit(solution)/shard_map/ppermute | solution.py:38
  33.3 1.3 %collective-permute-start.10 = (bf16[16,1152]{1,0:T(8,128)(2,1)S(1)}, bf16[16,1152]{1,0:T(8,128)(2,1)S(1)}, u32[]{:S(2)}, u32[]{:S(2)}) collective-permute-start(bf16[16,1152]{1,0:T(8,128)(2,1)S(1)} %get-tuple-element.56), channel_id=1, source_target_pairs={{0,12},{4,8},{8,4},{12,0},{1,13},{5,9},{9,5},{13,1},{2,14},{6,10},... | collective-permute-start | bytes 110600 | tf_op jit(solution)/shard_map/ppermute | solution.py:38
  34.9 2.7 %collective-permute-start.5 = (f32[32,1280]{1,0:T(8,128)S(1)}, f32[32,1280]{1,0:T(8,128)S(1)}, u32[]{:S(2)}, u32[]{:S(2)}) collective-permute-start(f32[32,1280]{1,0:T(8,128)S(1)} %slice.125), channel_id=1, source_target_pairs={{0,8},{4,12},{8,0},{12,4},{1,9},{5,13},{9,1},{13,5},{2,10},{6,14},... | collective-permute-start | bytes 491528 | tf_op jit(solution)/shard_map/ppermute | solution.py:38
  37.5 1.9 %collective-permute-done.10 = bf16[16,1152]{1,0:T(8,128)(2,1)S(1)} collective-permute-done((bf16[16,1152]{1,0:T(8,128)(2,1)S(1)}, bf16[16,1152]{1,0:T(8,128)(2,1)S(1)}, u32[]{:S(2)}, u32[]{:S(2)}) %collective-permute-start.10) | collective-permute-done | bytes 36896 | tf_op jit(solution)/shard_map/ppermute | solution.py:38
  39.5 0.2 fusion.6
  39.7 6.0 %collective-permute-done.5 = f32[32,1280]{1,0:T(8,128)S(1)} collective-permute-done((f32[32,1280]{1,0:T(8,128)S(1)}, f32[32,1280]{1,0:T(8,128)S(1)}, u32[]{:S(2)}, u32[]{:S(2)}) %collective-permute-start.5) | collective-permute-done | bytes 163872 | tf_op jit(solution)/shard_map/ppermute | solution.py:38
  45.8 0.1 fusion.36
  46.0 0.1 fusion.16
  46.1 0.2 fusion.31
  46.4 0.8 select_reduce_fusion
  47.1 0.2 fusion.15
  47.4 0.4 fusion
  47.9 1.8 %collective-permute-start.13 = (bf16[32,1536]{1,0:T(8,128)(2,1)S(1)}, bf16[32,1536]{1,0:T(8,128)(2,1)S(1)}, u32[]{:S(2)}, u32[]{:S(2)}) collective-permute-start(bf16[32,1536]{1,0:T(8,128)(2,1)S(1)} %get-tuple-element.88), channel_id=1, source_target_pairs={{0,12},{4,8},{8,4},{12,0},{1,13},{5,9},{9,5},{13,1},{2,14},{6,10},... | collective-permute-start | bytes 294920 | tf_op jit(solution)/shard_map/ppermute | solution.py:38
  49.7 2.6 %collective-permute-start.12 = (bf16[32,1536]{1,0:T(8,128)(2,1)S(1)}, bf16[32,1536]{1,0:T(8,128)(2,1)S(1)}, u32[]{:S(2)}, u32[]{:S(2)}) collective-permute-start(bf16[32,1536]{1,0:T(8,128)(2,1)S(1)} %get-tuple-element.90), channel_id=1, source_target_pairs={{0,8},{4,12},{8,0},{12,4},{1,9},{5,13},{9,1},{13,5},{2,10},{6,14},... | collective-permute-start | bytes 294920 | tf_op jit(solution)/shard_map/ppermute | solution.py:38
  52.3 3.1 %collective-permute-done.13.in3_ref = bf16[32,1536]{1,0:T(8,128)(2,1)S(1)} collective-permute-done((bf16[32,1536]{1,0:T(8,128)(2,1)S(1)}, bf16[32,1536]{1,0:T(8,128)(2,1)S(1)}, u32[]{:S(2)}, u32[]{:S(2)}) %collective-permute-start.13) | collective-permute-done | bytes 98336 | tf_op jit(solution)/shard_map/ppermute | solution.py:38
  55.4 2.3 %collective-permute-done.11.in1_ref = bf16[32,1536]{1,0:T(8,128)(2,1)S(1)} collective-permute-done((bf16[32,1536]{1,0:T(8,128)(2,1)S(1)}, bf16[32,1536]{1,0:T(8,128)(2,1)S(1)}, u32[]{:S(2)}, u32[]{:S(2)}) %collective-permute-start.11) | collective-permute-done | bytes 98336 | tf_op jit(solution)/shard_map/ppermute | solution.py:38
  57.8 0.8 collective-permute-done.12.in2_ref
  58.5 1.3 %shard_map.181 = (f32[64,2048]{1,0:T(8,128)S(1)}, f32[64,2048]{1,0:T(8,128)S(1)}) custom-call(s32[2]{0:T(128)S(1)} %pad_add_fusion.place_ref, bf16[32,1536]{1,0:T(8,128)(2,1)S(1)} %get-tuple-element.91.own_ref, bf16[32,1536]{1,0:T(8,128)(2,1)S(1)} %collective-permute-done.11.in1_ref, bf16[32,1536]{1,0:T(8,128)(2,1)S(1)} %collective-permute-done.12.in2_ref, ...), custom_call_target="tpu_custom_call" | custom-call | flops 1000 | bytes 1000 | tf_op jit(solution)/shard_map/pallas_call | solution.py:58
  59.9 1.9 %collective-permute-done.14 = f32[64,2048]{1,0:T(8,128)S(1)} collective-permute-done((f32[64,2048]{1,0:T(8,128)S(1)}, f32[64,2048]{1,0:T(8,128)S(1)}, u32[]{:S(2)}, u32[]{:S(2)}) %collective-permute-start.14) | collective-permute-done | bytes 524320 | tf_op jit(solution)/shard_map/ppermute | solution.py:38
  61.9 0.1 abs_reduce_fusion
  62.0 0.1 multiply_convert_fusion
  62.2 1.6 %collective-permute-start.15 = (f16[32,2176]{1,0:T(8,128)(2,1)S(1)}, f16[32,2176]{1,0:T(8,128)(2,1)S(1)}, u32[]{:S(2)}, u32[]{:S(2)}) collective-permute-start(f16[32,2176]{1,0:T(8,128)(2,1)S(1)} %pad_maximum_fusion.3), channel_id=1, source_target_pairs={{0,2},{1,3},{2,0},{3,1},{4,6},{5,7},{6,4},{7,5},{8,10},{9,11},{10,... | collective-permute-start | bytes 417800 | tf_op jit(solution)/shard_map/ppermute | solution.py:38
  63.9 4.1 %collective-permute-done.15 = f16[32,2176]{1,0:T(8,128)(2,1)S(1)} collective-permute-done((f16[32,2176]{1,0:T(8,128)(2,1)S(1)}, f16[32,2176]{1,0:T(8,128)(2,1)S(1)}, u32[]{:S(2)}, u32[]{:S(2)}) %collective-permute-start.15) | collective-permute-done | bytes 139296 | tf_op jit(solution)/shard_map/ppermute | solution.py:38
  68.0 0.1 convert_reduce_fusion
  68.1 0.2 multiply_reduce_fusion
  68.4 1.6 %collective-permute-start.20 = (f32[32]{0:T(128)S(1)}, f32[32]{0:T(128)S(1)}, u32[]{:S(2)}, u32[]{:S(2)}) collective-permute-start(f32[32]{0:T(128)S(1)} %get-tuple-element.74), channel_id=1, source_target_pairs={{0,12},{4,8},{8,4},{12,0},{1,13},{5,9},{9,5},{13,1},{2,14},{6,10},... | collective-permute-start | bytes 392 | tf_op jit(solution)/shard_map/ppermute | solution.py:38
  70.0 0.4 collective-permute-start.19
  70.4 2.4 %collective-permute-start.18 = (f32[32]{0:T(128)S(1)}, f32[32]{0:T(128)S(1)}, u32[]{:S(2)}, u32[]{:S(2)}) collective-permute-start(f32[32]{0:T(128)S(1)} %get-tuple-element.74), channel_id=1, source_target_pairs={{0,4},{4,0},{8,12},{12,8},{1,5},{5,1},{9,13},{13,9},{2,6},{6,2},{1... | collective-permute-start | bytes 392 | tf_op jit(solution)/shard_map/ppermute | solution.py:38
  72.8 1.6 %collective-permute-start.16 = (bf16[32,2048]{1,0:T(8,128)(2,1)S(1)}, bf16[32,2048]{1,0:T(8,128)(2,1)S(1)}, u32[]{:S(2)}, u32[]{:S(2)}) collective-permute-start(bf16[32,2048]{1,0:T(8,128)(2,1)S(1)} %get-tuple-element.75.own_ref), channel_id=1, source_target_pairs={{0,2},{1,3},{2,0},{3,1},{4,6},{5,7},{6,4},{7,5},{8,10},{9,11},{10,... | collective-permute-start | bytes 393224 | tf_op jit(solution)/shard_map/ppermute | solution.py:38
  74.4 1.6 %collective-permute-start.21 = (f32[1,32]{1,0:T(1,128)S(1)}, f32[1,32]{1,0:T(1,128)S(1)}, u32[]{:S(2)}, u32[]{:S(2)}) collective-permute-start(f32[1,32]{1,0:T(1,128)S(1)} %rsqrt_bitcast_fusion), channel_id=1, source_target_pairs={{0,2},{1,3},{2,0},{3,1},{4,6},{5,7},{6,4},{7,5},{8,10},{9,11},{10,... | collective-permute-start | bytes 392 | tf_op jit(solution)/shard_map/ppermute | solution.py:38
  76.1 1.7 %collective-permute-done.16.across_ref = bf16[32,2048]{1,0:T(8,128)(2,1)S(1)} collective-permute-done((bf16[32,2048]{1,0:T(8,128)(2,1)S(1)}, bf16[32,2048]{1,0:T(8,128)(2,1)S(1)}, u32[]{:S(2)}, u32[]{:S(2)}) %collective-permute-start.16) | collective-permute-done | bytes 131104 | tf_op jit(solution)/shard_map/ppermute | solution.py:38
  77.9 0.2 collective-permute-done.21
  78.1 0.4 collective-permute-start.22
  78.5 0.2 multiply_reduce_fusion.2
  78.7 0.8 collective-permute-done.22
  79.5 2.0 %shard_map.182 = (f32[64,2048]{1,0:T(8,128)S(1)}, f32[64,2048]{1,0:T(8,128)S(1)}) custom-call(s32[2]{0:T(128)S(1)} %pad_add_fusion.place_ref, bf16[32,2048]{1,0:T(8,128)(2,1)S(1)} %get-tuple-element.75.own_ref, bf16[32,2048]{1,0:T(8,128)(2,1)S(1)} %collective-permute-done.16.across_ref, bf16[64,2048]{1,0:T(8,128)(2,1)S(1)} %collective-permute-done.17.pair_ref, ...), custom_call_target="tpu_custom_call" | custom-call | flops 1000 | bytes 1000 | tf_op jit(solution)/shard_map/pallas_call | solution.py:58
  81.6 1.8 %collective-permute-start.23 = (f16[64,2048]{1,0:T(8,128)(2,1)S(1)}, f16[64,2048]{1,0:T(8,128)(2,1)S(1)}, u32[]{:S(2)}, u32[]{:S(2)}) collective-permute-start(f16[64,2048]{1,0:T(8,128)(2,1)S(1)} %convert_element_type.104), channel_id=1, source_target_pairs={{0,4},{4,0},{8,12},{12,8},{1,5},{5,1},{9,13},{13,9},{2,6},{6,2},{1... | collective-permute-start | bytes 786440 | tf_op jit(solution)/shard_map/ppermute | solution.py:38
  83.3 2.0 %shard_map.183 = (f32[64,2048]{1,0:T(8,128)S(1)}, f32[64,2048]{1,0:T(8,128)S(1)}) custom-call(s32[2]{0:T(128)S(1)} %pad_add_fusion.place_ref, bf16[32,2048]{1,0:T(8,128)(2,1)S(1)} %get-tuple-element.75.own_ref, bf16[32,2048]{1,0:T(8,128)(2,1)S(1)} %collective-permute-done.16.across_ref, bf16[64,2048]{1,0:T(8,128)(2,1)S(1)} %collective-permute-done.17.pair_ref, ...), custom_call_target="tpu_custom_call" | custom-call | flops 1000 | bytes 1000 | tf_op jit(solution)/shard_map/pallas_call | solution.py:58
  85.4 1.0 collective-permute-start.26
  86.5 1.2 %collective-permute-start.25 = (f16[32,2048]{1,0:T(8,128)(2,1)S(1)}, f16[32,2048]{1,0:T(8,128)(2,1)S(1)}, u32[]{:S(2)}, u32[]{:S(2)}) collective-permute-start(f16[32,2048]{1,0:T(8,128)(2,1)S(1)} %get-tuple-element.78), channel_id=1, source_target_pairs={{0,4},{4,0},{8,12},{12,8},{1,5},{5,1},{9,13},{13,9},{2,6},{6,2},{1... | collective-permute-start | bytes 393224 | tf_op jit(solution)/shard_map/ppermute | solution.py:38
  87.7 2.3 %collective-permute-start.27 = (f16[32,2048]{1,0:T(8,128)(2,1)S(1)}, f16[32,2048]{1,0:T(8,128)(2,1)S(1)}, u32[]{:S(2)}, u32[]{:S(2)}) collective-permute-start(f16[32,2048]{1,0:T(8,128)(2,1)S(1)} %get-tuple-element.79), channel_id=1, source_target_pairs={{0,12},{4,8},{8,4},{12,0},{1,13},{5,9},{9,5},{13,1},{2,14},{6,10},... | collective-permute-start | bytes 393224 | tf_op jit(solution)/shard_map/ppermute | solution.py:38
  90.0 2.9 %collective-permute-done.23 = f16[64,2048]{1,0:T(8,128)(2,1)S(1)} collective-permute-done((f16[64,2048]{1,0:T(8,128)(2,1)S(1)}, f16[64,2048]{1,0:T(8,128)(2,1)S(1)}, u32[]{:S(2)}, u32[]{:S(2)}) %collective-permute-start.23) | collective-permute-done | bytes 262176 | tf_op jit(solution)/shard_map/ppermute | solution.py:38
  93.0 0.6 collective-permute-start.24
  93.6 2.0 %collective-permute-done.26 = f16[32,2048]{1,0:T(8,128)(2,1)S(1)} collective-permute-done((f16[32,2048]{1,0:T(8,128)(2,1)S(1)}, f16[32,2048]{1,0:T(8,128)(2,1)S(1)}, u32[]{:S(2)}, u32[]{:S(2)}) %collective-permute-start.26) | collective-permute-done | bytes 131104 | tf_op jit(solution)/shard_map/ppermute | solution.py:38
  95.6 0.1 collective-permute-done.25
  95.7 4.9 %collective-permute-done.27 = f16[32,2048]{1,0:T(8,128)(2,1)S(1)} collective-permute-done((f16[32,2048]{1,0:T(8,128)(2,1)S(1)}, f16[32,2048]{1,0:T(8,128)(2,1)S(1)}, u32[]{:S(2)}, u32[]{:S(2)}) %collective-permute-start.27) | collective-permute-done | bytes 131104 | tf_op jit(solution)/shard_map/ppermute | solution.py:38
  100.7 5.1 %collective-permute-done.24 = f16[32,2048]{1,0:T(8,128)(2,1)S(1)} collective-permute-done((f16[32,2048]{1,0:T(8,128)(2,1)S(1)}, f16[32,2048]{1,0:T(8,128)(2,1)S(1)}, u32[]{:S(2)}, u32[]{:S(2)}) %collective-permute-start.24) | collective-permute-done | bytes 131104 | tf_op jit(solution)/shard_map/ppermute | solution.py:38
  105.9 1.2 %copy.20 = f32[32,2,2048]{2,1,0:T(2,128)} copy(f32[32,2,2048]{2,0,1:T(8,128)S(1)} %pad_maximum_fusion) | data formatting | bytes 1048576
  (81 shorter events, 1.6 us)
Async XLA Ops:
  0.6 45.7 %copy-start = (bf16[32,1,128,128]{3,2,1,0:T(8,128)(2,1)S(1)}, bf16[32,1,128,128]{3,2,1,0:T(8,128)(2,1)}, u32[]{:S(2)}) copy-start(bf16[32,1,128,128]{3,2,1,0:T(8,128)(2,1)} %param.26) | copy-start | bytes 3145732
  2.9 8.5 %collective-permute-start = (bf16[32,2176]{1,0:T(8,128)(2,1)S(1)}, bf16[32,2176]{1,0:T(8,128)(2,1)S(1)}, u32[]{:S(2)}, u32[]{:S(2)}) collective-permute-start(bf16[32,2176]{1,0:T(8,128)(2,1)S(1)} %get-tuple-element.36), channel_id=1, source_target_pairs={{0,4},{4,0},{8,12},{12,8},{1,5},{5,1},{9,13},{13,9},{2,6},{6,2},{1... | collective-permute-start | bytes 417800 | tf_op jit(solution)/shard_map/ppermute | solution.py:38
  6.0 13.5 %collective-permute-start.1 = (bf16[32,2176]{1,0:T(8,128)(2,1)S(1)}, bf16[32,2176]{1,0:T(8,128)(2,1)S(1)}, u32[]{:S(2)}, u32[]{:S(2)}) collective-permute-start(bf16[32,2176]{1,0:T(8,128)(2,1)S(1)} %get-tuple-element.37), channel_id=1, source_target_pairs={{0,8},{4,12},{8,0},{12,4},{1,9},{5,13},{9,1},{13,5},{2,10},{6,14},... | collective-permute-start | bytes 417800 | tf_op jit(solution)/shard_map/ppermute | solution.py:38
  8.6 10.9 %collective-permute-start.2 = (bf16[32,2176]{1,0:T(8,128)(2,1)S(1)}, bf16[32,2176]{1,0:T(8,128)(2,1)S(1)}, u32[]{:S(2)}, u32[]{:S(2)}) collective-permute-start(bf16[32,2176]{1,0:T(8,128)(2,1)S(1)} %get-tuple-element.38), channel_id=1, source_target_pairs={{0,12},{4,8},{8,4},{12,0},{1,13},{5,9},{9,5},{13,1},{2,14},{6,10},... | collective-permute-start | bytes 417800 | tf_op jit(solution)/shard_map/ppermute | solution.py:38
  8.6 70.9 %slice-start = ((s8[16777216]{0:T(1024)(128)(4,1)}), s8[4194304]{0:T(1024)(128)(4,1)S(1)}, s32[]{:S(2)}) async-start(s8[16777216]{0:T(1024)(128)(4,1)} %bitcast.61), calls=%async_computation | async-start | bytes 8388608
  19.5 2.3 %copy-start.6 = (bf16[2048,128]{1,0:T(8,128)(2,1)S(1)}, bf16[2048,128]{1,0:T(8,128)(2,1)}, u32[]{:S(2)}) copy-start(bf16[2048,128]{1,0:T(8,128)(2,1)} %value_ref.1) | copy-start | bytes 1572868
  19.5 1.7 %collective-permute-start.3 = (bf16[48,2048]{1,0:T(8,128)(2,1)S(1)}, bf16[48,2048]{1,0:T(8,128)(2,1)S(1)}, u32[]{:S(2)}, u32[]{:S(2)}) collective-permute-start(bf16[48,2048]{1,0:T(8,128)(2,1)S(1)} %pad_maximum_fusion.2), channel_id=1, source_target_pairs={{0,1},{1,0},{2,3},{3,2},{4,5},{5,4},{6,7},{7,6},{8,9},{9,8},{10,11... | collective-permute-start | bytes 589832 | tf_op jit(solution)/shard_map/ppermute | solution.py:38
  19.6 2.2 %copy-start.8 = (s32[32]{0:T(128)S(1)}, s32[32]{0:T(128)}, u32[]{:S(2)}) copy-start(s32[32]{0:T(128)} %param.29) | copy-start | bytes 388
  19.6 2.2 %copy-start.5 = (bf16[2048,128]{1,0:T(8,128)(2,1)S(1)}, bf16[2048,128]{1,0:T(8,128)(2,1)}, u32[]{:S(2)}) copy-start(bf16[2048,128]{1,0:T(8,128)(2,1)} %key_ref.1) | copy-start | bytes 1572868
  19.7 2.4 %copy-start.1 = (bf16[2048,1024]{1,0:T(8,128)(2,1)S(1)}, bf16[2048,1024]{1,0:T(8,128)(2,1)}, u32[]{:S(2)}) copy-start(bf16[2048,1024]{1,0:T(8,128)(2,1)} %query_ref.1) | copy-start | bytes 12582916
  19.7 59.8 %slice-start.1 = ((s8[16777216]{0:T(1024)(128)(4,1)}), s8[4194304]{0:T(1024)(128)(4,1)S(1)}, s32[]{:S(2)}) async-start(s8[16777216]{0:T(1024)(128)(4,1)} %bitcast.61), calls=%async_computation.1 | async-start | bytes 8388608
  21.2 4.6 %collective-permute-start.6 = (f32[64,128]{1,0:T(8,128)S(1)}, f32[64,128]{1,0:T(8,128)S(1)}, u32[]{:S(2)}, u32[]{:S(2)}) collective-permute-start(f32[64,128]{1,0:T(8,128)S(1)} %get-tuple-element.51), channel_id=1, source_target_pairs={{0,1},{1,0},{2,3},{3,2},{4,5},{5,4},{6,7},{7,6},{8,9},{9,8},{10,11... | collective-permute-start | bytes 98312 | tf_op jit(solution)/shard_map/ppermute | solution.py:38
  22.1 7.8 %copy-start.4 = (bf16[8,64,1024]{2,1,0:T(8,128)(2,1)S(1)}, bf16[8,64,1024]{2,1,0:T(8,128)(2,1)}, u32[]{:S(2)}) copy-start(bf16[8,64,1024]{2,1,0:T(8,128)(2,1)} %param.23) | copy-start | bytes 3145732
  22.1 7.8 %copy-start.7 = (bf16[8,64,128]{2,1,0:T(8,128)(2,1)S(1)}, bf16[8,64,128]{2,1,0:T(8,128)(2,1)}, u32[]{:S(2)}) copy-start(bf16[8,64,128]{2,1,0:T(8,128)(2,1)} %param.25) | copy-start | bytes 393220
  22.1 25.3 %copy-start.9 = (bf16[32,1,128,128]{3,2,1,0:T(8,128)(2,1)S(1)}, bf16[32,1,128,128]{3,2,1,0:T(8,128)(2,1)}, u32[]{:S(2)}) copy-start(bf16[32,1,128,128]{3,2,1,0:T(8,128)(2,1)} %param.27) | copy-start | bytes 3145732
  23.6 11.2 %collective-permute-start.4 = (f32[64,1280]{1,0:T(8,128)S(1)}, f32[64,1280]{1,0:T(8,128)S(1)}, u32[]{:S(2)}, u32[]{:S(2)}) collective-permute-start(f32[64,1280]{1,0:T(8,128)S(1)} %get-tuple-element.49), channel_id=1, source_target_pairs={{0,4},{4,0},{8,12},{12,8},{1,5},{5,1},{9,13},{13,9},{2,6},{6,2},{1... | collective-permute-start | bytes 983048 | tf_op jit(solution)/shard_map/ppermute | solution.py:38
  25.9 4.0 %collective-permute-start.7 = (f32[64,128]{1,0:T(8,128)S(1)}, f32[64,128]{1,0:T(8,128)S(1)}, u32[]{:S(2)}, u32[]{:S(2)}) collective-permute-start(f32[64,128]{1,0:T(8,128)S(1)} %add.67.near_ref), channel_id=1, source_target_pairs={{0,2},{1,3},{2,0},{3,1},{4,6},{5,7},{6,4},{7,5},{8,10},{9,11},{10,... | collective-permute-start | bytes 98312 | tf_op jit(solution)/shard_map/ppermute | solution.py:38
  29.8 49.6 %slice-start.2 = ((s8[16777216]{0:T(1024)(128)(4,1)}), s8[4194304]{0:T(1024)(128)(4,1)S(1)}, s32[]{:S(2)}) async-start(s8[16777216]{0:T(1024)(128)(4,1)} %bitcast.61), calls=%async_computation.2 | async-start | bytes 8388608
  30.2 7.3 %collective-permute-start.8 = (bf16[16,1152]{1,0:T(8,128)(2,1)S(1)}, bf16[16,1152]{1,0:T(8,128)(2,1)S(1)}, u32[]{:S(2)}, u32[]{:S(2)}) collective-permute-start(bf16[16,1152]{1,0:T(8,128)(2,1)S(1)} %get-tuple-element.54), channel_id=1, source_target_pairs={{0,4},{4,0},{8,12},{12,8},{1,5},{5,1},{9,13},{13,9},{2,6},{6,2},{1... | collective-permute-start | bytes 110600 | tf_op jit(solution)/shard_map/ppermute | solution.py:38
  30.3 7.2 %collective-permute-start.9 = (bf16[16,1152]{1,0:T(8,128)(2,1)S(1)}, bf16[16,1152]{1,0:T(8,128)(2,1)S(1)}, u32[]{:S(2)}, u32[]{:S(2)}) collective-permute-start(bf16[16,1152]{1,0:T(8,128)(2,1)S(1)} %get-tuple-element.55), channel_id=1, source_target_pairs={{0,8},{4,12},{8,0},{12,4},{1,9},{5,13},{9,1},{13,5},{2,10},{6,14},... | collective-permute-start | bytes 110600 | tf_op jit(solution)/shard_map/ppermute | solution.py:38
  33.3 6.1 %collective-permute-start.10 = (bf16[16,1152]{1,0:T(8,128)(2,1)S(1)}, bf16[16,1152]{1,0:T(8,128)(2,1)S(1)}, u32[]{:S(2)}, u32[]{:S(2)}) collective-permute-start(bf16[16,1152]{1,0:T(8,128)(2,1)S(1)} %get-tuple-element.56), channel_id=1, source_target_pairs={{0,12},{4,8},{8,4},{12,0},{1,13},{5,9},{9,5},{13,1},{2,14},{6,10},... | collective-permute-start | bytes 110600 | tf_op jit(solution)/shard_map/ppermute | solution.py:38
  34.9 10.8 %collective-permute-start.5 = (f32[32,1280]{1,0:T(8,128)S(1)}, f32[32,1280]{1,0:T(8,128)S(1)}, u32[]{:S(2)}, u32[]{:S(2)}) collective-permute-start(f32[32,1280]{1,0:T(8,128)S(1)} %slice.125), channel_id=1, source_target_pairs={{0,8},{4,12},{8,0},{12,4},{1,9},{5,13},{9,1},{13,5},{2,10},{6,14},... | collective-permute-start | bytes 491528 | tf_op jit(solution)/shard_map/ppermute | solution.py:38
  46.0 12.5 %copy-start.2 = (bf16[1024,2048]{1,0:T(8,128)(2,1)S(1)}, bf16[1024,2048]{1,0:T(8,128)(2,1)}, u32[]{:S(2)}) copy-start(bf16[1024,2048]{1,0:T(8,128)(2,1)} %weight_ref.3) | copy-start | bytes 12582916
  47.8 31.6 %slice-start.3 = ((s8[16777216]{0:T(1024)(128)(4,1)}), s8[4194304]{0:T(1024)(128)(4,1)S(1)}, s32[]{:S(2)}) async-start(s8[16777216]{0:T(1024)(128)(4,1)} %bitcast.61), calls=%async_computation.3 | async-start | bytes 8388608
  47.9 7.6 %collective-permute-start.13 = (bf16[32,1536]{1,0:T(8,128)(2,1)S(1)}, bf16[32,1536]{1,0:T(8,128)(2,1)S(1)}, u32[]{:S(2)}, u32[]{:S(2)}) collective-permute-start(bf16[32,1536]{1,0:T(8,128)(2,1)S(1)} %get-tuple-element.88), channel_id=1, source_target_pairs={{0,12},{4,8},{8,4},{12,0},{1,13},{5,9},{9,5},{13,1},{2,14},{6,10},... | collective-permute-start | bytes 294920 | tf_op jit(solution)/shard_map/ppermute | solution.py:38
  49.7 8.0 %collective-permute-start.11 = (bf16[32,1536]{1,0:T(8,128)(2,1)S(1)}, bf16[32,1536]{1,0:T(8,128)(2,1)S(1)}, u32[]{:S(2)}, u32[]{:S(2)}) collective-permute-start(bf16[32,1536]{1,0:T(8,128)(2,1)S(1)} %get-tuple-element.89), channel_id=1, source_target_pairs={{0,4},{4,0},{8,12},{12,8},{1,5},{5,1},{9,13},{13,9},{2,6},{6,2},{1... | collective-permute-start | bytes 294920 | tf_op jit(solution)/shard_map/ppermute | solution.py:38
  49.7 8.8 %collective-permute-start.12 = (bf16[32,1536]{1,0:T(8,128)(2,1)S(1)}, bf16[32,1536]{1,0:T(8,128)(2,1)S(1)}, u32[]{:S(2)}, u32[]{:S(2)}) collective-permute-start(bf16[32,1536]{1,0:T(8,128)(2,1)S(1)} %get-tuple-element.90), channel_id=1, source_target_pairs={{0,8},{4,12},{8,0},{12,4},{1,9},{5,13},{9,1},{13,5},{2,10},{6,14},... | collective-permute-start | bytes 294920 | tf_op jit(solution)/shard_map/ppermute | solution.py:38
  59.8 2.0 %collective-permute-start.14 = (f32[64,2048]{1,0:T(8,128)S(1)}, f32[64,2048]{1,0:T(8,128)S(1)}, u32[]{:S(2)}, u32[]{:S(2)}) collective-permute-start(f32[64,2048]{1,0:T(8,128)S(1)} %get-tuple-element.59), channel_id=1, source_target_pairs={{0,1},{1,0},{2,3},{3,2},{4,5},{5,4},{6,7},{7,6},{8,9},{9,8},{10,11... | collective-permute-start | bytes 1572872 | tf_op jit(solution)/shard_map/ppermute | solution.py:38
  62.2 5.8 %collective-permute-start.15 = (f16[32,2176]{1,0:T(8,128)(2,1)S(1)}, f16[32,2176]{1,0:T(8,128)(2,1)S(1)}, u32[]{:S(2)}, u32[]{:S(2)}) collective-permute-start(f16[32,2176]{1,0:T(8,128)(2,1)S(1)} %pad_maximum_fusion.3), channel_id=1, source_target_pairs={{0,2},{1,3},{2,0},{3,1},{4,6},{5,7},{6,4},{7,5},{8,10},{9,11},{10,... | collective-permute-start | bytes 417800 | tf_op jit(solution)/shard_map/ppermute | solution.py:38
  68.4 15.0 %copy-start.3 = (bf16[32,2048]{1,0:T(8,128)(2,1)}, bf16[32,2048]{1,0:T(8,128)(2,1)S(1)}, u32[]{:S(2)}) copy-start(bf16[32,2048]{1,0:T(8,128)(2,1)S(1)} %get-tuple-element.75.own_ref) | copy-start | bytes 393220
  68.4 6.0 %collective-permute-start.20 = (f32[32]{0:T(128)S(1)}, f32[32]{0:T(128)S(1)}, u32[]{:S(2)}, u32[]{:S(2)}) collective-permute-start(f32[32]{0:T(128)S(1)} %get-tuple-element.74), channel_id=1, source_target_pairs={{0,12},{4,8},{8,4},{12,0},{1,13},{5,9},{9,5},{13,1},{2,14},{6,10},... | collective-permute-start | bytes 392 | tf_op jit(solution)/shard_map/ppermute | solution.py:38
  70.0 4.4 %collective-permute-start.19 = (f32[32]{0:T(128)S(1)}, f32[32]{0:T(128)S(1)}, u32[]{:S(2)}, u32[]{:S(2)}) collective-permute-start(f32[32]{0:T(128)S(1)} %get-tuple-element.74), channel_id=1, source_target_pairs={{0,8},{4,12},{8,0},{12,4},{1,9},{5,13},{9,1},{13,5},{2,10},{6,14},... | collective-permute-start | bytes 392 | tf_op jit(solution)/shard_map/ppermute | solution.py:38
  70.4 4.0 %collective-permute-start.18 = (f32[32]{0:T(128)S(1)}, f32[32]{0:T(128)S(1)}, u32[]{:S(2)}, u32[]{:S(2)}) collective-permute-start(f32[32]{0:T(128)S(1)} %get-tuple-element.74), channel_id=1, source_target_pairs={{0,4},{4,0},{8,12},{12,8},{1,5},{5,1},{9,13},{13,9},{2,6},{6,2},{1... | collective-permute-start | bytes 392 | tf_op jit(solution)/shard_map/ppermute | solution.py:38
  72.8 5.0 %collective-permute-start.16 = (bf16[32,2048]{1,0:T(8,128)(2,1)S(1)}, bf16[32,2048]{1,0:T(8,128)(2,1)S(1)}, u32[]{:S(2)}, u32[]{:S(2)}) collective-permute-start(bf16[32,2048]{1,0:T(8,128)(2,1)S(1)} %get-tuple-element.75.own_ref), channel_id=1, source_target_pairs={{0,2},{1,3},{2,0},{3,1},{4,6},{5,7},{6,4},{7,5},{8,10},{9,11},{10,... | collective-permute-start | bytes 393224 | tf_op jit(solution)/shard_map/ppermute | solution.py:38
  74.4 3.6 %collective-permute-start.21 = (f32[1,32]{1,0:T(1,128)S(1)}, f32[1,32]{1,0:T(1,128)S(1)}, u32[]{:S(2)}, u32[]{:S(2)}) collective-permute-start(f32[1,32]{1,0:T(1,128)S(1)} %rsqrt_bitcast_fusion), channel_id=1, source_target_pairs={{0,2},{1,3},{2,0},{3,1},{4,6},{5,7},{6,4},{7,5},{8,10},{9,11},{10,... | collective-permute-start | bytes 392 | tf_op jit(solution)/shard_map/ppermute | solution.py:38
  77.8 1.6 %collective-permute-start.17 = (bf16[64,2048]{1,0:T(8,128)(2,1)S(1)}, bf16[64,2048]{1,0:T(8,128)(2,1)S(1)}, u32[]{:S(2)}, u32[]{:S(2)}) collective-permute-start(bf16[64,2048]{1,0:T(8,128)(2,1)S(1)} %pad_maximum_fusion.1), channel_id=1, source_target_pairs={{0,1},{1,0},{2,3},{3,2},{4,5},{5,4},{6,7},{7,6},{8,9},{9,8},{10,11... | collective-permute-start | bytes 786440 | tf_op jit(solution)/shard_map/ppermute | solution.py:38
  78.1 1.4 %collective-permute-start.22 = (f32[2,32]{1,0:T(2,128)S(1)}, f32[2,32]{1,0:T(2,128)S(1)}, u32[]{:S(2)}, u32[]{:S(2)}) collective-permute-start(f32[2,32]{1,0:T(2,128)S(1)} %pad_maximum_fusion.12), channel_id=1, source_target_pairs={{0,1},{1,0},{2,3},{3,2},{4,5},{5,4},{6,7},{7,6},{8,9},{9,8},{10,11... | collective-permute-start | bytes 776 | tf_op jit(solution)/shard_map/ppermute | solution.py:38
  81.6 11.3 %collective-permute-start.23 = (f16[64,2048]{1,0:T(8,128)(2,1)S(1)}, f16[64,2048]{1,0:T(8,128)(2,1)S(1)}, u32[]{:S(2)}, u32[]{:S(2)}) collective-permute-start(f16[64,2048]{1,0:T(8,128)(2,1)S(1)} %convert_element_type.104), channel_id=1, source_target_pairs={{0,4},{4,0},{8,12},{12,8},{1,5},{5,1},{9,13},{13,9},{2,6},{6,2},{1... | collective-permute-start | bytes 786440 | tf_op jit(solution)/shard_map/ppermute | solution.py:38
  85.4 10.1 %collective-permute-start.26 = (f16[32,2048]{1,0:T(8,128)(2,1)S(1)}, f16[32,2048]{1,0:T(8,128)(2,1)S(1)}, u32[]{:S(2)}, u32[]{:S(2)}) collective-permute-start(f16[32,2048]{1,0:T(8,128)(2,1)S(1)} %slice_convert_fusion), channel_id=1, source_target_pairs={{0,8},{4,12},{8,0},{12,4},{1,9},{5,13},{9,1},{13,5},{2,10},{6,14},... | collective-permute-start | bytes 393224 | tf_op jit(solution)/shard_map/ppermute | solution.py:38
  86.5 9.2 %collective-permute-start.25 = (f16[32,2048]{1,0:T(8,128)(2,1)S(1)}, f16[32,2048]{1,0:T(8,128)(2,1)S(1)}, u32[]{:S(2)}, u32[]{:S(2)}) collective-permute-start(f16[32,2048]{1,0:T(8,128)(2,1)S(1)} %get-tuple-element.78), channel_id=1, source_target_pairs={{0,4},{4,0},{8,12},{12,8},{1,5},{5,1},{9,13},{13,9},{2,6},{6,2},{1... | collective-permute-start | bytes 393224 | tf_op jit(solution)/shard_map/ppermute | solution.py:38
  87.7 12.9 %collective-permute-start.27 = (f16[32,2048]{1,0:T(8,128)(2,1)S(1)}, f16[32,2048]{1,0:T(8,128)(2,1)S(1)}, u32[]{:S(2)}, u32[]{:S(2)}) collective-permute-start(f16[32,2048]{1,0:T(8,128)(2,1)S(1)} %get-tuple-element.79), channel_id=1, source_target_pairs={{0,12},{4,8},{8,4},{12,0},{1,13},{5,9},{9,5},{13,1},{2,14},{6,10},... | collective-permute-start | bytes 393224 | tf_op jit(solution)/shard_map/ppermute | solution.py:38
  93.0 12.8 %collective-permute-start.24 = (f16[32,2048]{1,0:T(8,128)(2,1)S(1)}, f16[32,2048]{1,0:T(8,128)(2,1)S(1)}, u32[]{:S(2)}, u32[]{:S(2)}) collective-permute-start(f16[32,2048]{1,0:T(8,128)(2,1)S(1)} %slice_convert_fusion.1), channel_id=1, source_target_pairs={{0,8},{4,12},{8,0},{12,4},{1,9},{5,13},{9,1},{13,5},{2,10},{6,14},... | collective-permute-start | bytes 393224 | tf_op jit(solution)/shard_map/ppermute | solution.py:38

commit v5 on v4

--- a/solution.py
+++ b/solution.py
@@ -304,6 +304,35 @@
     send_ref[streams:] = out[3 * streams :]
 
 
+LEVELS = 30719.0
+LEVEL_STEP = 16416.0 / LEVELS
+
+
+def row_root(values):
+    largest = jnp.max(jnp.abs(values), axis=1, keepdims=True)
+    root = jnp.sqrt(16384.0 / jnp.maximum(largest, 1e-30))
+    return lax.reduce_precision(jnp.minimum(root, 65504.0), 5, 10)
+
+
+def encode(values, root):
+    scaled = values * (root * root) * (1.0 / LEVEL_STEP)
+    place = (jnp.round(jnp.abs(scaled)) + 1024.0) * (1.0 / 1024.0)
+    power = jnp.floor(place)
+    size = (1.0 + (place - power)) * jnp.exp2(power - 15.0)
+    code = jnp.where(scaled < 0, -size, size).astype(jnp.float16)
+    root = jnp.broadcast_to(root.astype(jnp.float16), (values.shape[0], 128))
+    return jnp.concatenate([code, root], axis=1)
+
+
+def decode(coded, width):
+    code = coded[:, :width].astype(jnp.float32)
+    root = coded[:, width : width + 1].astype(jnp.float32)
+    size = jnp.abs(code)
+    power = jnp.floor(jnp.log2(size))
+    steps = jnp.round((power + 14.0 + (size * jnp.exp2(-power) - 1.0)) * 1024.0)
+    return jnp.where(code < 0, -steps, steps) * (LEVEL_STEP / (root * root))
+
+
 def per_device_four(
     tokens,
     attention_gain,
@@ -473,13 +502,9 @@
         resident=[output_weight],
     )
     pair = kept + swap(sent, "tensor", 1)
-    leaving = pair[str_dev:]
-    largest = jnp.max(jnp.abs(leaving), axis=1, keepdims=True)
-    row_scale = jnp.minimum(16384.0 / jnp.maximum(largest, 1e-30), 32768.0).astype(jnp.float16)
-    coded = (leaving * row_scale.astype(jnp.float32)).astype(jnp.float16)
-    coded = jnp.concatenate([coded, jnp.broadcast_to(row_scale, (str_dev, 128))], axis=1)
-    coded = swap(coded, "tensor", 2)
-    arrived = coded[:, :d_slice].astype(jnp.float32) / coded[:, d_slice : d_slice + 1].astype(jnp.float32)
+    pair_scale = row_root(pair[str_dev:])
+    coded = swap(encode(pair[str_dev:], pair_scale), "tensor", 2)
+    arrived = decode(coded, d_slice)
     summed_out = pair[:str_dev] + arrived
     hidden_out = summed_out.astype(jnp.bfloat16)
 

time: 107 us -> 108 us (level)
  no operation moved by 1% of the time
where the time goes in v5:
time: 108 us; the launch traced here: 107 us
  waiting for transfers between devices  48.7 us (45%)
  starting transfers between devices  38.4 us (36%)
  Pallas kernels  13.3 us (12%)
  other arithmetic  2.54 us (2%)
  local copies, waits for them, and re-layouts  1.74 us (2%)
  matrix products  1.62 us (2%)
  between operations  1.1 us (1%)
    ppermute x28, waiting for transfers between devices, swap(): return lax.ppermute(value, axis, [(i, i ^ distance) for i in range(size)])  48.7 us
    ppermute x28, starting transfers between devices, swap(): return lax.ppermute(value, axis, [(i, i ^ distance) for i in range(size)])  38.4 us
    pallas_call x8, Pallas kernels, call(): pl.pallas_call(kernel, out_shape=tuple(outs), in_specs=specs, out_specs=t...  13.3 us
  transfers between devices with their start and end apart: 28, of which 18 were waited for; matrix products, arithmetic and copies ran while one was open for 1% of the time, Pallas kernels for 7%

profile of v5, /device:TPU:0, one launch (start us, length us, event | category | flops | bytes accessed | tf_op | source)
XLA Modules:
  0.0 107.4 jit_solution(2346986667208718820)
XLA Ops:
  0.7 2.2 %shard_map.176 = (bf16[32,2048]{1,0:T(8,128)(2,1)S(1)}, bf16[16,2176]{1,0:T(8,128)(2,1)S(1)}, bf16[32,2176]{1,0:T(8,128)(2,1)S(1)}, bf16[32,2176]{1,0:T(8,128)(2...) custom-call(s32[2]{0:T(128)S(1)} %pad_add_fusion.place_ref, ...), custom_call_target="tpu_custom_call" | custom-call | flops 1000 | bytes 1000 | tf_op jit(solution)/shard_map/pallas_call | solution.py:58
  2.9 3.1 %collective-permute-start = (bf16[32,2176]{1,0:T(8,128)(2,1)S(1)}, bf16[32,2176]{1,0:T(8,128)(2,1)S(1)}, u32[]{:S(2)}, u32[]{:S(2)}) collective-permute-start(bf16[32,2176]{1,0:T(8,128)(2,1)S(1)} %get-tuple-element.36), channel_id=1, source_target_pairs={{0,4},{4,0},{8,12},{12,8},{1,5},{5,1},{9,13},{13,9},{2,6},{6,2},{1... | collective-permute-start | bytes 417800 | tf_op jit(solution)/shard_map/ppermute | solution.py:38
  6.0 2.6 %collective-permute-start.1 = (bf16[32,2176]{1,0:T(8,128)(2,1)S(1)}, bf16[32,2176]{1,0:T(8,128)(2,1)S(1)}, u32[]{:S(2)}, u32[]{:S(2)}) collective-permute-start(bf16[32,2176]{1,0:T(8,128)(2,1)S(1)} %get-tuple-element.37), channel_id=1, source_target_pairs={{0,8},{4,12},{8,0},{12,4},{1,9},{5,13},{9,1},{13,5},{2,10},{6,14},... | collective-permute-start | bytes 417800 | tf_op jit(solution)/shard_map/ppermute | solution.py:38
  8.6 2.4 %shard_map.177 = (bf16[512,2048]{1,0:T(8,128)(2,1)S(1)}, bf16[512,2048]{1,0:T(8,128)(2,1)S(1)}) custom-call(bf16[512,2048]{1,0:T(8,128)(2,1)} %bitcast.65, bf16[512,2048]{1,0:T(8,128)(2,1)} %bitcast.66, bf16[32,2048]{1,0:T(8,128)(2,1)S(1)} %get-tuple-element.35.after_hbm.own_ref), custom_call_target="tpu_custom_call" | custom-call | flops 1000 | bytes 1000 | tf_op jit(solution)/shard_map/pallas_call | solution.py:58
  10.9 0.5 collective-permute-done.in1_ref
  11.4 8.0 %collective-permute-done.1.in2_ref = bf16[32,2176]{1,0:T(8,128)(2,1)S(1)} collective-permute-done((bf16[32,2176]{1,0:T(8,128)(2,1)S(1)}, bf16[32,2176]{1,0:T(8,128)(2,1)S(1)}, u32[]{:S(2)}, u32[]{:S(2)}) %collective-permute-start.1) | collective-permute-done | bytes 139296 | tf_op jit(solution)/shard_map/ppermute | solution.py:38
  19.7 1.5 %shard_map.178 = (f32[64,128]{1,0:T(8,128)S(1)}, bf16[64,128]{1,0:T(8,128)(2,1)S(1)}) custom-call(bf16[16,2176]{1,0:T(8,128)(2,1)S(1)} %get-tuple-element.43.own_ref, bf16[32,2176]{1,0:T(8,128)(2,1)S(1)} %collective-permute-done.in1_ref, bf16[32,2176]{1,0:T(8,128)(2,1)S(1)} %collective-permute-done.1.in2_ref, ...), custom_call_target="tpu_custom_call" | custom-call | flops 1000 | bytes 1000 | tf_op jit(solution)/shard_map/pallas_call | solution.py:58
  21.2 0.5 collective-permute-start.6
  21.8 0.3 copy-done.1
  22.1 1.6 %shard_map.179 = (f32[64,1280]{1,0:T(8,128)S(1)}, f32[64,1280]{1,0:T(8,128)S(1)}) custom-call(s32[2]{0:T(128)S(1)} %pad_add_fusion.place_ref, bf16[32,2048]{1,0:T(8,128)(2,1)S(1)} %get-tuple-element.35.after_hbm.own_ref, bf16[32,2176]{1,0:T(8,128)(2,1)S(1)} %collective-permute-done.in1_ref, bf16[32,2176]{1,0:T(8,128)(2,1)S(1)} %collective-permute-done.1.in2_ref, ...), custom_call_target="tpu_custom_call" | custom-call | flops 1000 | bytes 1000 | tf_op jit(solution)/shard_map/pallas_call | solution.py:58
  23.6 2.2 %collective-permute-start.4 = (f32[64,1280]{1,0:T(8,128)S(1)}, f32[64,1280]{1,0:T(8,128)S(1)}, u32[]{:S(2)}, u32[]{:S(2)}) collective-permute-start(f32[64,1280]{1,0:T(8,128)S(1)} %get-tuple-element.49), channel_id=1, source_target_pairs={{0,4},{4,0},{8,12},{12,8},{1,5},{5,1},{9,13},{13,9},{2,6},{6,2},{1... | collective-permute-start | bytes 983048 | tf_op jit(solution)/shard_map/ppermute | solution.py:38
  25.9 1.5 %collective-permute-start.7 = (f32[64,128]{1,0:T(8,128)S(1)}, f32[64,128]{1,0:T(8,128)S(1)}, u32[]{:S(2)}, u32[]{:S(2)}) collective-permute-start(f32[64,128]{1,0:T(8,128)S(1)} %add.84.near_ref), channel_id=1, source_target_pairs={{0,2},{1,3},{2,0},{3,1},{4,6},{5,7},{6,4},{7,5},{8,10},{9,11},{10,... | collective-permute-start | bytes 98312 | tf_op jit(solution)/shard_map/ppermute | solution.py:38
  27.4 0.1 multiply_cosine_fusion.1
  27.5 2.3 %collective-permute-done.7.far_ref = f32[64,128]{1,0:T(8,128)S(1)} collective-permute-done((f32[64,128]{1,0:T(8,128)S(1)}, f32[64,128]{1,0:T(8,128)S(1)}, u32[]{:S(2)}, u32[]{:S(2)}) %collective-permute-start.7) | collective-permute-done | bytes 32800 | tf_op jit(solution)/shard_map/ppermute | solution.py:38
  29.8 0.4 shard_map.180
  30.2 0.1 collective-permute-start.8
  30.3 3.0 %collective-permute-start.9 = (bf16[16,1152]{1,0:T(8,128)(2,1)S(1)}, bf16[16,1152]{1,0:T(8,128)(2,1)S(1)}, u32[]{:S(2)}, u32[]{:S(2)}) collective-permute-start(bf16[16,1152]{1,0:T(8,128)(2,1)S(1)} %get-tuple-element.55), channel_id=1, source_target_pairs={{0,8},{4,12},{8,0},{12,4},{1,9},{5,13},{9,1},{13,5},{2,10},{6,14},... | collective-permute-start | bytes 110600 | tf_op jit(solution)/shard_map/ppermute | solution.py:38
  33.3 1.3 %collective-permute-start.10 = (bf16[16,1152]{1,0:T(8,128)(2,1)S(1)}, bf16[16,1152]{1,0:T(8,128)(2,1)S(1)}, u32[]{:S(2)}, u32[]{:S(2)}) collective-permute-start(bf16[16,1152]{1,0:T(8,128)(2,1)S(1)} %get-tuple-element.56), channel_id=1, source_target_pairs={{0,12},{4,8},{8,4},{12,0},{1,13},{5,9},{9,5},{13,1},{2,14},{6,10},... | collective-permute-start | bytes 110600 | tf_op jit(solution)/shard_map/ppermute | solution.py:38
  34.9 2.7 %collective-permute-start.5 = (f32[32,1280]{1,0:T(8,128)S(1)}, f32[32,1280]{1,0:T(8,128)S(1)}, u32[]{:S(2)}, u32[]{:S(2)}) collective-permute-start(f32[32,1280]{1,0:T(8,128)S(1)} %slice.126), channel_id=1, source_target_pairs={{0,8},{4,12},{8,0},{12,4},{1,9},{5,13},{9,1},{13,5},{2,10},{6,14},... | collective-permute-start | bytes 491528 | tf_op jit(solution)/shard_map/ppermute | solution.py:38
  37.5 1.9 %collective-permute-done.10 = bf16[16,1152]{1,0:T(8,128)(2,1)S(1)} collective-permute-done((bf16[16,1152]{1,0:T(8,128)(2,1)S(1)}, bf16[16,1152]{1,0:T(8,128)(2,1)S(1)}, u32[]{:S(2)}, u32[]{:S(2)}) %collective-permute-start.10) | collective-permute-done | bytes 36896 | tf_op jit(solution)/shard_map/ppermute | solution.py:38
  39.5 0.2 fusion.25
  39.7 6.0 %collective-permute-done.5 = f32[32,1280]{1,0:T(8,128)S(1)} collective-permute-done((f32[32,1280]{1,0:T(8,128)S(1)}, f32[32,1280]{1,0:T(8,128)S(1)}, u32[]{:S(2)}, u32[]{:S(2)}) %collective-permute-start.5) | collective-permute-done | bytes 163872 | tf_op jit(solution)/shard_map/ppermute | solution.py:38
  45.8 0.1 fusion.56
  46.0 0.1 fusion.35
  46.1 0.2 fusion.51
  46.4 0.8 select_reduce_fusion
  47.1 0.2 fusion.34
  47.4 0.4 fusion
  47.9 1.8 %collective-permute-start.13 = (bf16[32,1536]{1,0:T(8,128)(2,1)S(1)}, bf16[32,1536]{1,0:T(8,128)(2,1)S(1)}, u32[]{:S(2)}, u32[]{:S(2)}) collective-permute-start(bf16[32,1536]{1,0:T(8,128)(2,1)S(1)} %get-tuple-element.88), channel_id=1, source_target_pairs={{0,12},{4,8},{8,4},{12,0},{1,13},{5,9},{9,5},{13,1},{2,14},{6,10},... | collective-permute-start | bytes 294920 | tf_op jit(solution)/shard_map/ppermute | solution.py:38
  49.7 2.6 %collective-permute-start.12 = (bf16[32,1536]{1,0:T(8,128)(2,1)S(1)}, bf16[32,1536]{1,0:T(8,128)(2,1)S(1)}, u32[]{:S(2)}, u32[]{:S(2)}) collective-permute-start(bf16[32,1536]{1,0:T(8,128)(2,1)S(1)} %get-tuple-element.90), channel_id=1, source_target_pairs={{0,8},{4,12},{8,0},{12,4},{1,9},{5,13},{9,1},{13,5},{2,10},{6,14},... | collective-permute-start | bytes 294920 | tf_op jit(solution)/shard_map/ppermute | solution.py:38
  52.3 3.1 %collective-permute-done.13.in3_ref = bf16[32,1536]{1,0:T(8,128)(2,1)S(1)} collective-permute-done((bf16[32,1536]{1,0:T(8,128)(2,1)S(1)}, bf16[32,1536]{1,0:T(8,128)(2,1)S(1)}, u32[]{:S(2)}, u32[]{:S(2)}) %collective-permute-start.13) | collective-permute-done | bytes 98336 | tf_op jit(solution)/shard_map/ppermute | solution.py:38
  55.4 2.3 %collective-permute-done.11.in1_ref = bf16[32,1536]{1,0:T(8,128)(2,1)S(1)} collective-permute-done((bf16[32,1536]{1,0:T(8,128)(2,1)S(1)}, bf16[32,1536]{1,0:T(8,128)(2,1)S(1)}, u32[]{:S(2)}, u32[]{:S(2)}) %collective-permute-start.11) | collective-permute-done | bytes 98336 | tf_op jit(solution)/shard_map/ppermute | solution.py:38
  57.8 0.8 collective-permute-done.12.in2_ref
  58.5 1.3 %shard_map.181 = (f32[64,2048]{1,0:T(8,128)S(1)}, f32[64,2048]{1,0:T(8,128)S(1)}) custom-call(s32[2]{0:T(128)S(1)} %pad_add_fusion.place_ref, bf16[32,1536]{1,0:T(8,128)(2,1)S(1)} %get-tuple-element.91.own_ref, bf16[32,1536]{1,0:T(8,128)(2,1)S(1)} %collective-permute-done.11.in1_ref, bf16[32,1536]{1,0:T(8,128)(2,1)S(1)} %collective-permute-done.12.in2_ref, ...), custom_call_target="tpu_custom_call" | custom-call | flops 1000 | bytes 1000 | tf_op jit(solution)/shard_map/pallas_call | solution.py:58
  59.9 1.9 %collective-permute-done.14 = f32[64,2048]{1,0:T(8,128)S(1)} collective-permute-done((f32[64,2048]{1,0:T(8,128)S(1)}, f32[64,2048]{1,0:T(8,128)S(1)}, u32[]{:S(2)}, u32[]{:S(2)}) %collective-permute-start.14) | collective-permute-done | bytes 524320 | tf_op jit(solution)/shard_map/ppermute | solution.py:38
  61.9 0.1 abs_reduce_fusion
  62.0 0.2 fusion.21
  62.4 1.6 %collective-permute-start.15 = (f16[32,2176]{1,0:T(8,128)(2,1)S(1)}, f16[32,2176]{1,0:T(8,128)(2,1)S(1)}, u32[]{:S(2)}, u32[]{:S(2)}) collective-permute-start(f16[32,2176]{1,0:T(8,128)(2,1)S(1)} %pad_maximum_fusion.3), channel_id=1, source_target_pairs={{0,2},{1,3},{2,0},{3,1},{4,6},{5,7},{6,4},{7,5},{8,10},{9,11},{10,... | collective-permute-start | bytes 417800 | tf_op jit(solution)/shard_map/ppermute | solution.py:38
  64.0 4.1 %collective-permute-done.15 = f16[32,2176]{1,0:T(8,128)(2,1)S(1)} collective-permute-done((f16[32,2176]{1,0:T(8,128)(2,1)S(1)}, f16[32,2176]{1,0:T(8,128)(2,1)S(1)}, u32[]{:S(2)}, u32[]{:S(2)}) %collective-permute-start.15) | collective-permute-done | bytes 139296 | tf_op jit(solution)/shard_map/ppermute | solution.py:38
  68.2 0.1 fusion.50
  68.3 0.3 multiply_reduce_fusion
  68.6 1.6 %collective-permute-start.20 = (f32[32]{0:T(128)S(1)}, f32[32]{0:T(128)S(1)}, u32[]{:S(2)}, u32[]{:S(2)}) collective-permute-start(f32[32]{0:T(128)S(1)} %get-tuple-element.74), channel_id=1, source_target_pairs={{0,12},{4,8},{8,4},{12,0},{1,13},{5,9},{9,5},{13,1},{2,14},{6,10},... | collective-permute-start | bytes 392 | tf_op jit(solution)/shard_map/ppermute | solution.py:38
  70.2 0.4 collective-permute-start.19
  70.7 2.4 %collective-permute-start.18 = (f32[32]{0:T(128)S(1)}, f32[32]{0:T(128)S(1)}, u32[]{:S(2)}, u32[]{:S(2)}) collective-permute-start(f32[32]{0:T(128)S(1)} %get-tuple-element.74), channel_id=1, source_target_pairs={{0,4},{4,0},{8,12},{12,8},{1,5},{5,1},{9,13},{13,9},{2,6},{6,2},{1... | collective-permute-start | bytes 392 | tf_op jit(solution)/shard_map/ppermute | solution.py:38
  73.1 1.6 %collective-permute-start.16 = (bf16[32,2048]{1,0:T(8,128)(2,1)S(1)}, bf16[32,2048]{1,0:T(8,128)(2,1)S(1)}, u32[]{:S(2)}, u32[]{:S(2)}) collective-permute-start(bf16[32,2048]{1,0:T(8,128)(2,1)S(1)} %get-tuple-element.75.own_ref), channel_id=1, source_target_pairs={{0,2},{1,3},{2,0},{3,1},{4,6},{5,7},{6,4},{7,5},{8,10},{9,11},{10,... | collective-permute-start | bytes 393224 | tf_op jit(solution)/shard_map/ppermute | solution.py:38
  74.7 1.6 %collective-permute-start.21 = (f32[1,32]{1,0:T(1,128)S(1)}, f32[1,32]{1,0:T(1,128)S(1)}, u32[]{:S(2)}, u32[]{:S(2)}) collective-permute-start(f32[1,32]{1,0:T(1,128)S(1)} %rsqrt_bitcast_fusion), channel_id=1, source_target_pairs={{0,2},{1,3},{2,0},{3,1},{4,6},{5,7},{6,4},{7,5},{8,10},{9,11},{10,... | collective-permute-start | bytes 392 | tf_op jit(solution)/shard_map/ppermute | solution.py:38
  76.3 1.7 %collective-permute-done.16.across_ref = bf16[32,2048]{1,0:T(8,128)(2,1)S(1)} collective-permute-done((bf16[32,2048]{1,0:T(8,128)(2,1)S(1)}, bf16[32,2048]{1,0:T(8,128)(2,1)S(1)}, u32[]{:S(2)}, u32[]{:S(2)}) %collective-permute-start.16) | collective-permute-done | bytes 131104 | tf_op jit(solution)/shard_map/ppermute | solution.py:38
  78.2 0.2 collective-permute-done.21
  78.3 0.4 collective-permute-start.22
  78.7 0.2 multiply_reduce_fusion.2
  78.9 0.8 collective-permute-done.22
  79.7 2.0 %shard_map.182 = (f32[64,2048]{1,0:T(8,128)S(1)}, f32[64,2048]{1,0:T(8,128)S(1)}) custom-call(s32[2]{0:T(128)S(1)} %pad_add_fusion.place_ref, bf16[32,2048]{1,0:T(8,128)(2,1)S(1)} %get-tuple-element.75.own_ref, bf16[32,2048]{1,0:T(8,128)(2,1)S(1)} %collective-permute-done.16.across_ref, bf16[64,2048]{1,0:T(8,128)(2,1)S(1)} %collective-permute-done.17.pair_ref, ...), custom_call_target="tpu_custom_call" | custom-call | flops 1000 | bytes 1000 | tf_op jit(solution)/shard_map/pallas_call | solution.py:58
  81.8 1.8 %collective-permute-start.23 = (f16[64,2048]{1,0:T(8,128)(2,1)S(1)}, f16[64,2048]{1,0:T(8,128)(2,1)S(1)}, u32[]{:S(2)}, u32[]{:S(2)}) collective-permute-start(f16[64,2048]{1,0:T(8,128)(2,1)S(1)} %convert_element_type.95), channel_id=1, source_target_pairs={{0,4},{4,0},{8,12},{12,8},{1,5},{5,1},{9,13},{13,9},{2,6},{6,2},{1... | collective-permute-start | bytes 786440 | tf_op jit(solution)/shard_map/ppermute | solution.py:38
  83.6 2.0 %shard_map.183 = (f32[64,2048]{1,0:T(8,128)S(1)}, f32[64,2048]{1,0:T(8,128)S(1)}) custom-call(s32[2]{0:T(128)S(1)} %pad_add_fusion.place_ref, bf16[32,2048]{1,0:T(8,128)(2,1)S(1)} %get-tuple-element.75.own_ref, bf16[32,2048]{1,0:T(8,128)(2,1)S(1)} %collective-permute-done.16.across_ref, bf16[64,2048]{1,0:T(8,128)(2,1)S(1)} %collective-permute-done.17.pair_ref, ...), custom_call_target="tpu_custom_call" | custom-call | flops 1000 | bytes 1000 | tf_op jit(solution)/shard_map/pallas_call | solution.py:58
  85.7 1.0 collective-permute-start.26
  86.7 1.2 %collective-permute-start.25 = (f16[32,2048]{1,0:T(8,128)(2,1)S(1)}, f16[32,2048]{1,0:T(8,128)(2,1)S(1)}, u32[]{:S(2)}, u32[]{:S(2)}) collective-permute-start(f16[32,2048]{1,0:T(8,128)(2,1)S(1)} %get-tuple-element.78), channel_id=1, source_target_pairs={{0,4},{4,0},{8,12},{12,8},{1,5},{5,1},{9,13},{13,9},{2,6},{6,2},{1... | collective-permute-start | bytes 393224 | tf_op jit(solution)/shard_map/ppermute | solution.py:38
  88.0 2.3 %collective-permute-start.27 = (f16[32,2048]{1,0:T(8,128)(2,1)S(1)}, f16[32,2048]{1,0:T(8,128)(2,1)S(1)}, u32[]{:S(2)}, u32[]{:S(2)}) collective-permute-start(f16[32,2048]{1,0:T(8,128)(2,1)S(1)} %get-tuple-element.79), channel_id=1, source_target_pairs={{0,12},{4,8},{8,4},{12,0},{1,13},{5,9},{9,5},{13,1},{2,14},{6,10},... | collective-permute-start | bytes 393224 | tf_op jit(solution)/shard_map/ppermute | solution.py:38
  90.2 2.9 %collective-permute-done.23 = f16[64,2048]{1,0:T(8,128)(2,1)S(1)} collective-permute-done((f16[64,2048]{1,0:T(8,128)(2,1)S(1)}, f16[64,2048]{1,0:T(8,128)(2,1)S(1)}, u32[]{:S(2)}, u32[]{:S(2)}) %collective-permute-start.23) | collective-permute-done | bytes 262176 | tf_op jit(solution)/shard_map/ppermute | solution.py:38
  93.2 0.6 collective-permute-start.24
  93.8 2.0 %collective-permute-done.26 = f16[32,2048]{1,0:T(8,128)(2,1)S(1)} collective-permute-done((f16[32,2048]{1,0:T(8,128)(2,1)S(1)}, f16[32,2048]{1,0:T(8,128)(2,1)S(1)}, u32[]{:S(2)}, u32[]{:S(2)}) %collective-permute-start.26) | collective-permute-done | bytes 131104 | tf_op jit(solution)/shard_map/ppermute | solution.py:38
  95.8 0.1 collective-permute-done.25
  95.9 4.9 %collective-permute-done.27 = f16[32,2048]{1,0:T(8,128)(2,1)S(1)} collective-permute-done((f16[32,2048]{1,0:T(8,128)(2,1)S(1)}, f16[32,2048]{1,0:T(8,128)(2,1)S(1)}, u32[]{:S(2)}, u32[]{:S(2)}) %collective-permute-start.27) | collective-permute-done | bytes 131104 | tf_op jit(solution)/shard_map/ppermute | solution.py:38
  100.9 5.1 %collective-permute-done.24 = f16[32,2048]{1,0:T(8,128)(2,1)S(1)} collective-permute-done((f16[32,2048]{1,0:T(8,128)(2,1)S(1)}, f16[32,2048]{1,0:T(8,128)(2,1)S(1)}, u32[]{:S(2)}, u32[]{:S(2)}) %collective-permute-start.24) | collective-permute-done | bytes 131104 | tf_op jit(solution)/shard_map/ppermute | solution.py:38
  106.2 1.2 %copy.20 = f32[32,2,2048]{2,1,0:T(2,128)} copy(f32[32,2,2048]{2,0,1:T(8,128)S(1)} %pad_maximum_fusion) | data formatting | bytes 1048576
  (82 shorter events, 1.6 us)
Async XLA Ops:
  0.6 45.7 %copy-start = (bf16[32,1,128,128]{3,2,1,0:T(8,128)(2,1)S(1)}, bf16[32,1,128,128]{3,2,1,0:T(8,128)(2,1)}, u32[]{:S(2)}) copy-start(bf16[32,1,128,128]{3,2,1,0:T(8,128)(2,1)} %param.26) | copy-start | bytes 3145732
  2.9 8.5 %collective-permute-start = (bf16[32,2176]{1,0:T(8,128)(2,1)S(1)}, bf16[32,2176]{1,0:T(8,128)(2,1)S(1)}, u32[]{:S(2)}, u32[]{:S(2)}) collective-permute-start(bf16[32,2176]{1,0:T(8,128)(2,1)S(1)} %get-tuple-element.36), channel_id=1, source_target_pairs={{0,4},{4,0},{8,12},{12,8},{1,5},{5,1},{9,13},{13,9},{2,6},{6,2},{1... | collective-permute-start | bytes 417800 | tf_op jit(solution)/shard_map/ppermute | solution.py:38
  6.0 13.5 %collective-permute-start.1 = (bf16[32,2176]{1,0:T(8,128)(2,1)S(1)}, bf16[32,2176]{1,0:T(8,128)(2,1)S(1)}, u32[]{:S(2)}, u32[]{:S(2)}) collective-permute-start(bf16[32,2176]{1,0:T(8,128)(2,1)S(1)} %get-tuple-element.37), channel_id=1, source_target_pairs={{0,8},{4,12},{8,0},{12,4},{1,9},{5,13},{9,1},{13,5},{2,10},{6,14},... | collective-permute-start | bytes 417800 | tf_op jit(solution)/shard_map/ppermute | solution.py:38
  8.6 10.9 %collective-permute-start.2 = (bf16[32,2176]{1,0:T(8,128)(2,1)S(1)}, bf16[32,2176]{1,0:T(8,128)(2,1)S(1)}, u32[]{:S(2)}, u32[]{:S(2)}) collective-permute-start(bf16[32,2176]{1,0:T(8,128)(2,1)S(1)} %get-tuple-element.38), channel_id=1, source_target_pairs={{0,12},{4,8},{8,4},{12,0},{1,13},{5,9},{9,5},{13,1},{2,14},{6,10},... | collective-permute-start | bytes 417800 | tf_op jit(solution)/shard_map/ppermute | solution.py:38
  8.6 71.1 %slice-start = ((s8[16777216]{0:T(1024)(128)(4,1)}), s8[4194304]{0:T(1024)(128)(4,1)S(1)}, s32[]{:S(2)}) async-start(s8[16777216]{0:T(1024)(128)(4,1)} %bitcast.61), calls=%async_computation | async-start | bytes 8388608
  19.5 2.3 %copy-start.6 = (bf16[2048,128]{1,0:T(8,128)(2,1)S(1)}, bf16[2048,128]{1,0:T(8,128)(2,1)}, u32[]{:S(2)}) copy-start(bf16[2048,128]{1,0:T(8,128)(2,1)} %value_ref.1) | copy-start | bytes 1572868
  19.5 1.7 %collective-permute-start.3 = (bf16[48,2048]{1,0:T(8,128)(2,1)S(1)}, bf16[48,2048]{1,0:T(8,128)(2,1)S(1)}, u32[]{:S(2)}, u32[]{:S(2)}) collective-permute-start(bf16[48,2048]{1,0:T(8,128)(2,1)S(1)} %pad_maximum_fusion.2), channel_id=1, source_target_pairs={{0,1},{1,0},{2,3},{3,2},{4,5},{5,4},{6,7},{7,6},{8,9},{9,8},{10,11... | collective-permute-start | bytes 589832 | tf_op jit(solution)/shard_map/ppermute | solution.py:38
  19.6 2.2 %copy-start.8 = (s32[32]{0:T(128)S(1)}, s32[32]{0:T(128)}, u32[]{:S(2)}) copy-start(s32[32]{0:T(128)} %param.29) | copy-start | bytes 388
  19.6 2.2 %copy-start.5 = (bf16[2048,128]{1,0:T(8,128)(2,1)S(1)}, bf16[2048,128]{1,0:T(8,128)(2,1)}, u32[]{:S(2)}) copy-start(bf16[2048,128]{1,0:T(8,128)(2,1)} %key_ref.1) | copy-start | bytes 1572868
  19.7 2.4 %copy-start.1 = (bf16[2048,1024]{1,0:T(8,128)(2,1)S(1)}, bf16[2048,1024]{1,0:T(8,128)(2,1)}, u32[]{:S(2)}) copy-start(bf16[2048,1024]{1,0:T(8,128)(2,1)} %query_ref.1) | copy-start | bytes 12582916
  19.7 60.0 %slice-start.1 = ((s8[16777216]{0:T(1024)(128)(4,1)}), s8[4194304]{0:T(1024)(128)(4,1)S(1)}, s32[]{:S(2)}) async-start(s8[16777216]{0:T(1024)(128)(4,1)} %bitcast.61), calls=%async_computation.1 | async-start | bytes 8388608
  21.2 4.6 %collective-permute-start.6 = (f32[64,128]{1,0:T(8,128)S(1)}, f32[64,128]{1,0:T(8,128)S(1)}, u32[]{:S(2)}, u32[]{:S(2)}) collective-permute-start(f32[64,128]{1,0:T(8,128)S(1)} %get-tuple-element.51), channel_id=1, source_target_pairs={{0,1},{1,0},{2,3},{3,2},{4,5},{5,4},{6,7},{7,6},{8,9},{9,8},{10,11... | collective-permute-start | bytes 98312 | tf_op jit(solution)/shard_map/ppermute | solution.py:38
  22.1 7.8 %copy-start.4 = (bf16[8,64,1024]{2,1,0:T(8,128)(2,1)S(1)}, bf16[8,64,1024]{2,1,0:T(8,128)(2,1)}, u32[]{:S(2)}) copy-start(bf16[8,64,1024]{2,1,0:T(8,128)(2,1)} %param.23) | copy-start | bytes 3145732
  22.1 7.8 %copy-start.7 = (bf16[8,64,128]{2,1,0:T(8,128)(2,1)S(1)}, bf16[8,64,128]{2,1,0:T(8,128)(2,1)}, u32[]{:S(2)}) copy-start(bf16[8,64,128]{2,1,0:T(8,128)(2,1)} %param.25) | copy-start | bytes 393220
  22.1 25.3 %copy-start.9 = (bf16[32,1,128,128]{3,2,1,0:T(8,128)(2,1)S(1)}, bf16[32,1,128,128]{3,2,1,0:T(8,128)(2,1)}, u32[]{:S(2)}) copy-start(bf16[32,1,128,128]{3,2,1,0:T(8,128)(2,1)} %param.27) | copy-start | bytes 3145732
  23.6 11.2 %collective-permute-start.4 = (f32[64,1280]{1,0:T(8,128)S(1)}, f32[64,1280]{1,0:T(8,128)S(1)}, u32[]{:S(2)}, u32[]{:S(2)}) collective-permute-start(f32[64,1280]{1,0:T(8,128)S(1)} %get-tuple-element.49), channel_id=1, source_target_pairs={{0,4},{4,0},{8,12},{12,8},{1,5},{5,1},{9,13},{13,9},{2,6},{6,2},{1... | collective-permute-start | bytes 983048 | tf_op jit(solution)/shard_map/ppermute | solution.py:38
  25.9 4.0 %collective-permute-start.7 = (f32[64,128]{1,0:T(8,128)S(1)}, f32[64,128]{1,0:T(8,128)S(1)}, u32[]{:S(2)}, u32[]{:S(2)}) collective-permute-start(f32[64,128]{1,0:T(8,128)S(1)} %add.84.near_ref), channel_id=1, source_target_pairs={{0,2},{1,3},{2,0},{3,1},{4,6},{5,7},{6,4},{7,5},{8,10},{9,11},{10,... | collective-permute-start | bytes 98312 | tf_op jit(solution)/shard_map/ppermute | solution.py:38
  29.8 49.9 %slice-start.2 = ((s8[16777216]{0:T(1024)(128)(4,1)}), s8[4194304]{0:T(1024)(128)(4,1)S(1)}, s32[]{:S(2)}) async-start(s8[16777216]{0:T(1024)(128)(4,1)} %bitcast.61), calls=%async_computation.2 | async-start | bytes 8388608
  30.2 7.3 %collective-permute-start.8 = (bf16[16,1152]{1,0:T(8,128)(2,1)S(1)}, bf16[16,1152]{1,0:T(8,128)(2,1)S(1)}, u32[]{:S(2)}, u32[]{:S(2)}) collective-permute-start(bf16[16,1152]{1,0:T(8,128)(2,1)S(1)} %get-tuple-element.54), channel_id=1, source_target_pairs={{0,4},{4,0},{8,12},{12,8},{1,5},{5,1},{9,13},{13,9},{2,6},{6,2},{1... | collective-permute-start | bytes 110600 | tf_op jit(solution)/shard_map/ppermute | solution.py:38
  30.3 7.2 %collective-permute-start.9 = (bf16[16,1152]{1,0:T(8,128)(2,1)S(1)}, bf16[16,1152]{1,0:T(8,128)(2,1)S(1)}, u32[]{:S(2)}, u32[]{:S(2)}) collective-permute-start(bf16[16,1152]{1,0:T(8,128)(2,1)S(1)} %get-tuple-element.55), channel_id=1, source_target_pairs={{0,8},{4,12},{8,0},{12,4},{1,9},{5,13},{9,1},{13,5},{2,10},{6,14},... | collective-permute-start | bytes 110600 | tf_op jit(solution)/shard_map/ppermute | solution.py:38
  33.3 6.1 %collective-permute-start.10 = (bf16[16,1152]{1,0:T(8,128)(2,1)S(1)}, bf16[16,1152]{1,0:T(8,128)(2,1)S(1)}, u32[]{:S(2)}, u32[]{:S(2)}) collective-permute-start(bf16[16,1152]{1,0:T(8,128)(2,1)S(1)} %get-tuple-element.56), channel_id=1, source_target_pairs={{0,12},{4,8},{8,4},{12,0},{1,13},{5,9},{9,5},{13,1},{2,14},{6,10},... | collective-permute-start | bytes 110600 | tf_op jit(solution)/shard_map/ppermute | solution.py:38
  34.9 10.8 %collective-permute-start.5 = (f32[32,1280]{1,0:T(8,128)S(1)}, f32[32,1280]{1,0:T(8,128)S(1)}, u32[]{:S(2)}, u32[]{:S(2)}) collective-permute-start(f32[32,1280]{1,0:T(8,128)S(1)} %slice.126), channel_id=1, source_target_pairs={{0,8},{4,12},{8,0},{12,4},{1,9},{5,13},{9,1},{13,5},{2,10},{6,14},... | collective-permute-start | bytes 491528 | tf_op jit(solution)/shard_map/ppermute | solution.py:38
  46.0 12.5 %copy-start.2 = (bf16[1024,2048]{1,0:T(8,128)(2,1)S(1)}, bf16[1024,2048]{1,0:T(8,128)(2,1)}, u32[]{:S(2)}) copy-start(bf16[1024,2048]{1,0:T(8,128)(2,1)} %weight_ref.3) | copy-start | bytes 12582916
  47.8 31.9 %slice-start.3 = ((s8[16777216]{0:T(1024)(128)(4,1)}), s8[4194304]{0:T(1024)(128)(4,1)S(1)}, s32[]{:S(2)}) async-start(s8[16777216]{0:T(1024)(128)(4,1)} %bitcast.61), calls=%async_computation.3 | async-start | bytes 8388608
  47.9 7.6 %collective-permute-start.13 = (bf16[32,1536]{1,0:T(8,128)(2,1)S(1)}, bf16[32,1536]{1,0:T(8,128)(2,1)S(1)}, u32[]{:S(2)}, u32[]{:S(2)}) collective-permute-start(bf16[32,1536]{1,0:T(8,128)(2,1)S(1)} %get-tuple-element.88), channel_id=1, source_target_pairs={{0,12},{4,8},{8,4},{12,0},{1,13},{5,9},{9,5},{13,1},{2,14},{6,10},... | collective-permute-start | bytes 294920 | tf_op jit(solution)/shard_map/ppermute | solution.py:38
  49.7 8.0 %collective-permute-start.11 = (bf16[32,1536]{1,0:T(8,128)(2,1)S(1)}, bf16[32,1536]{1,0:T(8,128)(2,1)S(1)}, u32[]{:S(2)}, u32[]{:S(2)}) collective-permute-start(bf16[32,1536]{1,0:T(8,128)(2,1)S(1)} %get-tuple-element.89), channel_id=1, source_target_pairs={{0,4},{4,0},{8,12},{12,8},{1,5},{5,1},{9,13},{13,9},{2,6},{6,2},{1... | collective-permute-start | bytes 294920 | tf_op jit(solution)/shard_map/ppermute | solution.py:38
  49.7 8.8 %collective-permute-start.12 = (bf16[32,1536]{1,0:T(8,128)(2,1)S(1)}, bf16[32,1536]{1,0:T(8,128)(2,1)S(1)}, u32[]{:S(2)}, u32[]{:S(2)}) collective-permute-start(bf16[32,1536]{1,0:T(8,128)(2,1)S(1)} %get-tuple-element.90), channel_id=1, source_target_pairs={{0,8},{4,12},{8,0},{12,4},{1,9},{5,13},{9,1},{13,5},{2,10},{6,14},... | collective-permute-start | bytes 294920 | tf_op jit(solution)/shard_map/ppermute | solution.py:38
  59.8 2.0 %collective-permute-start.14 = (f32[64,2048]{1,0:T(8,128)S(1)}, f32[64,2048]{1,0:T(8,128)S(1)}, u32[]{:S(2)}, u32[]{:S(2)}) collective-permute-start(f32[64,2048]{1,0:T(8,128)S(1)} %get-tuple-element.59), channel_id=1, source_target_pairs={{0,1},{1,0},{2,3},{3,2},{4,5},{5,4},{6,7},{7,6},{8,9},{9,8},{10,11... | collective-permute-start | bytes 1572872 | tf_op jit(solution)/shard_map/ppermute | solution.py:38
  62.4 5.8 %collective-permute-start.15 = (f16[32,2176]{1,0:T(8,128)(2,1)S(1)}, f16[32,2176]{1,0:T(8,128)(2,1)S(1)}, u32[]{:S(2)}, u32[]{:S(2)}) collective-permute-start(f16[32,2176]{1,0:T(8,128)(2,1)S(1)} %pad_maximum_fusion.3), channel_id=1, source_target_pairs={{0,2},{1,3},{2,0},{3,1},{4,6},{5,7},{6,4},{7,5},{8,10},{9,11},{10,... | collective-permute-start | bytes 417800 | tf_op jit(solution)/shard_map/ppermute | solution.py:38
  68.6 15.0 %copy-start.3 = (bf16[32,2048]{1,0:T(8,128)(2,1)}, bf16[32,2048]{1,0:T(8,128)(2,1)S(1)}, u32[]{:S(2)}) copy-start(bf16[32,2048]{1,0:T(8,128)(2,1)S(1)} %get-tuple-element.75.own_ref) | copy-start | bytes 393220
  68.6 6.0 %collective-permute-start.20 = (f32[32]{0:T(128)S(1)}, f32[32]{0:T(128)S(1)}, u32[]{:S(2)}, u32[]{:S(2)}) collective-permute-start(f32[32]{0:T(128)S(1)} %get-tuple-element.74), channel_id=1, source_target_pairs={{0,12},{4,8},{8,4},{12,0},{1,13},{5,9},{9,5},{13,1},{2,14},{6,10},... | collective-permute-start | bytes 392 | tf_op jit(solution)/shard_map/ppermute | solution.py:38
  70.2 4.4 %collective-permute-start.19 = (f32[32]{0:T(128)S(1)}, f32[32]{0:T(128)S(1)}, u32[]{:S(2)}, u32[]{:S(2)}) collective-permute-start(f32[32]{0:T(128)S(1)} %get-tuple-element.74), channel_id=1, source_target_pairs={{0,8},{4,12},{8,0},{12,4},{1,9},{5,13},{9,1},{13,5},{2,10},{6,14},... | collective-permute-start | bytes 392 | tf_op jit(solution)/shard_map/ppermute | solution.py:38
  70.7 4.0 %collective-permute-start.18 = (f32[32]{0:T(128)S(1)}, f32[32]{0:T(128)S(1)}, u32[]{:S(2)}, u32[]{:S(2)}) collective-permute-start(f32[32]{0:T(128)S(1)} %get-tuple-element.74), channel_id=1, source_target_pairs={{0,4},{4,0},{8,12},{12,8},{1,5},{5,1},{9,13},{13,9},{2,6},{6,2},{1... | collective-permute-start | bytes 392 | tf_op jit(solution)/shard_map/ppermute | solution.py:38
  73.1 5.0 %collective-permute-start.16 = (bf16[32,2048]{1,0:T(8,128)(2,1)S(1)}, bf16[32,2048]{1,0:T(8,128)(2,1)S(1)}, u32[]{:S(2)}, u32[]{:S(2)}) collective-permute-start(bf16[32,2048]{1,0:T(8,128)(2,1)S(1)} %get-tuple-element.75.own_ref), channel_id=1, source_target_pairs={{0,2},{1,3},{2,0},{3,1},{4,6},{5,7},{6,4},{7,5},{8,10},{9,11},{10,... | collective-permute-start | bytes 393224 | tf_op jit(solution)/shard_map/ppermute | solution.py:38
  74.7 3.6 %collective-permute-start.21 = (f32[1,32]{1,0:T(1,128)S(1)}, f32[1,32]{1,0:T(1,128)S(1)}, u32[]{:S(2)}, u32[]{:S(2)}) collective-permute-start(f32[1,32]{1,0:T(1,128)S(1)} %rsqrt_bitcast_fusion), channel_id=1, source_target_pairs={{0,2},{1,3},{2,0},{3,1},{4,6},{5,7},{6,4},{7,5},{8,10},{9,11},{10,... | collective-permute-start | bytes 392 | tf_op jit(solution)/shard_map/ppermute | solution.py:38
  78.1 1.6 %collective-permute-start.17 = (bf16[64,2048]{1,0:T(8,128)(2,1)S(1)}, bf16[64,2048]{1,0:T(8,128)(2,1)S(1)}, u32[]{:S(2)}, u32[]{:S(2)}) collective-permute-start(bf16[64,2048]{1,0:T(8,128)(2,1)S(1)} %pad_maximum_fusion.1), channel_id=1, source_target_pairs={{0,1},{1,0},{2,3},{3,2},{4,5},{5,4},{6,7},{7,6},{8,9},{9,8},{10,11... | collective-permute-start | bytes 786440 | tf_op jit(solution)/shard_map/ppermute | solution.py:38
  78.3 1.4 %collective-permute-start.22 = (f32[2,32]{1,0:T(2,128)S(1)}, f32[2,32]{1,0:T(2,128)S(1)}, u32[]{:S(2)}, u32[]{:S(2)}) collective-permute-start(f32[2,32]{1,0:T(2,128)S(1)} %pad_maximum_fusion.12), channel_id=1, source_target_pairs={{0,1},{1,0},{2,3},{3,2},{4,5},{5,4},{6,7},{7,6},{8,9},{9,8},{10,11... | collective-permute-start | bytes 776 | tf_op jit(solution)/shard_map/ppermute | solution.py:38
  81.8 11.3 %collective-permute-start.23 = (f16[64,2048]{1,0:T(8,128)(2,1)S(1)}, f16[64,2048]{1,0:T(8,128)(2,1)S(1)}, u32[]{:S(2)}, u32[]{:S(2)}) collective-permute-start(f16[64,2048]{1,0:T(8,128)(2,1)S(1)} %convert_element_type.95), channel_id=1, source_target_pairs={{0,4},{4,0},{8,12},{12,8},{1,5},{5,1},{9,13},{13,9},{2,6},{6,2},{1... | collective-permute-start | bytes 786440 | tf_op jit(solution)/shard_map/ppermute | solution.py:38
  85.7 10.1 %collective-permute-start.26 = (f16[32,2048]{1,0:T(8,128)(2,1)S(1)}, f16[32,2048]{1,0:T(8,128)(2,1)S(1)}, u32[]{:S(2)}, u32[]{:S(2)}) collective-permute-start(f16[32,2048]{1,0:T(8,128)(2,1)S(1)} %slice_convert_fusion), channel_id=1, source_target_pairs={{0,8},{4,12},{8,0},{12,4},{1,9},{5,13},{9,1},{13,5},{2,10},{6,14},... | collective-permute-start | bytes 393224 | tf_op jit(solution)/shard_map/ppermute | solution.py:38
  86.7 9.2 %collective-permute-start.25 = (f16[32,2048]{1,0:T(8,128)(2,1)S(1)}, f16[32,2048]{1,0:T(8,128)(2,1)S(1)}, u32[]{:S(2)}, u32[]{:S(2)}) collective-permute-start(f16[32,2048]{1,0:T(8,128)(2,1)S(1)} %get-tuple-element.78), channel_id=1, source_target_pairs={{0,4},{4,0},{8,12},{12,8},{1,5},{5,1},{9,13},{13,9},{2,6},{6,2},{1... | collective-permute-start | bytes 393224 | tf_op jit(solution)/shard_map/ppermute | solution.py:38
  88.0 12.9 %collective-permute-start.27 = (f16[32,2048]{1,0:T(8,128)(2,1)S(1)}, f16[32,2048]{1,0:T(8,128)(2,1)S(1)}, u32[]{:S(2)}, u32[]{:S(2)}) collective-permute-start(f16[32,2048]{1,0:T(8,128)(2,1)S(1)} %get-tuple-element.79), channel_id=1, source_target_pairs={{0,12},{4,8},{8,4},{12,0},{1,13},{5,9},{9,5},{13,1},{2,14},{6,10},... | collective-permute-start | bytes 393224 | tf_op jit(solution)/shard_map/ppermute | solution.py:38
  93.2 12.8 %collective-permute-start.24 = (f16[32,2048]{1,0:T(8,128)(2,1)S(1)}, f16[32,2048]{1,0:T(8,128)(2,1)S(1)}, u32[]{:S(2)}, u32[]{:S(2)}) collective-permute-start(f16[32,2048]{1,0:T(8,128)(2,1)S(1)} %slice_convert_fusion.1), channel_id=1, source_target_pairs={{0,8},{4,12},{8,0},{12,4},{1,9},{5,13},{9,1},{13,5},{2,10},{6,14},... | collective-permute-start | bytes 393224 | tf_op jit(solution)/shard_map/ppermute | solution.py:38

commit v6 on v5

--- a/solution.py
+++ b/solution.py
@@ -294,6 +294,11 @@
         rows_ref[pl.ds(at, streams), :] = (
             piece.astype(jnp.float32) * scale * gain_ref[...]
         ).astype(jnp.bfloat16)
+    columns_kernel(first, rows_ref, weight_ref, keep_ref, send_ref)
+
+
+def columns_kernel(first, rows_ref, weight_ref, keep_ref, send_ref):
+    streams = keep_ref.shape[0] // 2
     width = keep_ref.shape[1]
     out = 16.0 * jnp.dot(
         rows_ref[...], weight_ref[:, first : first + width], preferred_element_type=jnp.float32
@@ -522,22 +527,20 @@
     width = codebook_weight.shape[1] // 2
     outs = []
 
-    def head(first, ids):
-        return call(
-            functools.partial(head_kernel, first),
-            [shaped((2 * str_dev, width), jnp.float32)] * 2,
-            [hidden_out, across, hidden_pair, scale, final_slice],
-            [ids],
-            [pltpu.VMEM((n_adapter * str_dev, d_slice), bf16)],
-            resident=[codebook_weight],
-        )
-
     def moved(block, k):
         return swap(block.astype(jnp.float16), "adapter", k).astype(jnp.float32)
 
-    kept, sent = head(0, place_ids)
-    kept, place_ids = lax.optimization_barrier((kept, place_ids))
-    kept_far, sent_far = head(width, place_ids)
+    sums = [shaped((2 * str_dev, width), jnp.float32)] * 2
+    kept, sent, final_rows = call(
+        functools.partial(head_kernel, 0),
+        sums + [shaped((n_adapter * str_dev, d_slice), bf16)],
+        [hidden_out, across, hidden_pair, scale, final_slice],
+        [place_ids],
+        resident=[codebook_weight],
+    )
+    kept_far, sent_far = call(
+        functools.partial(columns_kernel, width), sums, [final_rows], resident=[codebook_weight]
+    )
     kept = kept + moved(sent, 1)
     first_total = kept[:str_dev] + moved(kept[str_dev:], 2)
     second_total = (

time: 108 us -> 107 us (level)
  no operation moved by 1% of the time
where the time goes in v6:
time: 107 us
  waiting for transfers between devices  48.7 us (46%)
  starting transfers between devices  38.3 us (36%)
  Pallas kernels  12.6 us (12%)
  other arithmetic  2.51 us (2%)
  local copies, waits for them, and re-layouts  1.74 us (2%)
  matrix products  1.62 us (2%)
  between operations  1.12 us (1%)
    ppermute x28, waiting for transfers between devices, swap(): return lax.ppermute(value, axis, [(i, i ^ distance) for i in range(size)])  48.7 us
    ppermute x28, starting transfers between devices, swap(): return lax.ppermute(value, axis, [(i, i ^ distance) for i in range(size)])  38.3 us
    pallas_call x8, Pallas kernels, call(): pl.pallas_call(kernel, out_shape=tuple(outs), in_specs=specs, out_specs=t...  12.6 us
  transfers between devices with their start and end apart: 28, of which 18 were waited for; matrix products, arithmetic and copies ran while one was open for 1% of the time, Pallas kernels for 7%

profile of v6, /device:TPU:0, one launch (start us, length us, event | category | flops | bytes accessed | tf_op | source)
XLA Modules:
  0.0 106.6 jit_solution(14136887751556265526)
XLA Ops:
  0.7 2.2 %shard_map.176 = (bf16[32,2048]{1,0:T(8,128)(2,1)S(1)}, bf16[16,2176]{1,0:T(8,128)(2,1)S(1)}, bf16[32,2176]{1,0:T(8,128)(2,1)S(1)}, bf16[32,2176]{1,0:T(8,128)(2...) custom-call(s32[2]{0:T(128)S(1)} %pad_add_fusion.place_ref, ...), custom_call_target="tpu_custom_call" | custom-call | flops 1000 | bytes 1000 | tf_op jit(solution)/shard_map/pallas_call | solution.py:58
  2.9 3.1 %collective-permute-start = (bf16[32,2176]{1,0:T(8,128)(2,1)S(1)}, bf16[32,2176]{1,0:T(8,128)(2,1)S(1)}, u32[]{:S(2)}, u32[]{:S(2)}) collective-permute-start(bf16[32,2176]{1,0:T(8,128)(2,1)S(1)} %get-tuple-element.35), channel_id=1, source_target_pairs={{0,4},{4,0},{8,12},{12,8},{1,5},{5,1},{9,13},{13,9},{2,6},{6,2},{1... | collective-permute-start | bytes 417800 | tf_op jit(solution)/shard_map/ppermute | solution.py:38
  6.0 2.6 %collective-permute-start.1 = (bf16[32,2176]{1,0:T(8,128)(2,1)S(1)}, bf16[32,2176]{1,0:T(8,128)(2,1)S(1)}, u32[]{:S(2)}, u32[]{:S(2)}) collective-permute-start(bf16[32,2176]{1,0:T(8,128)(2,1)S(1)} %get-tuple-element.36), channel_id=1, source_target_pairs={{0,8},{4,12},{8,0},{12,4},{1,9},{5,13},{9,1},{13,5},{2,10},{6,14},... | collective-permute-start | bytes 417800 | tf_op jit(solution)/shard_map/ppermute | solution.py:38
  8.6 2.4 %shard_map.177 = (bf16[512,2048]{1,0:T(8,128)(2,1)S(1)}, bf16[512,2048]{1,0:T(8,128)(2,1)S(1)}) custom-call(bf16[512,2048]{1,0:T(8,128)(2,1)} %bitcast.65, bf16[512,2048]{1,0:T(8,128)(2,1)} %bitcast.66, bf16[32,2048]{1,0:T(8,128)(2,1)S(1)} %get-tuple-element.34.after_hbm.own_ref), custom_call_target="tpu_custom_call" | custom-call | flops 1000 | bytes 1000 | tf_op jit(solution)/shard_map/pallas_call | solution.py:58
  10.9 0.5 collective-permute-done.in1_ref
  11.4 8.0 %collective-permute-done.1.in2_ref = bf16[32,2176]{1,0:T(8,128)(2,1)S(1)} collective-permute-done((bf16[32,2176]{1,0:T(8,128)(2,1)S(1)}, bf16[32,2176]{1,0:T(8,128)(2,1)S(1)}, u32[]{:S(2)}, u32[]{:S(2)}) %collective-permute-start.1) | collective-permute-done | bytes 139296 | tf_op jit(solution)/shard_map/ppermute | solution.py:38
  19.7 1.5 %shard_map.178 = (f32[64,128]{1,0:T(8,128)S(1)}, bf16[64,128]{1,0:T(8,128)(2,1)S(1)}) custom-call(bf16[16,2176]{1,0:T(8,128)(2,1)S(1)} %get-tuple-element.42.own_ref, bf16[32,2176]{1,0:T(8,128)(2,1)S(1)} %collective-permute-done.in1_ref, bf16[32,2176]{1,0:T(8,128)(2,1)S(1)} %collective-permute-done.1.in2_ref, ...), custom_call_target="tpu_custom_call" | custom-call | flops 1000 | bytes 1000 | tf_op jit(solution)/shard_map/pallas_call | solution.py:58
  21.2 0.5 collective-permute-start.6
  21.8 0.3 copy-done.1
  22.1 1.6 %shard_map.179 = (f32[64,1280]{1,0:T(8,128)S(1)}, f32[64,1280]{1,0:T(8,128)S(1)}) custom-call(s32[2]{0:T(128)S(1)} %pad_add_fusion.place_ref, bf16[32,2048]{1,0:T(8,128)(2,1)S(1)} %get-tuple-element.34.after_hbm.own_ref, bf16[32,2176]{1,0:T(8,128)(2,1)S(1)} %collective-permute-done.in1_ref, bf16[32,2176]{1,0:T(8,128)(2,1)S(1)} %collective-permute-done.1.in2_ref, ...), custom_call_target="tpu_custom_call" | custom-call | flops 1000 | bytes 1000 | tf_op jit(solution)/shard_map/pallas_call | solution.py:58
  23.6 2.2 %collective-permute-start.4 = (f32[64,1280]{1,0:T(8,128)S(1)}, f32[64,1280]{1,0:T(8,128)S(1)}, u32[]{:S(2)}, u32[]{:S(2)}) collective-permute-start(f32[64,1280]{1,0:T(8,128)S(1)} %get-tuple-element.48), channel_id=1, source_target_pairs={{0,4},{4,0},{8,12},{12,8},{1,5},{5,1},{9,13},{13,9},{2,6},{6,2},{1... | collective-permute-start | bytes 983048 | tf_op jit(solution)/shard_map/ppermute | solution.py:38
  25.9 1.5 %collective-permute-start.7 = (f32[64,128]{1,0:T(8,128)S(1)}, f32[64,128]{1,0:T(8,128)S(1)}, u32[]{:S(2)}, u32[]{:S(2)}) collective-permute-start(f32[64,128]{1,0:T(8,128)S(1)} %add.84.near_ref), channel_id=1, source_target_pairs={{0,2},{1,3},{2,0},{3,1},{4,6},{5,7},{6,4},{7,5},{8,10},{9,11},{10,... | collective-permute-start | bytes 98312 | tf_op jit(solution)/shard_map/ppermute | solution.py:38
  27.4 0.1 multiply_cosine_fusion.1
  27.5 2.3 %collective-permute-done.7.far_ref = f32[64,128]{1,0:T(8,128)S(1)} collective-permute-done((f32[64,128]{1,0:T(8,128)S(1)}, f32[64,128]{1,0:T(8,128)S(1)}, u32[]{:S(2)}, u32[]{:S(2)}) %collective-permute-start.7) | collective-permute-done | bytes 32800 | tf_op jit(solution)/shard_map/ppermute | solution.py:38
  29.8 0.4 shard_map.180
  30.2 0.1 collective-permute-start.8
  30.3 3.0 %collective-permute-start.9 = (bf16[16,1152]{1,0:T(8,128)(2,1)S(1)}, bf16[16,1152]{1,0:T(8,128)(2,1)S(1)}, u32[]{:S(2)}, u32[]{:S(2)}) collective-permute-start(bf16[16,1152]{1,0:T(8,128)(2,1)S(1)} %get-tuple-element.54), channel_id=1, source_target_pairs={{0,8},{4,12},{8,0},{12,4},{1,9},{5,13},{9,1},{13,5},{2,10},{6,14},... | collective-permute-start | bytes 110600 | tf_op jit(solution)/shard_map/ppermute | solution.py:38
  33.3 1.3 %collective-permute-start.10 = (bf16[16,1152]{1,0:T(8,128)(2,1)S(1)}, bf16[16,1152]{1,0:T(8,128)(2,1)S(1)}, u32[]{:S(2)}, u32[]{:S(2)}) collective-permute-start(bf16[16,1152]{1,0:T(8,128)(2,1)S(1)} %get-tuple-element.55), channel_id=1, source_target_pairs={{0,12},{4,8},{8,4},{12,0},{1,13},{5,9},{9,5},{13,1},{2,14},{6,10},... | collective-permute-start | bytes 110600 | tf_op jit(solution)/shard_map/ppermute | solution.py:38
  34.9 2.7 %collective-permute-start.5 = (f32[32,1280]{1,0:T(8,128)S(1)}, f32[32,1280]{1,0:T(8,128)S(1)}, u32[]{:S(2)}, u32[]{:S(2)}) collective-permute-start(f32[32,1280]{1,0:T(8,128)S(1)} %slice.126), channel_id=1, source_target_pairs={{0,8},{4,12},{8,0},{12,4},{1,9},{5,13},{9,1},{13,5},{2,10},{6,14},... | collective-permute-start | bytes 491528 | tf_op jit(solution)/shard_map/ppermute | solution.py:38
  37.5 1.9 %collective-permute-done.10 = bf16[16,1152]{1,0:T(8,128)(2,1)S(1)} collective-permute-done((bf16[16,1152]{1,0:T(8,128)(2,1)S(1)}, bf16[16,1152]{1,0:T(8,128)(2,1)S(1)}, u32[]{:S(2)}, u32[]{:S(2)}) %collective-permute-start.10) | collective-permute-done | bytes 36896 | tf_op jit(solution)/shard_map/ppermute | solution.py:38
  39.5 0.2 fusion.25
  39.7 6.0 %collective-permute-done.5 = f32[32,1280]{1,0:T(8,128)S(1)} collective-permute-done((f32[32,1280]{1,0:T(8,128)S(1)}, f32[32,1280]{1,0:T(8,128)S(1)}, u32[]{:S(2)}, u32[]{:S(2)}) %collective-permute-start.5) | collective-permute-done | bytes 163872 | tf_op jit(solution)/shard_map/ppermute | solution.py:38
  45.8 0.1 fusion.56
  46.0 0.1 fusion.35
  46.1 0.2 fusion.51
  46.4 0.8 select_reduce_fusion
  47.1 0.2 fusion.34
  47.4 0.4 fusion
  47.9 1.8 %collective-permute-start.13 = (bf16[32,1536]{1,0:T(8,128)(2,1)S(1)}, bf16[32,1536]{1,0:T(8,128)(2,1)S(1)}, u32[]{:S(2)}, u32[]{:S(2)}) collective-permute-start(bf16[32,1536]{1,0:T(8,128)(2,1)S(1)} %get-tuple-element.86), channel_id=1, source_target_pairs={{0,12},{4,8},{8,4},{12,0},{1,13},{5,9},{9,5},{13,1},{2,14},{6,10},... | collective-permute-start | bytes 294920 | tf_op jit(solution)/shard_map/ppermute | solution.py:38
  49.7 2.6 %collective-permute-start.12 = (bf16[32,1536]{1,0:T(8,128)(2,1)S(1)}, bf16[32,1536]{1,0:T(8,128)(2,1)S(1)}, u32[]{:S(2)}, u32[]{:S(2)}) collective-permute-start(bf16[32,1536]{1,0:T(8,128)(2,1)S(1)} %get-tuple-element.88), channel_id=1, source_target_pairs={{0,8},{4,12},{8,0},{12,4},{1,9},{5,13},{9,1},{13,5},{2,10},{6,14},... | collective-permute-start | bytes 294920 | tf_op jit(solution)/shard_map/ppermute | solution.py:38
  52.3 3.1 %collective-permute-done.13.in3_ref = bf16[32,1536]{1,0:T(8,128)(2,1)S(1)} collective-permute-done((bf16[32,1536]{1,0:T(8,128)(2,1)S(1)}, bf16[32,1536]{1,0:T(8,128)(2,1)S(1)}, u32[]{:S(2)}, u32[]{:S(2)}) %collective-permute-start.13) | collective-permute-done | bytes 98336 | tf_op jit(solution)/shard_map/ppermute | solution.py:38
  55.4 2.3 %collective-permute-done.11.in1_ref = bf16[32,1536]{1,0:T(8,128)(2,1)S(1)} collective-permute-done((bf16[32,1536]{1,0:T(8,128)(2,1)S(1)}, bf16[32,1536]{1,0:T(8,128)(2,1)S(1)}, u32[]{:S(2)}, u32[]{:S(2)}) %collective-permute-start.11) | collective-permute-done | bytes 98336 | tf_op jit(solution)/shard_map/ppermute | solution.py:38
  57.8 0.8 collective-permute-done.12.in2_ref
  58.5 1.3 %shard_map.181 = (f32[64,2048]{1,0:T(8,128)S(1)}, f32[64,2048]{1,0:T(8,128)S(1)}) custom-call(s32[2]{0:T(128)S(1)} %pad_add_fusion.place_ref, bf16[32,1536]{1,0:T(8,128)(2,1)S(1)} %get-tuple-element.89.own_ref, bf16[32,1536]{1,0:T(8,128)(2,1)S(1)} %collective-permute-done.11.in1_ref, bf16[32,1536]{1,0:T(8,128)(2,1)S(1)} %collective-permute-done.12.in2_ref, ...), custom_call_target="tpu_custom_call" | custom-call | flops 1000 | bytes 1000 | tf_op jit(solution)/shard_map/pallas_call | solution.py:58
  59.9 1.9 %collective-permute-done.14 = f32[64,2048]{1,0:T(8,128)S(1)} collective-permute-done((f32[64,2048]{1,0:T(8,128)S(1)}, f32[64,2048]{1,0:T(8,128)S(1)}, u32[]{:S(2)}, u32[]{:S(2)}) %collective-permute-start.14) | collective-permute-done | bytes 524320 | tf_op jit(solution)/shard_map/ppermute | solution.py:38
  61.9 0.1 abs_reduce_fusion
  62.1 0.2 fusion.21
  62.4 1.6 %collective-permute-start.15 = (f16[32,2176]{1,0:T(8,128)(2,1)S(1)}, f16[32,2176]{1,0:T(8,128)(2,1)S(1)}, u32[]{:S(2)}, u32[]{:S(2)}) collective-permute-start(f16[32,2176]{1,0:T(8,128)(2,1)S(1)} %pad_maximum_fusion.3), channel_id=1, source_target_pairs={{0,2},{1,3},{2,0},{3,1},{4,6},{5,7},{6,4},{7,5},{8,10},{9,11},{10,... | collective-permute-start | bytes 417800 | tf_op jit(solution)/shard_map/ppermute | solution.py:38
  64.0 4.1 %collective-permute-done.15 = f16[32,2176]{1,0:T(8,128)(2,1)S(1)} collective-permute-done((f16[32,2176]{1,0:T(8,128)(2,1)S(1)}, f16[32,2176]{1,0:T(8,128)(2,1)S(1)}, u32[]{:S(2)}, u32[]{:S(2)}) %collective-permute-start.15) | collective-permute-done | bytes 139296 | tf_op jit(solution)/shard_map/ppermute | solution.py:38
  68.2 0.1 fusion.50
  68.3 0.3 multiply_reduce_fusion
  68.6 1.6 %collective-permute-start.20 = (f32[32]{0:T(128)S(1)}, f32[32]{0:T(128)S(1)}, u32[]{:S(2)}, u32[]{:S(2)}) collective-permute-start(f32[32]{0:T(128)S(1)} %get-tuple-element.72), channel_id=1, source_target_pairs={{0,12},{4,8},{8,4},{12,0},{1,13},{5,9},{9,5},{13,1},{2,14},{6,10},... | collective-permute-start | bytes 392 | tf_op jit(solution)/shard_map/ppermute | solution.py:38
  70.2 0.4 collective-permute-start.19
  70.7 2.4 %collective-permute-start.18 = (f32[32]{0:T(128)S(1)}, f32[32]{0:T(128)S(1)}, u32[]{:S(2)}, u32[]{:S(2)}) collective-permute-start(f32[32]{0:T(128)S(1)} %get-tuple-element.72), channel_id=1, source_target_pairs={{0,4},{4,0},{8,12},{12,8},{1,5},{5,1},{9,13},{13,9},{2,6},{6,2},{1... | collective-permute-start | bytes 392 | tf_op jit(solution)/shard_map/ppermute | solution.py:38
  73.1 1.6 %collective-permute-start.16 = (bf16[32,2048]{1,0:T(8,128)(2,1)S(1)}, bf16[32,2048]{1,0:T(8,128)(2,1)S(1)}, u32[]{:S(2)}, u32[]{:S(2)}) collective-permute-start(bf16[32,2048]{1,0:T(8,128)(2,1)S(1)} %get-tuple-element.73.own_ref), channel_id=1, source_target_pairs={{0,2},{1,3},{2,0},{3,1},{4,6},{5,7},{6,4},{7,5},{8,10},{9,11},{10,... | collective-permute-start | bytes 393224 | tf_op jit(solution)/shard_map/ppermute | solution.py:38
  74.7 1.6 %collective-permute-start.21 = (f32[1,32]{1,0:T(1,128)S(1)}, f32[1,32]{1,0:T(1,128)S(1)}, u32[]{:S(2)}, u32[]{:S(2)}) collective-permute-start(f32[1,32]{1,0:T(1,128)S(1)} %rsqrt_bitcast_fusion), channel_id=1, source_target_pairs={{0,2},{1,3},{2,0},{3,1},{4,6},{5,7},{6,4},{7,5},{8,10},{9,11},{10,... | collective-permute-start | bytes 392 | tf_op jit(solution)/shard_map/ppermute | solution.py:38
  76.3 1.7 %collective-permute-done.16.across_ref = bf16[32,2048]{1,0:T(8,128)(2,1)S(1)} collective-permute-done((bf16[32,2048]{1,0:T(8,128)(2,1)S(1)}, bf16[32,2048]{1,0:T(8,128)(2,1)S(1)}, u32[]{:S(2)}, u32[]{:S(2)}) %collective-permute-start.16) | collective-permute-done | bytes 131104 | tf_op jit(solution)/shard_map/ppermute | solution.py:38
  78.2 0.1 collective-permute-done.21
  78.3 0.4 collective-permute-start.22
  78.7 0.2 multiply_reduce_fusion.2
  78.9 0.8 collective-permute-done.22
  79.7 2.0 %shard_map.182 = (f32[64,2048]{1,0:T(8,128)S(1)}, f32[64,2048]{1,0:T(8,128)S(1)}, bf16[128,2048]{1,0:T(8,128)(2,1)S(1)}) custom-call(s32[2]{0:T(128)S(1)} %pad_add_fusion.place_ref, bf16[32,2048]{1,0:T(8,128)(2,1)S(1)} %get-tuple-element.73.own_ref, bf16[32,2048]{1,0:T(8,128)(2,1)S(1)} %collective-permute-done.16.across_ref, ...), custom_call_target="tpu_custom_call" | custom-call | flops 1000 | bytes 1000 | tf_op jit(solution)/shard_map/pallas_call | solution.py:58
  81.8 1.8 %collective-permute-start.23 = (f16[64,2048]{1,0:T(8,128)(2,1)S(1)}, f16[64,2048]{1,0:T(8,128)(2,1)S(1)}, u32[]{:S(2)}, u32[]{:S(2)}) collective-permute-start(f16[64,2048]{1,0:T(8,128)(2,1)S(1)} %convert_element_type.95), channel_id=1, source_target_pairs={{0,4},{4,0},{8,12},{12,8},{1,5},{5,1},{9,13},{13,9},{2,6},{6,2},{1... | collective-permute-start | bytes 786440 | tf_op jit(solution)/shard_map/ppermute | solution.py:38
  83.6 1.3 %shard_map.183 = (f32[64,2048]{1,0:T(8,128)S(1)}, f32[64,2048]{1,0:T(8,128)S(1)}) custom-call(bf16[128,2048]{1,0:T(8,128)(2,1)S(1)} %get-tuple-element.63.rows_ref, bf16[2048,4096]{1,0:T(8,128)(2,1)S(1)} %bitcast.62), custom_call_target="tpu_custom_call" | custom-call | flops 1000 | bytes 1000 | tf_op jit(solution)/shard_map/pallas_call | solution.py:58
  84.9 1.0 collective-permute-start.26
  86.0 1.2 %collective-permute-start.25 = (f16[32,2048]{1,0:T(8,128)(2,1)S(1)}, f16[32,2048]{1,0:T(8,128)(2,1)S(1)}, u32[]{:S(2)}, u32[]{:S(2)}) collective-permute-start(f16[32,2048]{1,0:T(8,128)(2,1)S(1)} %get-tuple-element.76), channel_id=1, source_target_pairs={{0,4},{4,0},{8,12},{12,8},{1,5},{5,1},{9,13},{13,9},{2,6},{6,2},{1... | collective-permute-start | bytes 393224 | tf_op jit(solution)/shard_map/ppermute | solution.py:38
  87.2 2.3 %collective-permute-start.27 = (f16[32,2048]{1,0:T(8,128)(2,1)S(1)}, f16[32,2048]{1,0:T(8,128)(2,1)S(1)}, u32[]{:S(2)}, u32[]{:S(2)}) collective-permute-start(f16[32,2048]{1,0:T(8,128)(2,1)S(1)} %get-tuple-element.77), channel_id=1, source_target_pairs={{0,12},{4,8},{8,4},{12,0},{1,13},{5,9},{9,5},{13,1},{2,14},{6,10},... | collective-permute-start | bytes 393224 | tf_op jit(solution)/shard_map/ppermute | solution.py:38
  89.5 4.0 %collective-permute-done.23 = f16[64,2048]{1,0:T(8,128)(2,1)S(1)} collective-permute-done((f16[64,2048]{1,0:T(8,128)(2,1)S(1)}, f16[64,2048]{1,0:T(8,128)(2,1)S(1)}, u32[]{:S(2)}, u32[]{:S(2)}) %collective-permute-start.23) | collective-permute-done | bytes 262176 | tf_op jit(solution)/shard_map/ppermute | solution.py:38
  93.6 0.6 collective-permute-start.24
  94.2 0.8 collective-permute-done.26
  95.0 1.0 collective-permute-done.25
  96.0 4.8 %collective-permute-done.27 = f16[32,2048]{1,0:T(8,128)(2,1)S(1)} collective-permute-done((f16[32,2048]{1,0:T(8,128)(2,1)S(1)}, f16[32,2048]{1,0:T(8,128)(2,1)S(1)}, u32[]{:S(2)}, u32[]{:S(2)}) %collective-permute-start.27) | collective-permute-done | bytes 131104 | tf_op jit(solution)/shard_map/ppermute | solution.py:38
  100.9 4.4 %collective-permute-done.24 = f16[32,2048]{1,0:T(8,128)(2,1)S(1)} collective-permute-done((f16[32,2048]{1,0:T(8,128)(2,1)S(1)}, f16[32,2048]{1,0:T(8,128)(2,1)S(1)}, u32[]{:S(2)}, u32[]{:S(2)}) %collective-permute-start.24) | collective-permute-done | bytes 131104 | tf_op jit(solution)/shard_map/ppermute | solution.py:38
  105.4 1.2 %copy.20 = f32[32,2,2048]{2,1,0:T(2,128)} copy(f32[32,2,2048]{2,0,1:T(8,128)S(1)} %pad_maximum_fusion) | data formatting | bytes 1048576
  (82 shorter events, 1.6 us)
Async XLA Ops:
  0.6 45.7 %copy-start = (bf16[32,1,128,128]{3,2,1,0:T(8,128)(2,1)S(1)}, bf16[32,1,128,128]{3,2,1,0:T(8,128)(2,1)}, u32[]{:S(2)}) copy-start(bf16[32,1,128,128]{3,2,1,0:T(8,128)(2,1)} %param.26) | copy-start | bytes 3145732
  2.9 8.5 %collective-permute-start = (bf16[32,2176]{1,0:T(8,128)(2,1)S(1)}, bf16[32,2176]{1,0:T(8,128)(2,1)S(1)}, u32[]{:S(2)}, u32[]{:S(2)}) collective-permute-start(bf16[32,2176]{1,0:T(8,128)(2,1)S(1)} %get-tuple-element.35), channel_id=1, source_target_pairs={{0,4},{4,0},{8,12},{12,8},{1,5},{5,1},{9,13},{13,9},{2,6},{6,2},{1... | collective-permute-start | bytes 417800 | tf_op jit(solution)/shard_map/ppermute | solution.py:38
  6.0 13.5 %collective-permute-start.1 = (bf16[32,2176]{1,0:T(8,128)(2,1)S(1)}, bf16[32,2176]{1,0:T(8,128)(2,1)S(1)}, u32[]{:S(2)}, u32[]{:S(2)}) collective-permute-start(bf16[32,2176]{1,0:T(8,128)(2,1)S(1)} %get-tuple-element.36), channel_id=1, source_target_pairs={{0,8},{4,12},{8,0},{12,4},{1,9},{5,13},{9,1},{13,5},{2,10},{6,14},... | collective-permute-start | bytes 417800 | tf_op jit(solution)/shard_map/ppermute | solution.py:38
  8.6 10.9 %collective-permute-start.2 = (bf16[32,2176]{1,0:T(8,128)(2,1)S(1)}, bf16[32,2176]{1,0:T(8,128)(2,1)S(1)}, u32[]{:S(2)}, u32[]{:S(2)}) collective-permute-start(bf16[32,2176]{1,0:T(8,128)(2,1)S(1)} %get-tuple-element.37), channel_id=1, source_target_pairs={{0,12},{4,8},{8,4},{12,0},{1,13},{5,9},{9,5},{13,1},{2,14},{6,10},... | collective-permute-start | bytes 417800 | tf_op jit(solution)/shard_map/ppermute | solution.py:38
  8.6 71.1 %slice-start = ((s8[16777216]{0:T(1024)(128)(4,1)}), s8[4194304]{0:T(1024)(128)(4,1)S(1)}, s32[]{:S(2)}) async-start(s8[16777216]{0:T(1024)(128)(4,1)} %bitcast.61), calls=%async_computation | async-start | bytes 8388608
  19.5 2.3 %copy-start.6 = (bf16[2048,128]{1,0:T(8,128)(2,1)S(1)}, bf16[2048,128]{1,0:T(8,128)(2,1)}, u32[]{:S(2)}) copy-start(bf16[2048,128]{1,0:T(8,128)(2,1)} %value_ref.1) | copy-start | bytes 1572868
  19.5 1.7 %collective-permute-start.3 = (bf16[48,2048]{1,0:T(8,128)(2,1)S(1)}, bf16[48,2048]{1,0:T(8,128)(2,1)S(1)}, u32[]{:S(2)}, u32[]{:S(2)}) collective-permute-start(bf16[48,2048]{1,0:T(8,128)(2,1)S(1)} %pad_maximum_fusion.2), channel_id=1, source_target_pairs={{0,1},{1,0},{2,3},{3,2},{4,5},{5,4},{6,7},{7,6},{8,9},{9,8},{10,11... | collective-permute-start | bytes 589832 | tf_op jit(solution)/shard_map/ppermute | solution.py:38
  19.6 2.2 %copy-start.8 = (s32[32]{0:T(128)S(1)}, s32[32]{0:T(128)}, u32[]{:S(2)}) copy-start(s32[32]{0:T(128)} %param.29) | copy-start | bytes 388
  19.6 2.2 %copy-start.5 = (bf16[2048,128]{1,0:T(8,128)(2,1)S(1)}, bf16[2048,128]{1,0:T(8,128)(2,1)}, u32[]{:S(2)}) copy-start(bf16[2048,128]{1,0:T(8,128)(2,1)} %key_ref.1) | copy-start | bytes 1572868
  19.7 2.4 %copy-start.1 = (bf16[2048,1024]{1,0:T(8,128)(2,1)S(1)}, bf16[2048,1024]{1,0:T(8,128)(2,1)}, u32[]{:S(2)}) copy-start(bf16[2048,1024]{1,0:T(8,128)(2,1)} %query_ref.1) | copy-start | bytes 12582916
  19.7 60.0 %slice-start.1 = ((s8[16777216]{0:T(1024)(128)(4,1)}), s8[4194304]{0:T(1024)(128)(4,1)S(1)}, s32[]{:S(2)}) async-start(s8[16777216]{0:T(1024)(128)(4,1)} %bitcast.61), calls=%async_computation.1 | async-start | bytes 8388608
  21.2 4.6 %collective-permute-start.6 = (f32[64,128]{1,0:T(8,128)S(1)}, f32[64,128]{1,0:T(8,128)S(1)}, u32[]{:S(2)}, u32[]{:S(2)}) collective-permute-start(f32[64,128]{1,0:T(8,128)S(1)} %get-tuple-element.50), channel_id=1, source_target_pairs={{0,1},{1,0},{2,3},{3,2},{4,5},{5,4},{6,7},{7,6},{8,9},{9,8},{10,11... | collective-permute-start | bytes 98312 | tf_op jit(solution)/shard_map/ppermute | solution.py:38
  22.1 7.8 %copy-start.4 = (bf16[8,64,1024]{2,1,0:T(8,128)(2,1)S(1)}, bf16[8,64,1024]{2,1,0:T(8,128)(2,1)}, u32[]{:S(2)}) copy-start(bf16[8,64,1024]{2,1,0:T(8,128)(2,1)} %param.23) | copy-start | bytes 3145732
  22.1 7.8 %copy-start.7 = (bf16[8,64,128]{2,1,0:T(8,128)(2,1)S(1)}, bf16[8,64,128]{2,1,0:T(8,128)(2,1)}, u32[]{:S(2)}) copy-start(bf16[8,64,128]{2,1,0:T(8,128)(2,1)} %param.25) | copy-start | bytes 393220
  22.1 25.3 %copy-start.9 = (bf16[32,1,128,128]{3,2,1,0:T(8,128)(2,1)S(1)}, bf16[32,1,128,128]{3,2,1,0:T(8,128)(2,1)}, u32[]{:S(2)}) copy-start(bf16[32,1,128,128]{3,2,1,0:T(8,128)(2,1)} %param.27) | copy-start | bytes 3145732
  23.6 11.2 %collective-permute-start.4 = (f32[64,1280]{1,0:T(8,128)S(1)}, f32[64,1280]{1,0:T(8,128)S(1)}, u32[]{:S(2)}, u32[]{:S(2)}) collective-permute-start(f32[64,1280]{1,0:T(8,128)S(1)} %get-tuple-element.48), channel_id=1, source_target_pairs={{0,4},{4,0},{8,12},{12,8},{1,5},{5,1},{9,13},{13,9},{2,6},{6,2},{1... | collective-permute-start | bytes 983048 | tf_op jit(solution)/shard_map/ppermute | solution.py:38
  25.9 4.0 %collective-permute-start.7 = (f32[64,128]{1,0:T(8,128)S(1)}, f32[64,128]{1,0:T(8,128)S(1)}, u32[]{:S(2)}, u32[]{:S(2)}) collective-permute-start(f32[64,128]{1,0:T(8,128)S(1)} %add.84.near_ref), channel_id=1, source_target_pairs={{0,2},{1,3},{2,0},{3,1},{4,6},{5,7},{6,4},{7,5},{8,10},{9,11},{10,... | collective-permute-start | bytes 98312 | tf_op jit(solution)/shard_map/ppermute | solution.py:38
  29.8 49.9 %slice-start.2 = ((s8[16777216]{0:T(1024)(128)(4,1)}), s8[4194304]{0:T(1024)(128)(4,1)S(1)}, s32[]{:S(2)}) async-start(s8[16777216]{0:T(1024)(128)(4,1)} %bitcast.61), calls=%async_computation.2 | async-start | bytes 8388608
  30.2 7.3 %collective-permute-start.8 = (bf16[16,1152]{1,0:T(8,128)(2,1)S(1)}, bf16[16,1152]{1,0:T(8,128)(2,1)S(1)}, u32[]{:S(2)}, u32[]{:S(2)}) collective-permute-start(bf16[16,1152]{1,0:T(8,128)(2,1)S(1)} %get-tuple-element.53), channel_id=1, source_target_pairs={{0,4},{4,0},{8,12},{12,8},{1,5},{5,1},{9,13},{13,9},{2,6},{6,2},{1... | collective-permute-start | bytes 110600 | tf_op jit(solution)/shard_map/ppermute | solution.py:38
  30.3 7.2 %collective-permute-start.9 = (bf16[16,1152]{1,0:T(8,128)(2,1)S(1)}, bf16[16,1152]{1,0:T(8,128)(2,1)S(1)}, u32[]{:S(2)}, u32[]{:S(2)}) collective-permute-start(bf16[16,1152]{1,0:T(8,128)(2,1)S(1)} %get-tuple-element.54), channel_id=1, source_target_pairs={{0,8},{4,12},{8,0},{12,4},{1,9},{5,13},{9,1},{13,5},{2,10},{6,14},... | collective-permute-start | bytes 110600 | tf_op jit(solution)/shard_map/ppermute | solution.py:38
  33.3 6.1 %collective-permute-start.10 = (bf16[16,1152]{1,0:T(8,128)(2,1)S(1)}, bf16[16,1152]{1,0:T(8,128)(2,1)S(1)}, u32[]{:S(2)}, u32[]{:S(2)}) collective-permute-start(bf16[16,1152]{1,0:T(8,128)(2,1)S(1)} %get-tuple-element.55), channel_id=1, source_target_pairs={{0,12},{4,8},{8,4},{12,0},{1,13},{5,9},{9,5},{13,1},{2,14},{6,10},... | collective-permute-start | bytes 110600 | tf_op jit(solution)/shard_map/ppermute | solution.py:38
  34.9 10.8 %collective-permute-start.5 = (f32[32,1280]{1,0:T(8,128)S(1)}, f32[32,1280]{1,0:T(8,128)S(1)}, u32[]{:S(2)}, u32[]{:S(2)}) collective-permute-start(f32[32,1280]{1,0:T(8,128)S(1)} %slice.126), channel_id=1, source_target_pairs={{0,8},{4,12},{8,0},{12,4},{1,9},{5,13},{9,1},{13,5},{2,10},{6,14},... | collective-permute-start | bytes 491528 | tf_op jit(solution)/shard_map/ppermute | solution.py:38
  46.0 12.5 %copy-start.2 = (bf16[1024,2048]{1,0:T(8,128)(2,1)S(1)}, bf16[1024,2048]{1,0:T(8,128)(2,1)}, u32[]{:S(2)}) copy-start(bf16[1024,2048]{1,0:T(8,128)(2,1)} %weight_ref.3) | copy-start | bytes 12582916
  47.8 31.9 %slice-start.3 = ((s8[16777216]{0:T(1024)(128)(4,1)}), s8[4194304]{0:T(1024)(128)(4,1)S(1)}, s32[]{:S(2)}) async-start(s8[16777216]{0:T(1024)(128)(4,1)} %bitcast.61), calls=%async_computation.3 | async-start | bytes 8388608
  47.9 7.6 %collective-permute-start.13 = (bf16[32,1536]{1,0:T(8,128)(2,1)S(1)}, bf16[32,1536]{1,0:T(8,128)(2,1)S(1)}, u32[]{:S(2)}, u32[]{:S(2)}) collective-permute-start(bf16[32,1536]{1,0:T(8,128)(2,1)S(1)} %get-tuple-element.86), channel_id=1, source_target_pairs={{0,12},{4,8},{8,4},{12,0},{1,13},{5,9},{9,5},{13,1},{2,14},{6,10},... | collective-permute-start | bytes 294920 | tf_op jit(solution)/shard_map/ppermute | solution.py:38
  49.7 8.0 %collective-permute-start.11 = (bf16[32,1536]{1,0:T(8,128)(2,1)S(1)}, bf16[32,1536]{1,0:T(8,128)(2,1)S(1)}, u32[]{:S(2)}, u32[]{:S(2)}) collective-permute-start(bf16[32,1536]{1,0:T(8,128)(2,1)S(1)} %get-tuple-element.87), channel_id=1, source_target_pairs={{0,4},{4,0},{8,12},{12,8},{1,5},{5,1},{9,13},{13,9},{2,6},{6,2},{1... | collective-permute-start | bytes 294920 | tf_op jit(solution)/shard_map/ppermute | solution.py:38
  49.7 8.8 %collective-permute-start.12 = (bf16[32,1536]{1,0:T(8,128)(2,1)S(1)}, bf16[32,1536]{1,0:T(8,128)(2,1)S(1)}, u32[]{:S(2)}, u32[]{:S(2)}) collective-permute-start(bf16[32,1536]{1,0:T(8,128)(2,1)S(1)} %get-tuple-element.88), channel_id=1, source_target_pairs={{0,8},{4,12},{8,0},{12,4},{1,9},{5,13},{9,1},{13,5},{2,10},{6,14},... | collective-permute-start | bytes 294920 | tf_op jit(solution)/shard_map/ppermute | solution.py:38
  59.8 2.0 %collective-permute-start.14 = (f32[64,2048]{1,0:T(8,128)S(1)}, f32[64,2048]{1,0:T(8,128)S(1)}, u32[]{:S(2)}, u32[]{:S(2)}) collective-permute-start(f32[64,2048]{1,0:T(8,128)S(1)} %get-tuple-element.58), channel_id=1, source_target_pairs={{0,1},{1,0},{2,3},{3,2},{4,5},{5,4},{6,7},{7,6},{8,9},{9,8},{10,11... | collective-permute-start | bytes 1572872 | tf_op jit(solution)/shard_map/ppermute | solution.py:38
  62.4 5.8 %collective-permute-start.15 = (f16[32,2176]{1,0:T(8,128)(2,1)S(1)}, f16[32,2176]{1,0:T(8,128)(2,1)S(1)}, u32[]{:S(2)}, u32[]{:S(2)}) collective-permute-start(f16[32,2176]{1,0:T(8,128)(2,1)S(1)} %pad_maximum_fusion.3), channel_id=1, source_target_pairs={{0,2},{1,3},{2,0},{3,1},{4,6},{5,7},{6,4},{7,5},{8,10},{9,11},{10,... | collective-permute-start | bytes 417800 | tf_op jit(solution)/shard_map/ppermute | solution.py:38
  68.6 13.1 %copy-start.3 = (bf16[32,2048]{1,0:T(8,128)(2,1)}, bf16[32,2048]{1,0:T(8,128)(2,1)S(1)}, u32[]{:S(2)}) copy-start(bf16[32,2048]{1,0:T(8,128)(2,1)S(1)} %get-tuple-element.73.own_ref) | copy-start | bytes 393220
  68.6 6.0 %collective-permute-start.20 = (f32[32]{0:T(128)S(1)}, f32[32]{0:T(128)S(1)}, u32[]{:S(2)}, u32[]{:S(2)}) collective-permute-start(f32[32]{0:T(128)S(1)} %get-tuple-element.72), channel_id=1, source_target_pairs={{0,12},{4,8},{8,4},{12,0},{1,13},{5,9},{9,5},{13,1},{2,14},{6,10},... | collective-permute-start | bytes 392 | tf_op jit(solution)/shard_map/ppermute | solution.py:38
  70.2 4.4 %collective-permute-start.19 = (f32[32]{0:T(128)S(1)}, f32[32]{0:T(128)S(1)}, u32[]{:S(2)}, u32[]{:S(2)}) collective-permute-start(f32[32]{0:T(128)S(1)} %get-tuple-element.72), channel_id=1, source_target_pairs={{0,8},{4,12},{8,0},{12,4},{1,9},{5,13},{9,1},{13,5},{2,10},{6,14},... | collective-permute-start | bytes 392 | tf_op jit(solution)/shard_map/ppermute | solution.py:38
  70.7 4.0 %collective-permute-start.18 = (f32[32]{0:T(128)S(1)}, f32[32]{0:T(128)S(1)}, u32[]{:S(2)}, u32[]{:S(2)}) collective-permute-start(f32[32]{0:T(128)S(1)} %get-tuple-element.72), channel_id=1, source_target_pairs={{0,4},{4,0},{8,12},{12,8},{1,5},{5,1},{9,13},{13,9},{2,6},{6,2},{1... | collective-permute-start | bytes 392 | tf_op jit(solution)/shard_map/ppermute | solution.py:38
  73.1 5.0 %collective-permute-start.16 = (bf16[32,2048]{1,0:T(8,128)(2,1)S(1)}, bf16[32,2048]{1,0:T(8,128)(2,1)S(1)}, u32[]{:S(2)}, u32[]{:S(2)}) collective-permute-start(bf16[32,2048]{1,0:T(8,128)(2,1)S(1)} %get-tuple-element.73.own_ref), channel_id=1, source_target_pairs={{0,2},{1,3},{2,0},{3,1},{4,6},{5,7},{6,4},{7,5},{8,10},{9,11},{10,... | collective-permute-start | bytes 393224 | tf_op jit(solution)/shard_map/ppermute | solution.py:38
  74.7 3.6 %collective-permute-start.21 = (f32[1,32]{1,0:T(1,128)S(1)}, f32[1,32]{1,0:T(1,128)S(1)}, u32[]{:S(2)}, u32[]{:S(2)}) collective-permute-start(f32[1,32]{1,0:T(1,128)S(1)} %rsqrt_bitcast_fusion), channel_id=1, source_target_pairs={{0,2},{1,3},{2,0},{3,1},{4,6},{5,7},{6,4},{7,5},{8,10},{9,11},{10,... | collective-permute-start | bytes 392 | tf_op jit(solution)/shard_map/ppermute | solution.py:38
  78.1 1.6 %collective-permute-start.17 = (bf16[64,2048]{1,0:T(8,128)(2,1)S(1)}, bf16[64,2048]{1,0:T(8,128)(2,1)S(1)}, u32[]{:S(2)}, u32[]{:S(2)}) collective-permute-start(bf16[64,2048]{1,0:T(8,128)(2,1)S(1)} %pad_maximum_fusion.1), channel_id=1, source_target_pairs={{0,1},{1,0},{2,3},{3,2},{4,5},{5,4},{6,7},{7,6},{8,9},{9,8},{10,11... | collective-permute-start | bytes 786440 | tf_op jit(solution)/shard_map/ppermute | solution.py:38
  78.3 1.4 %collective-permute-start.22 = (f32[2,32]{1,0:T(2,128)S(1)}, f32[2,32]{1,0:T(2,128)S(1)}, u32[]{:S(2)}, u32[]{:S(2)}) collective-permute-start(f32[2,32]{1,0:T(2,128)S(1)} %pad_maximum_fusion.12), channel_id=1, source_target_pairs={{0,1},{1,0},{2,3},{3,2},{4,5},{5,4},{6,7},{7,6},{8,9},{9,8},{10,11... | collective-permute-start | bytes 776 | tf_op jit(solution)/shard_map/ppermute | solution.py:38
  81.8 11.7 %collective-permute-start.23 = (f16[64,2048]{1,0:T(8,128)(2,1)S(1)}, f16[64,2048]{1,0:T(8,128)(2,1)S(1)}, u32[]{:S(2)}, u32[]{:S(2)}) collective-permute-start(f16[64,2048]{1,0:T(8,128)(2,1)S(1)} %convert_element_type.95), channel_id=1, source_target_pairs={{0,4},{4,0},{8,12},{12,8},{1,5},{5,1},{9,13},{13,9},{2,6},{6,2},{1... | collective-permute-start | bytes 786440 | tf_op jit(solution)/shard_map/ppermute | solution.py:38
  84.9 10.1 %collective-permute-start.26 = (f16[32,2048]{1,0:T(8,128)(2,1)S(1)}, f16[32,2048]{1,0:T(8,128)(2,1)S(1)}, u32[]{:S(2)}, u32[]{:S(2)}) collective-permute-start(f16[32,2048]{1,0:T(8,128)(2,1)S(1)} %slice_convert_fusion), channel_id=1, source_target_pairs={{0,8},{4,12},{8,0},{12,4},{1,9},{5,13},{9,1},{13,5},{2,10},{6,14},... | collective-permute-start | bytes 393224 | tf_op jit(solution)/shard_map/ppermute | solution.py:38
  86.0 10.0 %collective-permute-start.25 = (f16[32,2048]{1,0:T(8,128)(2,1)S(1)}, f16[32,2048]{1,0:T(8,128)(2,1)S(1)}, u32[]{:S(2)}, u32[]{:S(2)}) collective-permute-start(f16[32,2048]{1,0:T(8,128)(2,1)S(1)} %get-tuple-element.76), channel_id=1, source_target_pairs={{0,4},{4,0},{8,12},{12,8},{1,5},{5,1},{9,13},{13,9},{2,6},{6,2},{1... | collective-permute-start | bytes 393224 | tf_op jit(solution)/shard_map/ppermute | solution.py:38
  87.2 13.6 %collective-permute-start.27 = (f16[32,2048]{1,0:T(8,128)(2,1)S(1)}, f16[32,2048]{1,0:T(8,128)(2,1)S(1)}, u32[]{:S(2)}, u32[]{:S(2)}) collective-permute-start(f16[32,2048]{1,0:T(8,128)(2,1)S(1)} %get-tuple-element.77), channel_id=1, source_target_pairs={{0,12},{4,8},{8,4},{12,0},{1,13},{5,9},{9,5},{13,1},{2,14},{6,10},... | collective-permute-start | bytes 393224 | tf_op jit(solution)/shard_map/ppermute | solution.py:38
  93.6 11.7 %collective-permute-start.24 = (f16[32,2048]{1,0:T(8,128)(2,1)S(1)}, f16[32,2048]{1,0:T(8,128)(2,1)S(1)}, u32[]{:S(2)}, u32[]{:S(2)}) collective-permute-start(f16[32,2048]{1,0:T(8,128)(2,1)S(1)} %slice_convert_fusion.1), channel_id=1, source_target_pairs={{0,8},{4,12},{8,0},{12,4},{1,9},{5,13},{9,1},{13,5},{2,10},{6,14},... | collective-permute-start | bytes 393224 | tf_op jit(solution)/shard_map/ppermute | solution.py:38
